TPU v7x, 32 devices: a whole 2x2x4 slice. The times are simulated.
32 devices in a mesh: blk: 8 (over z, x), group: 4 (over y, core).
Axes of the slice: x: 2, y: 2, z: 4, core: 2. Of those that a mesh axis runs over, the one named last changes fastest.
Arguments:
- user_factors: float32 [8192, 256], P(('blk', 'group')), may hold values from -1.5 to 1.5
- user_state: float32 [8192, 256], P(('blk', 'group')), may hold values from 0.5 to 20
- item_factors: float32 [8192, 256], P(('blk', 'group')), may hold values from -1.5 to 1.5
- item_state: float32 [8192, 256], P(('blk', 'group')), may hold values from 0.5 to 20
- counts: int32 [8192, 1024], P(('blk', 'group')), may hold values from 0 to 5
Outputs:
- users_out: float32 [8192, 256], P(('blk', 'group'))
- user_state_out: float32 [8192, 256], P(('blk', 'group'))
- items_out: float32 [8192, 256], P(('blk', 'group'))
- item_state_out: float32 [8192, 256], P(('blk', 'group'))
All inputs are finite; a program needn't handle non-finite values.
Results may differ from a plain program's by a relative error of at most 0.0003.
Values sent between devices are 32-bit elements; how exact they have to be, the bound alone decides.
No kernel may reach another device: no remote copies, remote signals or barrier semaphores. Data moves between devices by JAX's collectives and lax.ppermute only.
A program may use at most 64 MiB of HBM per device.

v0:
```python
import jax
import jax.numpy as jnp
from jax import lax
from jax.sharding import PartitionSpec as P

STRATA = 4


conf_scale = 0.5
ridge_weight = 0.01
step_rate = 0.1


def passed_along(value, axis, steps):
    count = lax.axis_size(axis)
    pairs = [(source, (source + steps) % count) for source in range(count)]
    return lax.ppermute(value, axis, pairs)


def transposed_dot(left, right):
    return lax.dot_general(left, right, (((0,), (0,)), ((), ())), precision=lax.Precision.HIGHEST)


def item_update(weighted_gap, users, items, item_acc):
    item_grad = 2.0 * transposed_dot(weighted_gap, users) + 2.0 * ridge_weight * items
    item_acc = item_acc + item_grad * item_grad
    return (items - step_rate * item_grad / jnp.sqrt(item_acc), item_acc)


def body(user_factors, user_state, item_factors, item_state, counts):
    highest = lax.Precision.HIGHEST
    item_rows = item_factors.shape[0]
    users, user_acc = (user_factors, user_state)
    items, item_acc = (item_factors, item_state)
    for stratum in range(STRATA):
        count_tile = counts[:, stratum * item_rows : (stratum + 1) * item_rows]
        predicted = lax.dot_general(users, items, (((1,), (1,)), ((), ())), precision=highest)
        prefer = (count_tile > 0).astype(jnp.float32)
        confidence = 1.0 + conf_scale * count_tile.astype(jnp.float32)
        weighted_gap = confidence * (predicted - prefer)
        user_grad = (
            2.0 * jnp.dot(weighted_gap, items, precision=highest) + 2.0 * ridge_weight * users
        )
        next_items, next_acc = item_update(weighted_gap, users, items, item_acc)
        next_items, next_acc = passed_along((next_items, next_acc), "blk", 1)
        user_acc = user_acc + user_grad * user_grad
        users = users - step_rate * user_grad / jnp.sqrt(user_acc)
        items, item_acc = (next_items, next_acc)
    items, item_acc = passed_along((items, item_acc), "group", 1)
    return (users, user_acc, items, item_acc)


def solution(mesh):
    return jax.shard_map(
        body,
        mesh=mesh,
        in_specs=(
            P(("blk", "group"), None),
            P(("blk", "group"), None),
            P(("blk", "group"), None),
            P(("blk", "group"), None),
            P(("blk", "group"), None),
        ),
        out_specs=(
            P(("blk", "group"), None),
            P(("blk", "group"), None),
            P(("blk", "group"), None),
            P(("blk", "group"), None),
        ),
        check_vma=False,
    )
```

profile of v0, /device:TPU:0, one launch (start us, length us, event | category | flops | bytes accessed | tf_op | source)
XLA Modules:
  0.0 75.8 jit_solution(5333553567235427446)
XLA Ops:
  0.6 0.0 copy-start.1
  0.6 0.0 copy-start
  0.7 0.0 copy-start.4
  0.7 1.6 %fusion.8 = f32[256,256]{1,0:T(8,128)S(1)} fusion(f32[256,256]{1,0:T(8,128)} %param.5, f32[256,256]{1,0:T(8,128)} %param.7, s32[256,1024]{1,0:T(8,128)} %param.9), kind=kOutput, calls=%fused_computation.20 | convolution fusion | flops 201785344 | bytes 1048576 | tf_op jit(solution)/shard_map/dot_general | solution.py:37
  2.3 0.0 copy-done.1
  2.3 0.0 copy-done
  2.3 0.0 copy-done.4
  2.3 0.0 copy-start.2
  2.3 0.6 multiply_subtract_fusion.6
  2.9 0.0 copy-start.3
  2.9 3.0 %collective-permute-start = (f32[256,256]{1,0:T(8,128)S(1)}, f32[256,256]{1,0:T(8,128)S(1)}, u32[]{:S(2)}, u32[]{:S(2)}) collective-permute-start(f32[256,256]{1,0:T(8,128)S(1)} %get-tuple-element.8), channel_id=1, source_target_pairs={{0,4},{4,8},{8,12},{12,16},{16,20},{20,24},{24,28},{28,0},{1,5},{5... | collective-permute-start | bytes 786440 | tf_op jit(solution)/shard_map/ppermute | solution.py:17
  5.9 1.5 %collective-permute-start.1 = (f32[256,256]{1,0:T(8,128)S(1)}, f32[256,256]{1,0:T(8,128)S(1)}, u32[]{:S(2)}, u32[]{:S(2)}) collective-permute-start(f32[256,256]{1,0:T(8,128)S(1)} %get-tuple-element.9), channel_id=1, source_target_pairs={{0,4},{4,8},{8,12},{12,16},{16,20},{20,24},{24,28},{28,0},{1,5},{5... | collective-permute-start | bytes 786440 | tf_op jit(solution)/shard_map/ppermute | solution.py:17
  7.5 0.0 copy-done.2
  7.5 0.4 multiply_subtract_fusion.7
  7.9 8.2 %collective-permute-done = f32[256,256]{1,0:T(8,128)S(1)} collective-permute-done((f32[256,256]{1,0:T(8,128)S(1)}, f32[256,256]{1,0:T(8,128)S(1)}, u32[]{:S(2)}, u32[]{:S(2)}) %collective-permute-start) | collective-permute-done | bytes 262176 | tf_op jit(solution)/shard_map/ppermute | solution.py:17
  16.1 0.0 copy-done.3
  16.1 0.4 fusion.5
  16.5 4.4 %collective-permute-done.1 = f32[256,256]{1,0:T(8,128)S(1)} collective-permute-done((f32[256,256]{1,0:T(8,128)S(1)}, f32[256,256]{1,0:T(8,128)S(1)}, u32[]{:S(2)}, u32[]{:S(2)}) %collective-permute-start.1) | collective-permute-done | bytes 262176 | tf_op jit(solution)/shard_map/ppermute | solution.py:17
  20.9 0.6 multiply_add_fusion.6
  21.5 0.1 collective-permute-start.3
  21.6 1.1 %collective-permute-start.2 = (f32[256,256]{1,0:T(8,128)S(1)}, f32[256,256]{1,0:T(8,128)S(1)}, u32[]{:S(2)}, u32[]{:S(2)}) collective-permute-start(f32[256,256]{1,0:T(8,128)S(1)} %get-tuple-element.15), channel_id=1, source_target_pairs={{0,4},{4,8},{8,12},{12,16},{16,20},{20,24},{24,28},{28,0},{1,5},{5... | collective-permute-start | bytes 786440 | tf_op jit(solution)/shard_map/ppermute | solution.py:17
  22.7 0.4 multiply_subtract_fusion.5
  23.2 14.2 %collective-permute-done.2 = f32[256,256]{1,0:T(8,128)S(1)} collective-permute-done((f32[256,256]{1,0:T(8,128)S(1)}, f32[256,256]{1,0:T(8,128)S(1)}, u32[]{:S(2)}, u32[]{:S(2)}) %collective-permute-start.2) | collective-permute-done | bytes 262176 | tf_op jit(solution)/shard_map/ppermute | solution.py:17
  37.4 0.4 fusion.3
  37.8 0.6 convolution_multiply_fusion.2
  38.4 0.0 collective-permute-done.3
  38.4 0.1 multiply_add_fusion.3
  38.5 0.1 collective-permute-start.5
  38.6 0.1 collective-permute-start.4
  38.6 0.4 multiply_subtract_fusion.3
  39.1 14.4 %collective-permute-done.4 = f32[256,256]{1,0:T(8,128)S(1)} collective-permute-done((f32[256,256]{1,0:T(8,128)S(1)}, f32[256,256]{1,0:T(8,128)S(1)}, u32[]{:S(2)}, u32[]{:S(2)}) %collective-permute-start.4) | collective-permute-done | bytes 262176 | tf_op jit(solution)/shard_map/ppermute | solution.py:17
  53.4 0.4 fusion.1
  53.9 0.6 convolution_multiply_fusion
  54.5 0.0 collective-permute-done.5
  54.5 0.1 multiply_add_fusion
  54.6 0.1 collective-permute-start.8
  54.6 0.1 collective-permute-start.6
  54.7 11.1 %collective-permute-done.8 = f32[256,256]{1,0:T(8,128)S(1)} collective-permute-done((f32[256,256]{1,0:T(8,128)S(1)}, f32[256,256]{1,0:T(8,128)S(1)}, u32[]{:S(2)}, u32[]{:S(2)}) %collective-permute-start.8) | collective-permute-done | bytes 262176 | tf_op jit(solution)/shard_map/ppermute | solution.py:17
  65.8 0.0 collective-permute-start.9
  65.8 2.8 %collective-permute-done.6 = f32[256,256]{1,0:T(8,128)S(1)} collective-permute-done((f32[256,256]{1,0:T(8,128)S(1)}, f32[256,256]{1,0:T(8,128)S(1)}, u32[]{:S(2)}, u32[]{:S(2)}) %collective-permute-start.6) | collective-permute-done | bytes 262176 | tf_op jit(solution)/shard_map/ppermute | solution.py:17
  68.6 0.0 collective-permute-start.7
  68.6 1.2 %multiply_subtract_fusion.1 = (f32[256,256]{1,0:T(8,128)}, f32[256,256]{1,0:T(8,128)}) fusion(f32[256,256]{1,0:T(8,128)S(1)} %get-tuple-element.18, f32[256,256]{1,0:T(8,128)S(1)} %get-tuple-element.7, f32[256,256]{1,0:T(8,128)S(1)} %get-tuple-element.19, f32[256,256]{1,0:T(8,128)S(1)} %fusion.1, f32[256,256]{1,0:T(8,128)S(1)} %collective-permute-done.4), kind=kOutput, calls=%fused_computation.24 | convolution fusion | flops 201981952 | bytes 1835008 | tf_op jit(solution)/shard_map/dot_general | solution.py:42
  69.8 1.8 %collective-permute-done.9 = f32[256,256]{1,0:T(8,128)S(1)} collective-permute-done((f32[256,256]{1,0:T(8,128)S(1)}, f32[256,256]{1,0:T(8,128)S(1)}, u32[]{:S(2)}, u32[]{:S(2)}) %collective-permute-start.9) | collective-permute-done | bytes 262176 | tf_op jit(solution)/shard_map/ppermute | solution.py:17
  71.6 2.8 %collective-permute-done.7 = f32[256,256]{1,0:T(8,128)S(1)} collective-permute-done((f32[256,256]{1,0:T(8,128)S(1)}, f32[256,256]{1,0:T(8,128)S(1)}, u32[]{:S(2)}, u32[]{:S(2)}) %collective-permute-start.7) | collective-permute-done | bytes 262176 | tf_op jit(solution)/shard_map/ppermute | solution.py:17
  74.4 0.7 copy.11
  75.1 0.7 copy.12
Async XLA Ops:
  0.6 1.6 %copy-start.1 = (f32[256,256]{1,0:T(8,128)S(1)}, f32[256,256]{1,0:T(8,128)}, u32[]{:S(2)}) copy-start(f32[256,256]{1,0:T(8,128)} %param.7) | copy-start | bytes 786436
  0.6 1.6 %copy-start = (f32[256,256]{1,0:T(8,128)S(1)}, f32[256,256]{1,0:T(8,128)}, u32[]{:S(2)}) copy-start(f32[256,256]{1,0:T(8,128)} %param.5) | copy-start | bytes 786436
  0.7 1.6 %copy-start.4 = (f32[256,256]{1,0:T(8,128)S(1)}, f32[256,256]{1,0:T(8,128)}, u32[]{:S(2)}) copy-start(f32[256,256]{1,0:T(8,128)} %param.8) | copy-start | bytes 786436
  2.3 5.2 %copy-start.2 = (f32[256,256]{1,0:T(8,128)S(1)}, f32[256,256]{1,0:T(8,128)}, u32[]{:S(2)}) copy-start(f32[256,256]{1,0:T(8,128)} %param.6) | copy-start | bytes 786436
  2.9 13.2 %copy-start.3 = (s32[256,1024]{1,0:T(8,128)S(1)}, s32[256,1024]{1,0:T(8,128)}, u32[]{:S(2)}) copy-start(s32[256,1024]{1,0:T(8,128)} %param.9) | copy-start | bytes 3145732
  2.9 13.2 %collective-permute-start = (f32[256,256]{1,0:T(8,128)S(1)}, f32[256,256]{1,0:T(8,128)S(1)}, u32[]{:S(2)}, u32[]{:S(2)}) collective-permute-start(f32[256,256]{1,0:T(8,128)S(1)} %get-tuple-element.8), channel_id=1, source_target_pairs={{0,4},{4,8},{8,12},{12,16},{16,20},{20,24},{24,28},{28,0},{1,5},{5... | collective-permute-start | bytes 786440 | tf_op jit(solution)/shard_map/ppermute | solution.py:17
  5.9 15.0 %collective-permute-start.1 = (f32[256,256]{1,0:T(8,128)S(1)}, f32[256,256]{1,0:T(8,128)S(1)}, u32[]{:S(2)}, u32[]{:S(2)}) collective-permute-start(f32[256,256]{1,0:T(8,128)S(1)} %get-tuple-element.9), channel_id=1, source_target_pairs={{0,4},{4,8},{8,12},{12,16},{16,20},{20,24},{24,28},{28,0},{1,5},{5... | collective-permute-start | bytes 786440 | tf_op jit(solution)/shard_map/ppermute | solution.py:17
  21.5 16.9 %collective-permute-start.3 = (f32[256,256]{1,0:T(8,128)S(1)}, f32[256,256]{1,0:T(8,128)S(1)}, u32[]{:S(2)}, u32[]{:S(2)}) collective-permute-start(f32[256,256]{1,0:T(8,128)S(1)} %get-tuple-element.14), channel_id=1, source_target_pairs={{0,4},{4,8},{8,12},{12,16},{16,20},{20,24},{24,28},{28,0},{1,5},{5... | collective-permute-start | bytes 786440 | tf_op jit(solution)/shard_map/ppermute | solution.py:17
  21.6 15.8 %collective-permute-start.2 = (f32[256,256]{1,0:T(8,128)S(1)}, f32[256,256]{1,0:T(8,128)S(1)}, u32[]{:S(2)}, u32[]{:S(2)}) collective-permute-start(f32[256,256]{1,0:T(8,128)S(1)} %get-tuple-element.15), channel_id=1, source_target_pairs={{0,4},{4,8},{8,12},{12,16},{16,20},{20,24},{24,28},{28,0},{1,5},{5... | collective-permute-start | bytes 786440 | tf_op jit(solution)/shard_map/ppermute | solution.py:17
  38.5 16.0 %collective-permute-start.5 = (f32[256,256]{1,0:T(8,128)S(1)}, f32[256,256]{1,0:T(8,128)S(1)}, u32[]{:S(2)}, u32[]{:S(2)}) collective-permute-start(f32[256,256]{1,0:T(8,128)S(1)} %get-tuple-element.12), channel_id=1, source_target_pairs={{0,4},{4,8},{8,12},{12,16},{16,20},{20,24},{24,28},{28,0},{1,5},{5... | collective-permute-start | bytes 786440 | tf_op jit(solution)/shard_map/ppermute | solution.py:17
  38.6 14.9 %collective-permute-start.4 = (f32[256,256]{1,0:T(8,128)S(1)}, f32[256,256]{1,0:T(8,128)S(1)}, u32[]{:S(2)}, u32[]{:S(2)}) collective-permute-start(f32[256,256]{1,0:T(8,128)S(1)} %get-tuple-element.13), channel_id=1, source_target_pairs={{0,4},{4,8},{8,12},{12,16},{16,20},{20,24},{24,28},{28,0},{1,5},{5... | collective-permute-start | bytes 786440 | tf_op jit(solution)/shard_map/ppermute | solution.py:17
  54.6 11.2 %collective-permute-start.8 = (f32[256,256]{1,0:T(8,128)S(1)}, f32[256,256]{1,0:T(8,128)S(1)}, u32[]{:S(2)}, u32[]{:S(2)}) collective-permute-start(f32[256,256]{1,0:T(8,128)S(1)} %get-tuple-element.10), channel_id=1, source_target_pairs={{0,4},{4,8},{8,12},{12,16},{16,20},{20,24},{24,28},{28,0},{1,5},{5... | collective-permute-start | bytes 786440 | tf_op jit(solution)/shard_map/ppermute | solution.py:17
  54.6 13.9 %collective-permute-start.6 = (f32[256,256]{1,0:T(8,128)S(1)}, f32[256,256]{1,0:T(8,128)S(1)}, u32[]{:S(2)}, u32[]{:S(2)}) collective-permute-start(f32[256,256]{1,0:T(8,128)S(1)} %get-tuple-element.11), channel_id=1, source_target_pairs={{0,4},{4,8},{8,12},{12,16},{16,20},{20,24},{24,28},{28,0},{1,5},{5... | collective-permute-start | bytes 786440 | tf_op jit(solution)/shard_map/ppermute | solution.py:17
  65.8 5.8 %collective-permute-start.9 = (f32[256,256]{1,0:T(8,128)S(1)}, f32[256,256]{1,0:T(8,128)S(1)}, u32[]{:S(2)}, u32[]{:S(2)}) collective-permute-start(f32[256,256]{1,0:T(8,128)S(1)} %collective-permute-done.8), channel_id=1, source_target_pairs={{0,1},{1,2},{2,3},{3,0},{4,5},{5,6},{6,7},{7,4},{8,9},{9,10},{10,1... | collective-permute-start | bytes 786440 | tf_op jit(solution)/shard_map/ppermute | solution.py:17
  68.6 5.8 %collective-permute-start.7 = (f32[256,256]{1,0:T(8,128)S(1)}, f32[256,256]{1,0:T(8,128)S(1)}, u32[]{:S(2)}, u32[]{:S(2)}) collective-permute-start(f32[256,256]{1,0:T(8,128)S(1)} %collective-permute-done.6), channel_id=1, source_target_pairs={{0,1},{1,2},{2,3},{3,0},{4,5},{5,6},{6,7},{7,4},{8,9},{9,10},{10,1... | collective-permute-start | bytes 786440 | tf_op jit(solution)/shard_map/ppermute | solution.py:17
where the time goes:
time: 75.9 us; the launch traced here: 75.8 us
  waiting for transfers between devices  59.6 us (79%)
  matrix products  7.79 us (10%)
  starting transfers between devices  5.97 us (8%)
  local copies, waits for them, and re-layouts  1.43 us (2%)
  between operations  0.85 us (1%)
    ppermute x10, waiting for transfers between devices, passed_along(): return lax.ppermute(value, axis, pairs)  59.6 us
    ppermute x10, starting transfers between devices, passed_along(): return lax.ppermute(value, axis, pairs)  5.97 us
    dot_general x4, matrix products, body(): lax.dot_general(users, items, (((1,), (1,)), ((), ())), precision=highest)  2.84 us
    dot_general x4, matrix products, body(): jnp.dot(weighted_gap, items, precision=highest)  2.53 us
    dot_general x4, matrix products, transposed_dot(): lax.dot_general(left, right, (((0,), (0,)), ((), ())), precision=lax.Prec...  2.43 us
  transfers between devices with their start and end apart: 10, of which 8 were waited for; matrix products, arithmetic and copies ran while one was open for 7% of the time, Pallas kernels for 0%

commit v1 on v0

v1 whole, which is shorter than its diff:
```python
import jax
import jax.numpy as jnp
from jax import lax
from jax.sharding import PartitionSpec as P

conf_scale = 0.5
ridge_weight = 0.01
step_rate = 0.1

PREC = lax.Precision.HIGH


def sent(value, where):
    n_blk, n_group = lax.axis_size("blk"), lax.axis_size("group")
    pairs = []
    for b in range(n_blk):
        for g in range(n_group):
            target = where(b, g)
            if target is not None:
                pairs.append((b * n_group + g, target[0] % n_blk * n_group + target[1] % n_group))
    return lax.ppermute(value, ("blk", "group"), pairs)


def weighted_gap(users, items, count_tile):
    predicted = lax.dot_general(users, items, (((1,), (1,)), ((), ())), precision=PREC)
    prefer = (count_tile > 0).astype(jnp.float32)
    confidence = 1.0 + conf_scale * count_tile.astype(jnp.float32)
    return confidence * (predicted - prefer)


def user_gradient(gap, users, items):
    return 2.0 * jnp.dot(gap, items, precision=PREC) + 2.0 * ridge_weight * users


def item_gradient(gap, users, items):
    product = lax.dot_general(gap, users, (((0,), (0,)), ((), ())), precision=PREC)
    return 2.0 * product + 2.0 * ridge_weight * items


def adagrad(factors, sums, gradient):
    sums = sums + gradient * gradient
    return factors - step_rate * gradient / jnp.sqrt(sums), sums


def body(users, user_acc, items, item_acc, counts):
    rows = items.shape[0]
    tiles = [counts[:, s * rows : (s + 1) * rows] for s in range(4)]
    odd = lax.axis_index("blk") % 2 == 1

    def two_strata(users, user_acc, items, item_acc, first, up):
        gap = weighted_gap(users, items, tiles[first])
        grad_v = item_gradient(gap, users, items)
        grad_u = user_gradient(gap, users, items)
        items, item_acc = adagrad(items, item_acc, grad_v)
        users, user_acc = adagrad(users, user_acc, grad_u)

        visitor = sent(items, lambda b, g: (b + 1, g))
        items, item_acc, users = lax.optimization_barrier((items, item_acc, users))
        ahead = sent(jnp.where(odd, item_acc, items), lambda b, g: (b + 2, g + up))
        even_acc = sent(item_acc, lambda b, g: (b + 2, g + up) if b % 2 == 0 else None)
        passed = sent(visitor, lambda b, g: (b + 1, g + up) if b % 2 == 0 else None)
        gap = weighted_gap(users, visitor, tiles[first + 1])
        grad_v = item_gradient(gap, users, visitor)
        grad_u = user_gradient(gap, users, visitor)
        grad_v = sent(grad_v, lambda b, g: (b + 1, g + up))
        users, user_acc = adagrad(users, user_acc, grad_u)
        items = jnp.where(odd, passed, ahead)
        item_acc = jnp.where(odd, ahead, even_acc)
        items, item_acc = adagrad(items, item_acc, grad_v)
        return users, user_acc, items, item_acc

    state = two_strata(users, user_acc, items, item_acc, 0, 0)
    return two_strata(*state, 2, 1)


def solution(mesh):
    spec = P(("blk", "group"), None)
    return jax.shard_map(body, mesh=mesh, in_specs=(spec,) * 5, out_specs=(spec,) * 4, check_vma=False)
```

time: 75.9 us -> 50.9 us (0.67)
  waiting for transfers between devices: 59.6 us -> 20 us
  starting transfers between devices: 5.97 us -> 22.5 us
  matrix products: 7.79 us -> 6.26 us
  local copies, waits for them, and re-layouts: 1.43 us -> 0.03 us
  other arithmetic: 0.16 us -> 1.01 us
    ppermute x10, waiting for transfers between devices: 59.6 us -> 20 us  [sent(): return lax.ppermute(value, ('blk', 'group'), pairs)]
    ppermute x10, starting transfers between devices: 5.97 us -> 22.5 us  [sent(): return lax.ppermute(value, ('blk', 'group'), pairs)]
    dot_general x12, matrix products: 7.79 us -> 6.26 us  [the longest x4 2.56 us: weighted_gap(): lax.dot_general(users, items, (((1,), (1,)), ((), ())), precision=PREC)]
    unnamed x12 -> x10, local copies, waits for them, and re-layouts: 1.43 us -> 0.03 us
    sub x0 -> x2, other arithmetic: none -> 0.94 us  [adagrad(): return (factors - step_rate * gradient / jnp.sqrt(sums), sums)]
  transfers between devices with their start and end apart: 10 -> 10, of which waited for: 8 -> 7; matrix products, arithmetic and copies ran while one was open for 7% -> 7% of each run, Pallas kernels for 0% -> 0%
where the time goes in v1:
time: 50.9 us; the launch traced here: 50.7 us
  starting transfers between devices  22.5 us (44%)
  waiting for transfers between devices  20 us (39%)
  matrix products  6.26 us (12%)
  other arithmetic  1.01 us (2%)
  between operations  0.86 us (2%)
    ppermute x10, starting transfers between devices, sent(): return lax.ppermute(value, ('blk', 'group'), pairs)  22.5 us
    ppermute x10, waiting for transfers between devices, sent(): return lax.ppermute(value, ('blk', 'group'), pairs)  20 us
    dot_general x4, matrix products, weighted_gap(): lax.dot_general(users, items, (((1,), (1,)), ((), ())), precision=PREC)  2.56 us
    dot_general x4, matrix products, user_gradient(): jnp.dot(gap, items, precision=PREC)  2.08 us
    dot_general x4, matrix products, item_gradient(): lax.dot_general(gap, users, (((0,), (0,)), ((), ())), precision=PREC)  1.62 us
  transfers between devices with their start and end apart: 10, of which 7 were waited for; matrix products, arithmetic and copies ran while one was open for 7% of the time, Pallas kernels for 0%

profile of v1, /device:TPU:0, one launch (start us, length us, event | category | flops | bytes accessed | tf_op | source)
XLA Modules:
  0.0 50.7 jit_solution(16201538097413224464)
XLA Ops:
  0.6 0.0 copy-start.1
  0.6 0.0 copy-start
  0.7 0.0 copy-start.4
  0.7 1.5 %fusion.8 = f32[256,256]{1,0:T(8,128)S(1)} fusion(f32[256,256]{1,0:T(8,128)} %param.5, f32[256,256]{1,0:T(8,128)} %param.7, s32[256,1024]{1,0:T(8,128)} %param.9), kind=kOutput, calls=%fused_computation.20 | convolution fusion | flops 101122048 | bytes 1048576 | tf_op jit(solution)/shard_map/dot_general | solution.py:25
  2.2 0.0 copy-done.1
  2.2 0.0 copy-done
  2.2 0.0 copy-done.4
  2.2 0.0 copy-start.2
  2.2 0.4 multiply_subtract_fusion.7
  2.7 0.0 copy-start.3
  2.7 3.0 %collective-permute-start = (f32[256,256]{1,0:T(8,128)S(1)}, f32[256,256]{1,0:T(8,128)S(1)}, u32[]{:S(2)}, u32[]{:S(2)}) collective-permute-start(f32[256,256]{1,0:T(8,128)S(1)} %get-tuple-element.11), channel_id=1, source_target_pairs={{0,4},{1,5},{2,6},{3,7},{4,8},{5,9},{6,10},{7,11},{8,12},{9,13},{1... | collective-permute-start | bytes 786440 | tf_op jit(solution)/shard_map/ppermute | solution.py:21
  5.7 0.0 copy-done.2
  5.7 0.3 multiply_subtract_fusion.6
  6.0 3.5 %collective-permute-start.4 = (f32[256,256]{1,0:T(8,128)S(1)}, f32[256,256]{1,0:T(8,128)S(1)}, u32[]{:S(2)}, u32[]{:S(2)}) collective-permute-start(f32[256,256]{1,0:T(8,128)S(1)} %get-tuple-element.10), channel_id=1, source_target_pairs={{0,8},{1,9},{2,10},{3,11},{8,16},{9,17},{10,18},{11,19},{16,24},{1... | collective-permute-start | bytes 786440 | tf_op jit(solution)/shard_map/ppermute | solution.py:21
  9.5 1.6 %collective-permute-start.2 = (f32[256,256]{1,0:T(8,128)S(1)}, f32[256,256]{1,0:T(8,128)S(1)}, u32[]{:S(2)}, u32[]{:S(2)}) collective-permute-start(f32[256,256]{1,0:T(8,128)S(1)} %broadcast_select_fusion.1), channel_id=1, source_target_pairs={{0,8},{1,9},{2,10},{3,11},{4,12},{5,13},{6,14},{7,15},{8,16},{9,17... | collective-permute-start | bytes 786440 | tf_op jit(solution)/shard_map/ppermute | solution.py:21
  11.2 4.7 %collective-permute-done = f32[256,256]{1,0:T(8,128)S(1)} collective-permute-done((f32[256,256]{1,0:T(8,128)S(1)}, f32[256,256]{1,0:T(8,128)S(1)}, u32[]{:S(2)}, u32[]{:S(2)}) %collective-permute-start) | collective-permute-done | bytes 262176 | tf_op jit(solution)/shard_map/ppermute | solution.py:21
  15.8 0.0 copy-done.3
  15.8 0.3 fusion.5
  16.2 0.4 multiply_add_fusion.8
  16.6 0.1 collective-permute-start.3
  16.7 3.4 %collective-permute-start.1 = (f32[256,256]{1,0:T(8,128)S(1)}, f32[256,256]{1,0:T(8,128)S(1)}, u32[]{:S(2)}, u32[]{:S(2)}) collective-permute-start(f32[256,256]{1,0:T(8,128)S(1)} %collective-permute-done), channel_id=1, source_target_pairs={{0,4},{1,5},{2,6},{3,7},{8,12},{9,13},{10,14},{11,15},{16,20},{17,... | collective-permute-start | bytes 786440 | tf_op jit(solution)/shard_map/ppermute | solution.py:21
  20.0 0.3 multiply_subtract_fusion.4
  20.4 2.8 %collective-permute-done.2 = f32[256,256]{1,0:T(8,128)S(1)} collective-permute-done((f32[256,256]{1,0:T(8,128)S(1)}, f32[256,256]{1,0:T(8,128)S(1)}, u32[]{:S(2)}, u32[]{:S(2)}) %collective-permute-start.2) | collective-permute-done | bytes 262176 | tf_op jit(solution)/shard_map/ppermute | solution.py:21
  23.1 0.0 collective-permute-done.4
  23.1 3.1 %collective-permute-done.3 = f32[256,256]{1,0:T(8,128)S(1)} collective-permute-done((f32[256,256]{1,0:T(8,128)S(1)}, f32[256,256]{1,0:T(8,128)S(1)}, u32[]{:S(2)}, u32[]{:S(2)}) %collective-permute-start.3) | collective-permute-done | bytes 262176 | tf_op jit(solution)/shard_map/ppermute | solution.py:21
  26.2 0.5 collective-permute-done.1
  26.7 0.1 multiply_subtract_fusion.5
  26.8 0.3 fusion.3
  27.2 0.4 multiply_subtract_fusion.3
  27.6 2.5 %collective-permute-start.5 = (f32[256,256]{1,0:T(8,128)S(1)}, f32[256,256]{1,0:T(8,128)S(1)}, u32[]{:S(2)}, u32[]{:S(2)}) collective-permute-start(f32[256,256]{1,0:T(8,128)S(1)} %get-tuple-element.15), channel_id=1, source_target_pairs={{0,4},{1,5},{2,6},{3,7},{4,8},{5,9},{6,10},{7,11},{8,12},{9,13},{1... | collective-permute-start | bytes 786440 | tf_op jit(solution)/shard_map/ppermute | solution.py:21
  30.1 0.3 multiply_subtract_fusion.2
  30.5 1.9 %collective-permute-start.9 = (f32[256,256]{1,0:T(8,128)S(1)}, f32[256,256]{1,0:T(8,128)S(1)}, u32[]{:S(2)}, u32[]{:S(2)}) collective-permute-start(f32[256,256]{1,0:T(8,128)S(1)} %get-tuple-element.14), channel_id=1, source_target_pairs={{0,9},{1,10},{2,11},{3,8},{8,17},{9,18},{10,19},{11,16},{16,25},{1... | collective-permute-start | bytes 786440 | tf_op jit(solution)/shard_map/ppermute | solution.py:21
  32.4 2.0 %collective-permute-start.7 = (f32[256,256]{1,0:T(8,128)S(1)}, f32[256,256]{1,0:T(8,128)S(1)}, u32[]{:S(2)}, u32[]{:S(2)}) collective-permute-start(f32[256,256]{1,0:T(8,128)S(1)} %broadcast_select_fusion), channel_id=1, source_target_pairs={{0,9},{1,10},{2,11},{3,8},{4,13},{5,14},{6,15},{7,12},{8,17},{9,18... | collective-permute-start | bytes 786440 | tf_op jit(solution)/shard_map/ppermute | solution.py:21
  34.4 2.8 %collective-permute-done.5 = f32[256,256]{1,0:T(8,128)S(1)} collective-permute-done((f32[256,256]{1,0:T(8,128)S(1)}, f32[256,256]{1,0:T(8,128)S(1)}, u32[]{:S(2)}, u32[]{:S(2)}) %collective-permute-start.5) | collective-permute-done | bytes 262176 | tf_op jit(solution)/shard_map/ppermute | solution.py:21
  37.2 0.3 fusion.1
  37.5 0.4 multiply_add_fusion.1
  37.9 0.1 collective-permute-start.8
  38.0 4.5 %collective-permute-start.6 = (f32[256,256]{1,0:T(8,128)S(1)}, f32[256,256]{1,0:T(8,128)S(1)}, u32[]{:S(2)}, u32[]{:S(2)}) collective-permute-start(f32[256,256]{1,0:T(8,128)S(1)} %collective-permute-done.5), channel_id=1, source_target_pairs={{0,5},{1,6},{2,7},{3,4},{8,13},{9,14},{10,15},{11,12},{16,21},{17,... | collective-permute-start | bytes 786440 | tf_op jit(solution)/shard_map/ppermute | solution.py:21
  42.5 1.1 %multiply_subtract_fusion.1 = (f32[256,256]{1,0:T(8,128)}, f32[256,256]{1,0:T(8,128)}) fusion(f32[256,256]{1,0:T(8,128)S(1)} %get-tuple-element.13, f32[256,256]{1,0:T(8,128)S(1)} %get-tuple-element.23, f32[256,256]{1,0:T(8,128)S(1)} %get-tuple-element.29, f32[256,256]{1,0:T(8,128)S(1)} %fusion.1, f32[256,256]{1,0:T(8,128)S(1)} %collective-permute-done.5), kind=kOutput, calls=%fused_computation.24 | convolution fusion | flops 101318656 | bytes 1835008 | tf_op jit(solution)/shard_map/dot_general | solution.py:32
  43.6 5.4 %collective-permute-done.7 = f32[256,256]{1,0:T(8,128)S(1)} collective-permute-done((f32[256,256]{1,0:T(8,128)S(1)}, f32[256,256]{1,0:T(8,128)S(1)}, u32[]{:S(2)}, u32[]{:S(2)}) %collective-permute-start.7) | collective-permute-done | bytes 262176 | tf_op jit(solution)/shard_map/ppermute | solution.py:21
  49.0 0.0 collective-permute-done.9
  49.0 0.8 %collective-permute-done.8 = f32[256,256]{1,0:T(8,128)S(1)} collective-permute-done((f32[256,256]{1,0:T(8,128)S(1)}, f32[256,256]{1,0:T(8,128)S(1)}, u32[]{:S(2)}, u32[]{:S(2)}) %collective-permute-start.8) | collective-permute-done | bytes 262176 | tf_op jit(solution)/shard_map/ppermute | solution.py:21
  49.8 0.0 collective-permute-done.6
  49.8 0.9 %multiply_subtract_fusion = (f32[256,256]{1,0:T(8,128)}, f32[256,256]{1,0:T(8,128)}) fusion(f32[256,256]{1,0:T(8,128)S(1)} %collective-permute-done.8, f32[256,256]{1,0:T(8,128)S(1)} %collective-permute-done.6, f32[256,256]{1,0:T(8,128)S(1)} %collective-permute-done.7, pred[]{:T(512)S(6)} %eq.5, f32[256,256]{1,0:T(8,128)S(1)} %collective-permute-done.9), kind=kLoop, calls=%fused_computation.21 | loop fusion | flops 458752 | bytes 1572865 | tf_op jit(solution)/shard_map/sub | solution.py:42
  (2 shorter events, 0.1 us)
Async XLA Ops:
  0.6 1.6 %copy-start.1 = (f32[256,256]{1,0:T(8,128)S(1)}, f32[256,256]{1,0:T(8,128)}, u32[]{:S(2)}) copy-start(f32[256,256]{1,0:T(8,128)} %param.7) | copy-start | bytes 786436
  0.6 1.6 %copy-start = (f32[256,256]{1,0:T(8,128)S(1)}, f32[256,256]{1,0:T(8,128)}, u32[]{:S(2)}) copy-start(f32[256,256]{1,0:T(8,128)} %param.5) | copy-start | bytes 786436
  0.7 1.6 %copy-start.4 = (f32[256,256]{1,0:T(8,128)S(1)}, f32[256,256]{1,0:T(8,128)}, u32[]{:S(2)}) copy-start(f32[256,256]{1,0:T(8,128)} %param.8) | copy-start | bytes 786436
  2.2 3.4 %copy-start.2 = (f32[256,256]{1,0:T(8,128)S(1)}, f32[256,256]{1,0:T(8,128)}, u32[]{:S(2)}) copy-start(f32[256,256]{1,0:T(8,128)} %param.6) | copy-start | bytes 786436
  2.7 13.2 %copy-start.3 = (s32[256,1024]{1,0:T(8,128)S(1)}, s32[256,1024]{1,0:T(8,128)}, u32[]{:S(2)}) copy-start(s32[256,1024]{1,0:T(8,128)} %param.9) | copy-start | bytes 3145732
  2.7 13.2 %collective-permute-start = (f32[256,256]{1,0:T(8,128)S(1)}, f32[256,256]{1,0:T(8,128)S(1)}, u32[]{:S(2)}, u32[]{:S(2)}) collective-permute-start(f32[256,256]{1,0:T(8,128)S(1)} %get-tuple-element.11), channel_id=1, source_target_pairs={{0,4},{1,5},{2,6},{3,7},{4,8},{5,9},{6,10},{7,11},{8,12},{9,13},{1... | collective-permute-start | bytes 786440 | tf_op jit(solution)/shard_map/ppermute | solution.py:21
  6.0 17.1 %collective-permute-start.4 = (f32[256,256]{1,0:T(8,128)S(1)}, f32[256,256]{1,0:T(8,128)S(1)}, u32[]{:S(2)}, u32[]{:S(2)}) collective-permute-start(f32[256,256]{1,0:T(8,128)S(1)} %get-tuple-element.10), channel_id=1, source_target_pairs={{0,8},{1,9},{2,10},{3,11},{8,16},{9,17},{10,18},{11,19},{16,24},{1... | collective-permute-start | bytes 786440 | tf_op jit(solution)/shard_map/ppermute | solution.py:21
  9.5 13.6 %collective-permute-start.2 = (f32[256,256]{1,0:T(8,128)S(1)}, f32[256,256]{1,0:T(8,128)S(1)}, u32[]{:S(2)}, u32[]{:S(2)}) collective-permute-start(f32[256,256]{1,0:T(8,128)S(1)} %broadcast_select_fusion.1), channel_id=1, source_target_pairs={{0,8},{1,9},{2,10},{3,11},{4,12},{5,13},{6,14},{7,15},{8,16},{9,17... | collective-permute-start | bytes 786440 | tf_op jit(solution)/shard_map/ppermute | solution.py:21
  16.6 9.6 %collective-permute-start.3 = (f32[256,256]{1,0:T(8,128)S(1)}, f32[256,256]{1,0:T(8,128)S(1)}, u32[]{:S(2)}, u32[]{:S(2)}) collective-permute-start(f32[256,256]{1,0:T(8,128)S(1)} %multiply_add_fusion.8), channel_id=1, source_target_pairs={{0,4},{1,5},{2,6},{3,7},{4,8},{5,9},{6,10},{7,11},{8,12},{9,13},{1... | collective-permute-start | bytes 786440 | tf_op jit(solution)/shard_map/ppermute | solution.py:21
  16.7 10.1 %collective-permute-start.1 = (f32[256,256]{1,0:T(8,128)S(1)}, f32[256,256]{1,0:T(8,128)S(1)}, u32[]{:S(2)}, u32[]{:S(2)}) collective-permute-start(f32[256,256]{1,0:T(8,128)S(1)} %collective-permute-done), channel_id=1, source_target_pairs={{0,4},{1,5},{2,6},{3,7},{8,12},{9,13},{10,14},{11,15},{16,20},{17,... | collective-permute-start | bytes 786440 | tf_op jit(solution)/shard_map/ppermute | solution.py:21
  27.6 9.6 %collective-permute-start.5 = (f32[256,256]{1,0:T(8,128)S(1)}, f32[256,256]{1,0:T(8,128)S(1)}, u32[]{:S(2)}, u32[]{:S(2)}) collective-permute-start(f32[256,256]{1,0:T(8,128)S(1)} %get-tuple-element.15), channel_id=1, source_target_pairs={{0,4},{1,5},{2,6},{3,7},{4,8},{5,9},{6,10},{7,11},{8,12},{9,13},{1... | collective-permute-start | bytes 786440 | tf_op jit(solution)/shard_map/ppermute | solution.py:21
  30.5 18.5 %collective-permute-start.9 = (f32[256,256]{1,0:T(8,128)S(1)}, f32[256,256]{1,0:T(8,128)S(1)}, u32[]{:S(2)}, u32[]{:S(2)}) collective-permute-start(f32[256,256]{1,0:T(8,128)S(1)} %get-tuple-element.14), channel_id=1, source_target_pairs={{0,9},{1,10},{2,11},{3,8},{8,17},{9,18},{10,19},{11,16},{16,25},{1... | collective-permute-start | bytes 786440 | tf_op jit(solution)/shard_map/ppermute | solution.py:21
  32.4 16.6 %collective-permute-start.7 = (f32[256,256]{1,0:T(8,128)S(1)}, f32[256,256]{1,0:T(8,128)S(1)}, u32[]{:S(2)}, u32[]{:S(2)}) collective-permute-start(f32[256,256]{1,0:T(8,128)S(1)} %broadcast_select_fusion), channel_id=1, source_target_pairs={{0,9},{1,10},{2,11},{3,8},{4,13},{5,14},{6,15},{7,12},{8,17},{9,18... | collective-permute-start | bytes 786440 | tf_op jit(solution)/shard_map/ppermute | solution.py:21
  37.9 11.9 %collective-permute-start.8 = (f32[256,256]{1,0:T(8,128)S(1)}, f32[256,256]{1,0:T(8,128)S(1)}, u32[]{:S(2)}, u32[]{:S(2)}) collective-permute-start(f32[256,256]{1,0:T(8,128)S(1)} %multiply_add_fusion.1), channel_id=1, source_target_pairs={{0,5},{1,6},{2,7},{3,4},{4,9},{5,10},{6,11},{7,8},{8,13},{9,14},{1... | collective-permute-start | bytes 786440 | tf_op jit(solution)/shard_map/ppermute | solution.py:21
  38.0 11.8 %collective-permute-start.6 = (f32[256,256]{1,0:T(8,128)S(1)}, f32[256,256]{1,0:T(8,128)S(1)}, u32[]{:S(2)}, u32[]{:S(2)}) collective-permute-start(f32[256,256]{1,0:T(8,128)S(1)} %collective-permute-done.5), channel_id=1, source_target_pairs={{0,5},{1,6},{2,7},{3,4},{8,13},{9,14},{10,15},{11,12},{16,21},{17,... | collective-permute-start | bytes 786440 | tf_op jit(solution)/shard_map/ppermute | solution.py:21

commit v2 on v1

--- a/solution.py
+++ b/solution.py
@@ -61,11 +61,12 @@
         passed = sent(visitor, lambda b, g: (b + 1, g + up) if b % 2 == 0 else None)
         gap = weighted_gap(users, visitor, tiles[first + 1])
         grad_v = item_gradient(gap, users, visitor)
-        grad_u = user_gradient(gap, users, visitor)
         grad_v = sent(grad_v, lambda b, g: (b + 1, g + up))
-        users, user_acc = adagrad(users, user_acc, grad_u)
         items = jnp.where(odd, passed, ahead)
         item_acc = jnp.where(odd, ahead, even_acc)
+        gap, items, item_acc = lax.optimization_barrier((gap, items, item_acc))
+        users, user_acc = adagrad(users, user_acc, user_gradient(gap, users, visitor))
+        users, items, item_acc, grad_v = lax.optimization_barrier((users, items, item_acc, grad_v))
         items, item_acc = adagrad(items, item_acc, grad_v)
         return users, user_acc, items, item_acc
 

time: 50.9 us -> 53.2 us (1.045)
  waiting for transfers between devices: 20 us -> 27 us
  starting transfers between devices: 22.5 us -> 17.7 us
    ppermute x10, waiting for transfers between devices: 20 us -> 27 us  [sent(): return lax.ppermute(value, ('blk', 'group'), pairs)]
    ppermute x10, starting transfers between devices: 22.5 us -> 17.7 us  [sent(): return lax.ppermute(value, ('blk', 'group'), pairs)]
where the time goes in v2:
time: 53.2 us; the launch traced here: 53 us
  waiting for transfers between devices  27 us (51%)
  starting transfers between devices  17.7 us (33%)
  matrix products  6.25 us (12%)
  other arithmetic  1.07 us (2%)
  between operations  0.88 us (2%)
    ppermute x10, waiting for transfers between devices, sent(): return lax.ppermute(value, ('blk', 'group'), pairs)  27 us
    ppermute x10, starting transfers between devices, sent(): return lax.ppermute(value, ('blk', 'group'), pairs)  17.7 us
    dot_general x4, matrix products, weighted_gap(): lax.dot_general(users, items, (((1,), (1,)), ((), ())), precision=PREC)  2.57 us
    dot_general x4, matrix products, user_gradient(): jnp.dot(gap, items, precision=PREC)  2.08 us
    dot_general x4, matrix products, item_gradient(): lax.dot_general(gap, users, (((0,), (0,)), ((), ())), precision=PREC)  1.61 us
  transfers between devices with their start and end apart: 10, of which 7 were waited for; matrix products, arithmetic and copies ran while one was open for 7% of the time, Pallas kernels for 0%

profile of v2, /device:TPU:0, one launch (start us, length us, event | category | flops | bytes accessed | tf_op | source)
XLA Modules:
  0.0 53.0 jit_solution(9148177616669916857)
XLA Ops:
  0.6 0.0 copy-start.1
  0.6 0.0 copy-start
  0.7 0.0 copy-start.4
  0.7 1.5 %fusion.9 = f32[256,256]{1,0:T(8,128)S(1)} fusion(f32[256,256]{1,0:T(8,128)} %param.5, f32[256,256]{1,0:T(8,128)} %param.7, s32[256,1024]{1,0:T(8,128)} %param.9), kind=kOutput, calls=%fused_computation.21 | convolution fusion | flops 101122048 | bytes 1048576 | tf_op jit(solution)/shard_map/dot_general | solution.py:25
  2.2 0.0 copy-done.1
  2.2 0.0 copy-done
  2.2 0.0 copy-done.4
  2.2 0.0 copy-start.2
  2.2 0.4 multiply_subtract_fusion.7
  2.7 0.0 copy-start.3
  2.7 3.0 %collective-permute-start = (f32[256,256]{1,0:T(8,128)S(1)}, f32[256,256]{1,0:T(8,128)S(1)}, u32[]{:S(2)}, u32[]{:S(2)}) collective-permute-start(f32[256,256]{1,0:T(8,128)S(1)} %get-tuple-element.26), channel_id=1, source_target_pairs={{0,4},{1,5},{2,6},{3,7},{4,8},{5,9},{6,10},{7,11},{8,12},{9,13},{1... | collective-permute-start | bytes 786440 | tf_op jit(solution)/shard_map/ppermute | solution.py:21
  5.7 0.0 copy-done.2
  5.7 0.3 multiply_subtract_fusion.6
  6.0 3.5 %collective-permute-start.3 = (f32[256,256]{1,0:T(8,128)S(1)}, f32[256,256]{1,0:T(8,128)S(1)}, u32[]{:S(2)}, u32[]{:S(2)}) collective-permute-start(f32[256,256]{1,0:T(8,128)S(1)} %get-tuple-element.25), channel_id=1, source_target_pairs={{0,8},{1,9},{2,10},{3,11},{8,16},{9,17},{10,18},{11,19},{16,24},{1... | collective-permute-start | bytes 786440 | tf_op jit(solution)/shard_map/ppermute | solution.py:21
  9.5 1.6 %collective-permute-start.2 = (f32[256,256]{1,0:T(8,128)S(1)}, f32[256,256]{1,0:T(8,128)S(1)}, u32[]{:S(2)}, u32[]{:S(2)}) collective-permute-start(f32[256,256]{1,0:T(8,128)S(1)} %broadcast_select_fusion.5), channel_id=1, source_target_pairs={{0,8},{1,9},{2,10},{3,11},{4,12},{5,13},{6,14},{7,15},{8,16},{9,17... | collective-permute-start | bytes 786440 | tf_op jit(solution)/shard_map/ppermute | solution.py:21
  11.2 4.7 %collective-permute-done = f32[256,256]{1,0:T(8,128)S(1)} collective-permute-done((f32[256,256]{1,0:T(8,128)S(1)}, f32[256,256]{1,0:T(8,128)S(1)}, u32[]{:S(2)}, u32[]{:S(2)}) %collective-permute-start) | collective-permute-done | bytes 262176 | tf_op jit(solution)/shard_map/ppermute | solution.py:21
  15.8 1.3 %collective-permute-start.1 = (f32[256,256]{1,0:T(8,128)S(1)}, f32[256,256]{1,0:T(8,128)S(1)}, u32[]{:S(2)}, u32[]{:S(2)}) collective-permute-start(f32[256,256]{1,0:T(8,128)S(1)} %collective-permute-done), channel_id=1, source_target_pairs={{0,4},{1,5},{2,6},{3,7},{8,12},{9,13},{10,14},{11,15},{16,20},{17,... | collective-permute-start | bytes 786440 | tf_op jit(solution)/shard_map/ppermute | solution.py:21
  17.1 0.0 copy-done.3
  17.1 0.3 fusion.6
  17.5 0.4 multiply_add_fusion.6
  17.9 0.1 collective-permute-start.4
  18.0 5.2 %collective-permute-done.2 = f32[256,256]{1,0:T(8,128)S(1)} collective-permute-done((f32[256,256]{1,0:T(8,128)S(1)}, f32[256,256]{1,0:T(8,128)S(1)}, u32[]{:S(2)}, u32[]{:S(2)}) %collective-permute-start.2) | collective-permute-done | bytes 262176 | tf_op jit(solution)/shard_map/ppermute | solution.py:21
  23.1 0.0 collective-permute-done.3
  23.1 0.7 %collective-permute-done.1 = f32[256,256]{1,0:T(8,128)S(1)} collective-permute-done((f32[256,256]{1,0:T(8,128)S(1)}, f32[256,256]{1,0:T(8,128)S(1)}, u32[]{:S(2)}, u32[]{:S(2)}) %collective-permute-start.1) | collective-permute-done | bytes 262176 | tf_op jit(solution)/shard_map/ppermute | solution.py:21
  23.9 0.1 broadcast_select_fusion.3
  23.9 0.3 multiply_subtract_fusion.5
  24.2 3.1 %collective-permute-done.4 = f32[256,256]{1,0:T(8,128)S(1)} collective-permute-done((f32[256,256]{1,0:T(8,128)S(1)}, f32[256,256]{1,0:T(8,128)S(1)}, u32[]{:S(2)}, u32[]{:S(2)}) %collective-permute-start.4) | collective-permute-done | bytes 262176 | tf_op jit(solution)/shard_map/ppermute | solution.py:21
  27.3 0.1 multiply_subtract_fusion.4
  27.4 0.3 fusion.4
  27.7 0.4 multiply_subtract_fusion.3
  28.1 2.4 %collective-permute-start.5 = (f32[256,256]{1,0:T(8,128)S(1)}, f32[256,256]{1,0:T(8,128)S(1)}, u32[]{:S(2)}, u32[]{:S(2)}) collective-permute-start(f32[256,256]{1,0:T(8,128)S(1)} %get-tuple-element.36), channel_id=1, source_target_pairs={{0,4},{1,5},{2,6},{3,7},{4,8},{5,9},{6,10},{7,11},{8,12},{9,13},{1... | collective-permute-start | bytes 786440 | tf_op jit(solution)/shard_map/ppermute | solution.py:21
  30.5 0.3 multiply_subtract_fusion.2
  30.9 1.9 %collective-permute-start.8 = (f32[256,256]{1,0:T(8,128)S(1)}, f32[256,256]{1,0:T(8,128)S(1)}, u32[]{:S(2)}, u32[]{:S(2)}) collective-permute-start(f32[256,256]{1,0:T(8,128)S(1)} %get-tuple-element.35), channel_id=1, source_target_pairs={{0,9},{1,10},{2,11},{3,8},{8,17},{9,18},{10,19},{11,16},{16,25},{1... | collective-permute-start | bytes 786440 | tf_op jit(solution)/shard_map/ppermute | solution.py:21
  32.8 2.6 %collective-permute-start.7 = (f32[256,256]{1,0:T(8,128)S(1)}, f32[256,256]{1,0:T(8,128)S(1)}, u32[]{:S(2)}, u32[]{:S(2)}) collective-permute-start(f32[256,256]{1,0:T(8,128)S(1)} %broadcast_select_fusion.2), channel_id=1, source_target_pairs={{0,9},{1,10},{2,11},{3,8},{4,13},{5,14},{6,15},{7,12},{8,17},{9,18... | collective-permute-start | bytes 786440 | tf_op jit(solution)/shard_map/ppermute | solution.py:21
  35.4 2.4 %collective-permute-done.5 = f32[256,256]{1,0:T(8,128)S(1)} collective-permute-done((f32[256,256]{1,0:T(8,128)S(1)}, f32[256,256]{1,0:T(8,128)S(1)}, u32[]{:S(2)}, u32[]{:S(2)}) %collective-permute-start.5) | collective-permute-done | bytes 262176 | tf_op jit(solution)/shard_map/ppermute | solution.py:21
  37.8 1.3 %collective-permute-start.6 = (f32[256,256]{1,0:T(8,128)S(1)}, f32[256,256]{1,0:T(8,128)S(1)}, u32[]{:S(2)}, u32[]{:S(2)}) collective-permute-start(f32[256,256]{1,0:T(8,128)S(1)} %collective-permute-done.5), channel_id=1, source_target_pairs={{0,5},{1,6},{2,7},{3,4},{8,13},{9,14},{10,15},{11,12},{16,21},{17,... | collective-permute-start | bytes 786440 | tf_op jit(solution)/shard_map/ppermute | solution.py:21
  39.1 0.3 fusion.1
  39.5 0.4 multiply_add_fusion.1
  39.9 0.1 collective-permute-start.9
  40.0 9.3 %collective-permute-done.7 = f32[256,256]{1,0:T(8,128)S(1)} collective-permute-done((f32[256,256]{1,0:T(8,128)S(1)}, f32[256,256]{1,0:T(8,128)S(1)}, u32[]{:S(2)}, u32[]{:S(2)}) %collective-permute-start.7) | collective-permute-done | bytes 262176 | tf_op jit(solution)/shard_map/ppermute | solution.py:21
  49.2 0.0 collective-permute-done.8
  49.2 0.0 collective-permute-done.6
  49.3 0.1 broadcast_select_fusion
  49.3 1.1 %multiply_subtract_fusion.1 = (f32[256,256]{1,0:T(8,128)}, f32[256,256]{1,0:T(8,128)}) fusion(f32[256,256]{1,0:T(8,128)S(1)} %get-tuple-element.34, f32[256,256]{1,0:T(8,128)S(1)} %get-tuple-element.51, f32[256,256]{1,0:T(8,128)S(1)} %get-tuple-element.61, f32[256,256]{1,0:T(8,128)S(1)} %fusion.1, f32[256,256]{1,0:T(8,128)S(1)} %collective-permute-done.5), kind=kOutput, calls=%fused_computation.25 | convolution fusion | flops 101318656 | bytes 1835008 | tf_op jit(solution)/shard_map/dot_general | solution.py:32
  50.4 1.7 %collective-permute-done.9 = f32[256,256]{1,0:T(8,128)S(1)} collective-permute-done((f32[256,256]{1,0:T(8,128)S(1)}, f32[256,256]{1,0:T(8,128)S(1)}, u32[]{:S(2)}, u32[]{:S(2)}) %collective-permute-start.9) | collective-permute-done | bytes 262176 | tf_op jit(solution)/shard_map/ppermute | solution.py:21
  52.1 0.8 %multiply_subtract_fusion = (f32[256,256]{1,0:T(8,128)}, f32[256,256]{1,0:T(8,128)}) fusion(f32[256,256]{1,0:T(8,128)S(1)} %get-tuple-element.41, f32[256,256]{1,0:T(8,128)S(1)} %collective-permute-done.9, f32[256,256]{1,0:T(8,128)S(1)} %get-tuple-element.43), kind=kLoop, calls=%fused_computation.22 | loop fusion | flops 327680 | bytes 1310720 | tf_op jit(solution)/shard_map/sub | solution.py:42
  (2 shorter events, 0.1 us)
Async XLA Ops:
  0.6 1.6 %copy-start.1 = (f32[256,256]{1,0:T(8,128)S(1)}, f32[256,256]{1,0:T(8,128)}, u32[]{:S(2)}) copy-start(f32[256,256]{1,0:T(8,128)} %param.7) | copy-start | bytes 786436
  0.6 1.6 %copy-start = (f32[256,256]{1,0:T(8,128)S(1)}, f32[256,256]{1,0:T(8,128)}, u32[]{:S(2)}) copy-start(f32[256,256]{1,0:T(8,128)} %param.5) | copy-start | bytes 786436
  0.7 1.6 %copy-start.4 = (f32[256,256]{1,0:T(8,128)S(1)}, f32[256,256]{1,0:T(8,128)}, u32[]{:S(2)}) copy-start(f32[256,256]{1,0:T(8,128)} %param.8) | copy-start | bytes 786436
  2.2 3.4 %copy-start.2 = (f32[256,256]{1,0:T(8,128)S(1)}, f32[256,256]{1,0:T(8,128)}, u32[]{:S(2)}) copy-start(f32[256,256]{1,0:T(8,128)} %param.6) | copy-start | bytes 786436
  2.7 14.5 %copy-start.3 = (s32[256,1024]{1,0:T(8,128)S(1)}, s32[256,1024]{1,0:T(8,128)}, u32[]{:S(2)}) copy-start(s32[256,1024]{1,0:T(8,128)} %param.9) | copy-start | bytes 3145732
  2.7 13.2 %collective-permute-start = (f32[256,256]{1,0:T(8,128)S(1)}, f32[256,256]{1,0:T(8,128)S(1)}, u32[]{:S(2)}, u32[]{:S(2)}) collective-permute-start(f32[256,256]{1,0:T(8,128)S(1)} %get-tuple-element.26), channel_id=1, source_target_pairs={{0,4},{1,5},{2,6},{3,7},{4,8},{5,9},{6,10},{7,11},{8,12},{9,13},{1... | collective-permute-start | bytes 786440 | tf_op jit(solution)/shard_map/ppermute | solution.py:21
  6.0 17.1 %collective-permute-start.3 = (f32[256,256]{1,0:T(8,128)S(1)}, f32[256,256]{1,0:T(8,128)S(1)}, u32[]{:S(2)}, u32[]{:S(2)}) collective-permute-start(f32[256,256]{1,0:T(8,128)S(1)} %get-tuple-element.25), channel_id=1, source_target_pairs={{0,8},{1,9},{2,10},{3,11},{8,16},{9,17},{10,18},{11,19},{16,24},{1... | collective-permute-start | bytes 786440 | tf_op jit(solution)/shard_map/ppermute | solution.py:21
  9.5 13.6 %collective-permute-start.2 = (f32[256,256]{1,0:T(8,128)S(1)}, f32[256,256]{1,0:T(8,128)S(1)}, u32[]{:S(2)}, u32[]{:S(2)}) collective-permute-start(f32[256,256]{1,0:T(8,128)S(1)} %broadcast_select_fusion.5), channel_id=1, source_target_pairs={{0,8},{1,9},{2,10},{3,11},{4,12},{5,13},{6,14},{7,15},{8,16},{9,17... | collective-permute-start | bytes 786440 | tf_op jit(solution)/shard_map/ppermute | solution.py:21
  15.8 8.0 %collective-permute-start.1 = (f32[256,256]{1,0:T(8,128)S(1)}, f32[256,256]{1,0:T(8,128)S(1)}, u32[]{:S(2)}, u32[]{:S(2)}) collective-permute-start(f32[256,256]{1,0:T(8,128)S(1)} %collective-permute-done), channel_id=1, source_target_pairs={{0,4},{1,5},{2,6},{3,7},{8,12},{9,13},{10,14},{11,15},{16,20},{17,... | collective-permute-start | bytes 786440 | tf_op jit(solution)/shard_map/ppermute | solution.py:21
  17.9 9.4 %collective-permute-start.4 = (f32[256,256]{1,0:T(8,128)S(1)}, f32[256,256]{1,0:T(8,128)S(1)}, u32[]{:S(2)}, u32[]{:S(2)}) collective-permute-start(f32[256,256]{1,0:T(8,128)S(1)} %multiply_add_fusion.6), channel_id=1, source_target_pairs={{0,4},{1,5},{2,6},{3,7},{4,8},{5,9},{6,10},{7,11},{8,12},{9,13},{1... | collective-permute-start | bytes 786440 | tf_op jit(solution)/shard_map/ppermute | solution.py:21
  28.1 9.7 %collective-permute-start.5 = (f32[256,256]{1,0:T(8,128)S(1)}, f32[256,256]{1,0:T(8,128)S(1)}, u32[]{:S(2)}, u32[]{:S(2)}) collective-permute-start(f32[256,256]{1,0:T(8,128)S(1)} %get-tuple-element.36), channel_id=1, source_target_pairs={{0,4},{1,5},{2,6},{3,7},{4,8},{5,9},{6,10},{7,11},{8,12},{9,13},{1... | collective-permute-start | bytes 786440 | tf_op jit(solution)/shard_map/ppermute | solution.py:21
  30.9 18.4 %collective-permute-start.8 = (f32[256,256]{1,0:T(8,128)S(1)}, f32[256,256]{1,0:T(8,128)S(1)}, u32[]{:S(2)}, u32[]{:S(2)}) collective-permute-start(f32[256,256]{1,0:T(8,128)S(1)} %get-tuple-element.35), channel_id=1, source_target_pairs={{0,9},{1,10},{2,11},{3,8},{8,17},{9,18},{10,19},{11,16},{16,25},{1... | collective-permute-start | bytes 786440 | tf_op jit(solution)/shard_map/ppermute | solution.py:21
  32.8 16.4 %collective-permute-start.7 = (f32[256,256]{1,0:T(8,128)S(1)}, f32[256,256]{1,0:T(8,128)S(1)}, u32[]{:S(2)}, u32[]{:S(2)}) collective-permute-start(f32[256,256]{1,0:T(8,128)S(1)} %broadcast_select_fusion.2), channel_id=1, source_target_pairs={{0,9},{1,10},{2,11},{3,8},{4,13},{5,14},{6,15},{7,12},{8,17},{9,18... | collective-permute-start | bytes 786440 | tf_op jit(solution)/shard_map/ppermute | solution.py:21
  37.8 11.4 %collective-permute-start.6 = (f32[256,256]{1,0:T(8,128)S(1)}, f32[256,256]{1,0:T(8,128)S(1)}, u32[]{:S(2)}, u32[]{:S(2)}) collective-permute-start(f32[256,256]{1,0:T(8,128)S(1)} %collective-permute-done.5), channel_id=1, source_target_pairs={{0,5},{1,6},{2,7},{3,4},{8,13},{9,14},{10,15},{11,12},{16,21},{17,... | collective-permute-start | bytes 786440 | tf_op jit(solution)/shard_map/ppermute | solution.py:21
  39.9 12.2 %collective-permute-start.9 = (f32[256,256]{1,0:T(8,128)S(1)}, f32[256,256]{1,0:T(8,128)S(1)}, u32[]{:S(2)}, u32[]{:S(2)}) collective-permute-start(f32[256,256]{1,0:T(8,128)S(1)} %multiply_add_fusion.1), channel_id=1, source_target_pairs={{0,5},{1,6},{2,7},{3,4},{4,9},{5,10},{6,11},{7,8},{8,13},{9,14},{1... | collective-permute-start | bytes 786440 | tf_op jit(solution)/shard_map/ppermute | solution.py:21

commit v3 on v1

--- a/solution.py
+++ b/solution.py
@@ -1,6 +1,8 @@
 import jax
 import jax.numpy as jnp
 from jax import lax
+from jax.experimental import pallas as pl
+from jax.experimental.pallas import tpu as pltpu
 from jax.sharding import PartitionSpec as P
 
 conf_scale = 0.5
@@ -21,6 +23,18 @@
     return lax.ppermute(value, ("blk", "group"), pairs)
 
 
+def halves(value):
+    high = value.astype(jnp.bfloat16)
+    return high, (value - high.astype(jnp.float32)).astype(jnp.bfloat16)
+
+
+def product(left, right, dims):
+    def dot(a, b):
+        return lax.dot_general(a, b, (dims, ((), ())), preferred_element_type=jnp.float32)
+
+    return dot(left[0], right[1]) + dot(left[1], right[0]) + dot(left[0], right[0])
+
+
 def weighted_gap(users, items, count_tile):
     predicted = lax.dot_general(users, items, (((1,), (1,)), ((), ())), precision=PREC)
     prefer = (count_tile > 0).astype(jnp.float32)
@@ -28,13 +42,39 @@
     return confidence * (predicted - prefer)
 
 
-def user_gradient(gap, users, items):
-    return 2.0 * jnp.dot(gap, items, precision=PREC) + 2.0 * ridge_weight * users
-
-
 def item_gradient(gap, users, items):
     product = lax.dot_general(gap, users, (((0,), (0,)), ((), ())), precision=PREC)
     return 2.0 * product + 2.0 * ridge_weight * items
+
+
+def pair_kernel(users_ref, items_ref, tile_ref, gap_ref, grad_ref):
+    users, items = users_ref[...], items_ref[...]
+    tile = tile_ref[...]
+    users_parts = halves(users)
+    predicted = product(users_parts, halves(items), ((1,), (1,)))
+    prefer = (tile > 0).astype(jnp.float32)
+    gap = (1.0 + conf_scale * tile.astype(jnp.float32)) * (predicted - prefer)
+    gap_ref[...] = gap
+    grad_ref[...] = 2.0 * product(halves(gap), users_parts, ((0,), (0,))) + 2.0 * ridge_weight * items
+
+
+def pair(users, items, counts, stratum):
+    rows = items.shape[0]
+    whole = pl.BlockSpec(items.shape, lambda i: (0, 0))
+    return pl.pallas_call(
+        pair_kernel,
+        out_shape=[jax.ShapeDtypeStruct((users.shape[0], rows), jnp.float32), jax.ShapeDtypeStruct(items.shape, jnp.float32)],
+        grid=(1,),
+        in_specs=[whole, whole, pl.BlockSpec((users.shape[0], rows), lambda i: (0, stratum))],
+        out_specs=[whole, whole],
+        compiler_params=pltpu.CompilerParams(vmem_limit_bytes=8 * 2**20),
+        cost_estimate=pl.CostEstimate(flops=12 * rows**3, bytes_accessed=5 * 4 * rows**2, transcendentals=0),
+        name="pair",
+    )(users, items, counts)
+
+
+def user_gradient(gap, users, items):
+    return 2.0 * jnp.dot(gap, items, precision=PREC) + 2.0 * ridge_weight * users
 
 
 def adagrad(factors, sums, gradient):
@@ -43,13 +83,14 @@
 
 
 def body(users, user_acc, items, item_acc, counts):
-    rows = items.shape[0]
-    tiles = [counts[:, s * rows : (s + 1) * rows] for s in range(4)]
     odd = lax.axis_index("blk") % 2 == 1
 
     def two_strata(users, user_acc, items, item_acc, first, up):
-        gap = weighted_gap(users, items, tiles[first])
-        grad_v = item_gradient(gap, users, items)
+        if first == 0:
+            gap = weighted_gap(users, items, counts[:, : items.shape[0]])
+            grad_v = item_gradient(gap, users, items)
+        else:
+            gap, grad_v = pair(users, items, counts, first)
         grad_u = user_gradient(gap, users, items)
         items, item_acc = adagrad(items, item_acc, grad_v)
         users, user_acc = adagrad(users, user_acc, grad_u)
@@ -59,8 +100,7 @@
         ahead = sent(jnp.where(odd, item_acc, items), lambda b, g: (b + 2, g + up))
         even_acc = sent(item_acc, lambda b, g: (b + 2, g + up) if b % 2 == 0 else None)
         passed = sent(visitor, lambda b, g: (b + 1, g + up) if b % 2 == 0 else None)
-        gap = weighted_gap(users, visitor, tiles[first + 1])
-        grad_v = item_gradient(gap, users, visitor)
+        gap, grad_v = pair(users, visitor, counts, first + 1)
         grad_u = user_gradient(gap, users, visitor)
         grad_v = sent(grad_v, lambda b, g: (b + 1, g + up))
         users, user_acc = adagrad(users, user_acc, grad_u)

time: 50.9 us -> 51 us (level)
  matrix products: 6.26 us -> 4.01 us
  Pallas kernels: 0 us -> 2.25 us
    pallas_call x0 -> x3, Pallas kernels: none -> 2.25 us  [pair(): pl.pallas_call(pair_kernel, out_shape=[jax.ShapeDtypeStruct((users.shape[...]
    dot_general x4 -> x1, matrix products: 1.62 us -> 0.41 us  [item_gradient(): lax.dot_general(gap, users, (((0,), (0,)), ((), ())), precision=PREC)]
    dot_general x4 -> x1, matrix products: 2.56 us -> 1.52 us  [weighted_gap(): lax.dot_general(users, items, (((1,), (1,)), ((), ())), precision=PREC)]
    sub x2 -> x3, other arithmetic: 0.94 us -> 1.03 us  [adagrad(): return (factors - step_rate * gradient / jnp.sqrt(sums), sums)]
  transfers between devices with their start and end apart: 10 -> 10, of which waited for: 7 -> 7; matrix products, arithmetic and copies ran while one was open for 7% -> 4% of each run, Pallas kernels for 0% -> 3%
where the time goes in v3:
time: 51 us; the launch traced here: 50.7 us
  starting transfers between devices  22.5 us (44%)
  waiting for transfers between devices  20 us (39%)
  matrix products  4.01 us (8%)
  Pallas kernels  2.25 us (4%)
  other arithmetic  1.1 us (2%)
  between operations  0.84 us (2%)
    ppermute x10, starting transfers between devices, sent(): return lax.ppermute(value, ('blk', 'group'), pairs)  22.5 us
    ppermute x10, waiting for transfers between devices, sent(): return lax.ppermute(value, ('blk', 'group'), pairs)  20 us
    pallas_call x3, Pallas kernels, pair(): pl.pallas_call(pair_kernel, out_shape=[jax.ShapeDtypeStruct((users.shape[...  2.25 us
    dot_general x4, matrix products, user_gradient(): jnp.dot(gap, items, precision=PREC)  2.08 us
    dot_general x1, matrix products, weighted_gap(): lax.dot_general(users, items, (((1,), (1,)), ((), ())), precision=PREC)  1.52 us
    sub x3, other arithmetic, adagrad(): return (factors - step_rate * gradient / jnp.sqrt(sums), sums)  1.03 us
  transfers between devices with their start and end apart: 10, of which 7 were waited for; matrix products, arithmetic and copies ran while one was open for 4% of the time, Pallas kernels for 3%

profile of v3, /device:TPU:0, one launch (start us, length us, event | category | flops | bytes accessed | tf_op | source)
XLA Modules:
  0.0 50.7 jit_solution(14552950422190735061)
XLA Ops:
  0.6 0.0 copy-start.2
  0.6 0.0 copy-start.1
  0.7 0.0 copy-start.4
  0.7 1.5 %fusion.5 = f32[256,256]{1,0:T(8,128)S(1)} fusion(f32[256,256]{1,0:T(8,128)} %param.5, f32[256,256]{1,0:T(8,128)} %param.7, s32[256,1024]{1,0:T(8,128)} %tile_ref.5), kind=kOutput, calls=%fused_computation.11 | convolution fusion | flops 101122048 | bytes 1048576 | tf_op jit(solution)/shard_map/dot_general | solution.py:39
  2.2 0.0 copy-done.2
  2.2 0.0 copy-done.1
  2.2 0.0 copy-done.4
  2.2 0.0 copy-start.3
  2.2 0.4 multiply_subtract_fusion.7
  2.7 0.0 copy-start
  2.7 3.0 %collective-permute-start = (f32[256,256]{1,0:T(8,128)S(1)}, f32[256,256]{1,0:T(8,128)S(1)}, u32[]{:S(2)}, u32[]{:S(2)}) collective-permute-start(f32[256,256]{1,0:T(8,128)S(1)} %get-tuple-element.17), channel_id=1, source_target_pairs={{0,4},{1,5},{2,6},{3,7},{4,8},{5,9},{6,10},{7,11},{8,12},{9,13},{1... | collective-permute-start | bytes 786440 | tf_op jit(solution)/shard_map/ppermute | solution.py:23
  5.7 0.0 copy-done.3
  5.7 0.3 multiply_subtract_fusion.6
  6.0 3.5 %collective-permute-start.4 = (f32[256,256]{1,0:T(8,128)S(1)}, f32[256,256]{1,0:T(8,128)S(1)}, u32[]{:S(2)}, u32[]{:S(2)}) collective-permute-start(f32[256,256]{1,0:T(8,128)S(1)} %get-tuple-element.16), channel_id=1, source_target_pairs={{0,8},{1,9},{2,10},{3,11},{8,16},{9,17},{10,18},{11,19},{16,24},{1... | collective-permute-start | bytes 786440 | tf_op jit(solution)/shard_map/ppermute | solution.py:23
  9.5 1.6 %collective-permute-start.2 = (f32[256,256]{1,0:T(8,128)S(1)}, f32[256,256]{1,0:T(8,128)S(1)}, u32[]{:S(2)}, u32[]{:S(2)}) collective-permute-start(f32[256,256]{1,0:T(8,128)S(1)} %broadcast_select_fusion.1), channel_id=1, source_target_pairs={{0,8},{1,9},{2,10},{3,11},{4,12},{5,13},{6,14},{7,15},{8,16},{9,17... | collective-permute-start | bytes 786440 | tf_op jit(solution)/shard_map/ppermute | solution.py:23
  11.2 4.7 %collective-permute-done.items_ref = f32[256,256]{1,0:T(8,128)S(1)} collective-permute-done((f32[256,256]{1,0:T(8,128)S(1)}, f32[256,256]{1,0:T(8,128)S(1)}, u32[]{:S(2)}, u32[]{:S(2)}) %collective-permute-start) | collective-permute-done | bytes 262176 | tf_op jit(solution)/shard_map/ppermute | solution.py:23
  15.8 0.0 copy-done
  15.8 0.7 %pair.3 = (f32[256,256]{1,0:T(8,128)S(1)}, f32[256,256]{1,0:T(8,128)S(1)}) custom-call(f32[256,256]{1,0:T(8,128)S(1)} %get-tuple-element.18.users_ref, f32[256,256]{1,0:T(8,128)S(1)} %collective-permute-done.items_ref, s32[256,1024]{1,0:T(8,128)S(1)} %copy-done), custom_call_target="tpu_custom_call" | custom-call | flops 201326592 | bytes 1310720 | tf_op jit(solution)/shard_map/pair/pallas_call | solution.py:64
  16.6 0.1 collective-permute-start.3
  16.7 3.4 %collective-permute-start.1 = (f32[256,256]{1,0:T(8,128)S(1)}, f32[256,256]{1,0:T(8,128)S(1)}, u32[]{:S(2)}, u32[]{:S(2)}) collective-permute-start(f32[256,256]{1,0:T(8,128)S(1)} %collective-permute-done.items_ref), channel_id=1, source_target_pairs={{0,4},{1,5},{2,6},{3,7},{8,12},{9,13},{10,14},{11,15},{16,20},{17,... | collective-permute-start | bytes 786440 | tf_op jit(solution)/shard_map/ppermute | solution.py:23
  20.0 0.3 multiply_subtract_fusion.4
  20.4 2.8 %collective-permute-done.2 = f32[256,256]{1,0:T(8,128)S(1)} collective-permute-done((f32[256,256]{1,0:T(8,128)S(1)}, f32[256,256]{1,0:T(8,128)S(1)}, u32[]{:S(2)}, u32[]{:S(2)}) %collective-permute-start.2) | collective-permute-done | bytes 262176 | tf_op jit(solution)/shard_map/ppermute | solution.py:23
  23.1 0.0 collective-permute-done.4
  23.1 3.1 %collective-permute-done.3 = f32[256,256]{1,0:T(8,128)S(1)} collective-permute-done((f32[256,256]{1,0:T(8,128)S(1)}, f32[256,256]{1,0:T(8,128)S(1)}, u32[]{:S(2)}, u32[]{:S(2)}) %collective-permute-start.3) | collective-permute-done | bytes 262176 | tf_op jit(solution)/shard_map/ppermute | solution.py:23
  26.2 0.5 collective-permute-done.1
  26.7 0.1 multiply_subtract_fusion.5.items_ref
  26.8 0.8 %pair.4 = (f32[256,256]{1,0:T(8,128)S(1)}, f32[256,256]{1,0:T(8,128)S(1)}) custom-call(f32[256,256]{1,0:T(8,128)S(1)} %get-tuple-element.34.users_ref, f32[256,256]{1,0:T(8,128)S(1)} %multiply_subtract_fusion.5.items_ref, s32[256,1024]{1,0:T(8,128)S(1)} %copy-done), custom_call_target="tpu_custom_call" | custom-call | flops 201326592 | bytes 1310720 | tf_op jit(solution)/shard_map/pair/pallas_call | solution.py:64
  27.6 0.1 multiply_subtract_fusion.3
  27.7 2.5 %collective-permute-start.5 = (f32[256,256]{1,0:T(8,128)S(1)}, f32[256,256]{1,0:T(8,128)S(1)}, u32[]{:S(2)}, u32[]{:S(2)}) collective-permute-start(f32[256,256]{1,0:T(8,128)S(1)} %get-tuple-element.26), channel_id=1, source_target_pairs={{0,4},{1,5},{2,6},{3,7},{4,8},{5,9},{6,10},{7,11},{8,12},{9,13},{1... | collective-permute-start | bytes 786440 | tf_op jit(solution)/shard_map/ppermute | solution.py:23
  30.2 0.3 multiply_subtract_fusion.2
  30.5 1.9 %collective-permute-start.9 = (f32[256,256]{1,0:T(8,128)S(1)}, f32[256,256]{1,0:T(8,128)S(1)}, u32[]{:S(2)}, u32[]{:S(2)}) collective-permute-start(f32[256,256]{1,0:T(8,128)S(1)} %get-tuple-element.25), channel_id=1, source_target_pairs={{0,9},{1,10},{2,11},{3,8},{8,17},{9,18},{10,19},{11,16},{16,25},{1... | collective-permute-start | bytes 786440 | tf_op jit(solution)/shard_map/ppermute | solution.py:23
  32.5 2.0 %collective-permute-start.7 = (f32[256,256]{1,0:T(8,128)S(1)}, f32[256,256]{1,0:T(8,128)S(1)}, u32[]{:S(2)}, u32[]{:S(2)}) collective-permute-start(f32[256,256]{1,0:T(8,128)S(1)} %broadcast_select_fusion), channel_id=1, source_target_pairs={{0,9},{1,10},{2,11},{3,8},{4,13},{5,14},{6,15},{7,12},{8,17},{9,18... | collective-permute-start | bytes 786440 | tf_op jit(solution)/shard_map/ppermute | solution.py:23
  34.5 2.8 %collective-permute-done.5.items_ref = f32[256,256]{1,0:T(8,128)S(1)} collective-permute-done((f32[256,256]{1,0:T(8,128)S(1)}, f32[256,256]{1,0:T(8,128)S(1)}, u32[]{:S(2)}, u32[]{:S(2)}) %collective-permute-start.5) | collective-permute-done | bytes 262176 | tf_op jit(solution)/shard_map/ppermute | solution.py:23
  37.2 0.7 %pair.5 = (f32[256,256]{1,0:T(8,128)S(1)}, f32[256,256]{1,0:T(8,128)S(1)}) custom-call(f32[256,256]{1,0:T(8,128)S(1)} %get-tuple-element.23.users_ref, f32[256,256]{1,0:T(8,128)S(1)} %collective-permute-done.5.items_ref, s32[256,1024]{1,0:T(8,128)S(1)} %copy-done), custom_call_target="tpu_custom_call" | custom-call | flops 201326592 | bytes 1310720 | tf_op jit(solution)/shard_map/pair/pallas_call | solution.py:64
  38.0 0.1 collective-permute-start.8
  38.0 4.5 %collective-permute-start.6 = (f32[256,256]{1,0:T(8,128)S(1)}, f32[256,256]{1,0:T(8,128)S(1)}, u32[]{:S(2)}, u32[]{:S(2)}) collective-permute-start(f32[256,256]{1,0:T(8,128)S(1)} %collective-permute-done.5.items_ref), channel_id=1, source_target_pairs={{0,5},{1,6},{2,7},{3,4},{8,13},{9,14},{10,15},{11,12},{16,21},{17,... | collective-permute-start | bytes 786440 | tf_op jit(solution)/shard_map/ppermute | solution.py:23
  42.6 1.1 %multiply_subtract_fusion.1 = (f32[256,256]{1,0:T(8,128)}, f32[256,256]{1,0:T(8,128)}) fusion(f32[256,256]{1,0:T(8,128)S(1)} %get-tuple-element.23.users_ref, f32[256,256]{1,0:T(8,128)S(1)} %get-tuple-element.35, f32[256,256]{1,0:T(8,128)S(1)} %get-tuple-element.41, f32[256,256]{1,0:T(8,128)S(1)} %get-tuple-element.24, ...), kind=kOutput, calls=%fused_computation.14 | convolution fusion | flops 101318656 | bytes 1835008 | tf_op jit(solution)/shard_map/dot_general | solution.py:77
  43.7 5.4 %collective-permute-done.7 = f32[256,256]{1,0:T(8,128)S(1)} collective-permute-done((f32[256,256]{1,0:T(8,128)S(1)}, f32[256,256]{1,0:T(8,128)S(1)}, u32[]{:S(2)}, u32[]{:S(2)}) %collective-permute-start.7) | collective-permute-done | bytes 262176 | tf_op jit(solution)/shard_map/ppermute | solution.py:23
  49.1 0.0 collective-permute-done.9
  49.1 0.8 %collective-permute-done.8 = f32[256,256]{1,0:T(8,128)S(1)} collective-permute-done((f32[256,256]{1,0:T(8,128)S(1)}, f32[256,256]{1,0:T(8,128)S(1)}, u32[]{:S(2)}, u32[]{:S(2)}) %collective-permute-start.8) | collective-permute-done | bytes 262176 | tf_op jit(solution)/shard_map/ppermute | solution.py:23
  49.9 0.0 collective-permute-done.6
  49.9 0.9 %multiply_subtract_fusion = (f32[256,256]{1,0:T(8,128)}, f32[256,256]{1,0:T(8,128)}) fusion(f32[256,256]{1,0:T(8,128)S(1)} %collective-permute-done.8, f32[256,256]{1,0:T(8,128)S(1)} %collective-permute-done.6, f32[256,256]{1,0:T(8,128)S(1)} %collective-permute-done.7, pred[]{:T(512)S(6)} %eq.5, f32[256,256]{1,0:T(8,128)S(1)} %collective-permute-done.9), kind=kLoop, calls=%fused_computation.12 | loop fusion | flops 458752 | bytes 1572865 | tf_op jit(solution)/shard_map/sub | solution.py:82
  (2 shorter events, 0.1 us)
Async XLA Ops:
  0.6 1.6 %copy-start.2 = (f32[256,256]{1,0:T(8,128)S(1)}, f32[256,256]{1,0:T(8,128)}, u32[]{:S(2)}) copy-start(f32[256,256]{1,0:T(8,128)} %param.7) | copy-start | bytes 786436
  0.6 1.6 %copy-start.1 = (f32[256,256]{1,0:T(8,128)S(1)}, f32[256,256]{1,0:T(8,128)}, u32[]{:S(2)}) copy-start(f32[256,256]{1,0:T(8,128)} %param.5) | copy-start | bytes 786436
  0.7 1.6 %copy-start.4 = (f32[256,256]{1,0:T(8,128)S(1)}, f32[256,256]{1,0:T(8,128)}, u32[]{:S(2)}) copy-start(f32[256,256]{1,0:T(8,128)} %param.8) | copy-start | bytes 786436
  2.2 3.4 %copy-start.3 = (f32[256,256]{1,0:T(8,128)S(1)}, f32[256,256]{1,0:T(8,128)}, u32[]{:S(2)}) copy-start(f32[256,256]{1,0:T(8,128)} %param.6) | copy-start | bytes 786436
  2.7 13.2 %copy-start = (s32[256,1024]{1,0:T(8,128)S(1)}, s32[256,1024]{1,0:T(8,128)}, u32[]{:S(2)}) copy-start(s32[256,1024]{1,0:T(8,128)} %tile_ref.5) | copy-start | bytes 3145732
  2.7 13.2 %collective-permute-start = (f32[256,256]{1,0:T(8,128)S(1)}, f32[256,256]{1,0:T(8,128)S(1)}, u32[]{:S(2)}, u32[]{:S(2)}) collective-permute-start(f32[256,256]{1,0:T(8,128)S(1)} %get-tuple-element.17), channel_id=1, source_target_pairs={{0,4},{1,5},{2,6},{3,7},{4,8},{5,9},{6,10},{7,11},{8,12},{9,13},{1... | collective-permute-start | bytes 786440 | tf_op jit(solution)/shard_map/ppermute | solution.py:23
  6.0 17.1 %collective-permute-start.4 = (f32[256,256]{1,0:T(8,128)S(1)}, f32[256,256]{1,0:T(8,128)S(1)}, u32[]{:S(2)}, u32[]{:S(2)}) collective-permute-start(f32[256,256]{1,0:T(8,128)S(1)} %get-tuple-element.16), channel_id=1, source_target_pairs={{0,8},{1,9},{2,10},{3,11},{8,16},{9,17},{10,18},{11,19},{16,24},{1... | collective-permute-start | bytes 786440 | tf_op jit(solution)/shard_map/ppermute | solution.py:23
  9.5 13.6 %collective-permute-start.2 = (f32[256,256]{1,0:T(8,128)S(1)}, f32[256,256]{1,0:T(8,128)S(1)}, u32[]{:S(2)}, u32[]{:S(2)}) collective-permute-start(f32[256,256]{1,0:T(8,128)S(1)} %broadcast_select_fusion.1), channel_id=1, source_target_pairs={{0,8},{1,9},{2,10},{3,11},{4,12},{5,13},{6,14},{7,15},{8,16},{9,17... | collective-permute-start | bytes 786440 | tf_op jit(solution)/shard_map/ppermute | solution.py:23
  16.6 9.6 %collective-permute-start.3 = (f32[256,256]{1,0:T(8,128)S(1)}, f32[256,256]{1,0:T(8,128)S(1)}, u32[]{:S(2)}, u32[]{:S(2)}) collective-permute-start(f32[256,256]{1,0:T(8,128)S(1)} %get-tuple-element.19), channel_id=1, source_target_pairs={{0,4},{1,5},{2,6},{3,7},{4,8},{5,9},{6,10},{7,11},{8,12},{9,13},{1... | collective-permute-start | bytes 786440 | tf_op jit(solution)/shard_map/ppermute | solution.py:23
  16.7 10.1 %collective-permute-start.1 = (f32[256,256]{1,0:T(8,128)S(1)}, f32[256,256]{1,0:T(8,128)S(1)}, u32[]{:S(2)}, u32[]{:S(2)}) collective-permute-start(f32[256,256]{1,0:T(8,128)S(1)} %collective-permute-done.items_ref), channel_id=1, source_target_pairs={{0,4},{1,5},{2,6},{3,7},{8,12},{9,13},{10,14},{11,15},{16,20},{17,... | collective-permute-start | bytes 786440 | tf_op jit(solution)/shard_map/ppermute | solution.py:23
  27.7 9.6 %collective-permute-start.5 = (f32[256,256]{1,0:T(8,128)S(1)}, f32[256,256]{1,0:T(8,128)S(1)}, u32[]{:S(2)}, u32[]{:S(2)}) collective-permute-start(f32[256,256]{1,0:T(8,128)S(1)} %get-tuple-element.26), channel_id=1, source_target_pairs={{0,4},{1,5},{2,6},{3,7},{4,8},{5,9},{6,10},{7,11},{8,12},{9,13},{1... | collective-permute-start | bytes 786440 | tf_op jit(solution)/shard_map/ppermute | solution.py:23
  30.5 18.5 %collective-permute-start.9 = (f32[256,256]{1,0:T(8,128)S(1)}, f32[256,256]{1,0:T(8,128)S(1)}, u32[]{:S(2)}, u32[]{:S(2)}) collective-permute-start(f32[256,256]{1,0:T(8,128)S(1)} %get-tuple-element.25), channel_id=1, source_target_pairs={{0,9},{1,10},{2,11},{3,8},{8,17},{9,18},{10,19},{11,16},{16,25},{1... | collective-permute-start | bytes 786440 | tf_op jit(solution)/shard_map/ppermute | solution.py:23
  32.5 16.6 %collective-permute-start.7 = (f32[256,256]{1,0:T(8,128)S(1)}, f32[256,256]{1,0:T(8,128)S(1)}, u32[]{:S(2)}, u32[]{:S(2)}) collective-permute-start(f32[256,256]{1,0:T(8,128)S(1)} %broadcast_select_fusion), channel_id=1, source_target_pairs={{0,9},{1,10},{2,11},{3,8},{4,13},{5,14},{6,15},{7,12},{8,17},{9,18... | collective-permute-start | bytes 786440 | tf_op jit(solution)/shard_map/ppermute | solution.py:23
  38.0 11.9 %collective-permute-start.8 = (f32[256,256]{1,0:T(8,128)S(1)}, f32[256,256]{1,0:T(8,128)S(1)}, u32[]{:S(2)}, u32[]{:S(2)}) collective-permute-start(f32[256,256]{1,0:T(8,128)S(1)} %get-tuple-element.27), channel_id=1, source_target_pairs={{0,5},{1,6},{2,7},{3,4},{4,9},{5,10},{6,11},{7,8},{8,13},{9,14},{1... | collective-permute-start | bytes 786440 | tf_op jit(solution)/shard_map/ppermute | solution.py:23
  38.0 11.8 %collective-permute-start.6 = (f32[256,256]{1,0:T(8,128)S(1)}, f32[256,256]{1,0:T(8,128)S(1)}, u32[]{:S(2)}, u32[]{:S(2)}) collective-permute-start(f32[256,256]{1,0:T(8,128)S(1)} %collective-permute-done.5.items_ref), channel_id=1, source_target_pairs={{0,5},{1,6},{2,7},{3,4},{8,13},{9,14},{10,15},{11,12},{16,21},{17,... | collective-permute-start | bytes 786440 | tf_op jit(solution)/shard_map/ppermute | solution.py:23

commit v4 on v2

v4 whole, which is shorter than its diff:
```python
import jax
import jax.numpy as jnp
from jax import lax
from jax.experimental import pallas as pl
from jax.experimental.pallas import tpu as pltpu
from jax.sharding import PartitionSpec as P

conf_scale = 0.5
ridge_weight = 0.01
step_rate = 0.1

PREC = lax.Precision.HIGH


def sent(value, where):
    n_blk, n_group = lax.axis_size("blk"), lax.axis_size("group")
    pairs = []
    for b in range(n_blk):
        for g in range(n_group):
            target = where(b, g)
            if target is not None:
                pairs.append((b * n_group + g, target[0] % n_blk * n_group + target[1] % n_group))
    return lax.ppermute(value, ("blk", "group"), pairs)


def halves(value):
    high = value.astype(jnp.bfloat16)
    return high, (value - high.astype(jnp.float32)).astype(jnp.bfloat16)


def product(left, right, dims):
    def dot(a, b):
        return lax.dot_general(a, b, (dims, ((), ())), preferred_element_type=jnp.float32)

    return dot(left[0], right[1]) + dot(left[1], right[0]) + dot(left[0], right[0])


def weighted_gap(users, items, count_tile):
    predicted = lax.dot_general(users, items, (((1,), (1,)), ((), ())), precision=PREC)
    prefer = (count_tile > 0).astype(jnp.float32)
    confidence = 1.0 + conf_scale * count_tile.astype(jnp.float32)
    return confidence * (predicted - prefer)


def item_gradient(gap, users, items):
    product = lax.dot_general(gap, users, (((0,), (0,)), ((), ())), precision=PREC)
    return 2.0 * product + 2.0 * ridge_weight * items


def pair_products(users, items, tile):
    users_parts = halves(users)
    predicted = product(users_parts, halves(items), ((1,), (1,)))
    prefer = (tile > 0).astype(jnp.float32)
    gap = (1.0 + conf_scale * tile.astype(jnp.float32)) * (predicted - prefer)
    return gap, 2.0 * product(halves(gap), users_parts, ((0,), (0,))) + 2.0 * ridge_weight * items


def visit_kernel(users_ref, items_ref, tile_ref, gap_ref, grad_ref):
    gap_ref[...], grad_ref[...] = pair_products(users_ref[...], items_ref[...], tile_ref[...])


def local_kernel(
    odd_ref, passed_ref, ahead_ref, even_acc_ref, old_grad_ref, users_ref, tile_ref, items_ref, gap_ref, new_items_ref, new_acc_ref
):
    odd = odd_ref[0] == 1
    ahead = ahead_ref[...]
    items, acc = adagrad(
        jnp.where(odd, passed_ref[...], ahead), jnp.where(odd, ahead, even_acc_ref[...]), old_grad_ref[...]
    )
    gap, grad = pair_products(users_ref[...], items, tile_ref[...])
    items_ref[...], gap_ref[...] = items, gap
    new_items_ref[...], new_acc_ref[...] = adagrad(items, acc, grad)


def on_vmem(kernel, name, outputs, *operands):
    here = pl.BlockSpec(memory_space=pltpu.VMEM)
    scalars = pl.BlockSpec(memory_space=pltpu.SMEM)
    shape = operands[-1].shape
    return pl.pallas_call(
        kernel,
        out_shape=[jax.ShapeDtypeStruct(shape, jnp.float32)] * outputs,
        in_specs=[scalars if operand.ndim == 1 else here for operand in operands],
        out_specs=[here] * outputs,
        compiler_params=pltpu.CompilerParams(vmem_limit_bytes=8 * 2**20),
        cost_estimate=pl.CostEstimate(flops=12 * shape[0] ** 3, bytes_accessed=5 * 4 * shape[0] ** 2, transcendentals=0),
        name=name,
    )(*operands)


def user_gradient(gap, users, items):
    return 2.0 * jnp.dot(gap, items, precision=PREC) + 2.0 * ridge_weight * users


def adagrad(factors, sums, gradient):
    sums = sums + gradient * gradient
    return factors - step_rate * gradient / jnp.sqrt(sums), sums


def body(users, user_acc, items, item_acc, counts):
    rows = items.shape[0]
    tiles = [counts[:, s * rows : (s + 1) * rows] for s in range(4)]
    odd = lax.axis_index("blk") % 2 == 1
    odd_flag = odd.astype(jnp.int32).reshape(1)

    def send_off(users, items, item_acc, up):
        visitor = sent(items, lambda b, g: (b + 1, g))
        items, item_acc, users = lax.optimization_barrier((items, item_acc, users))
        ahead = sent(jnp.where(odd, item_acc, items), lambda b, g: (b + 2, g + up))
        even_acc = sent(item_acc, lambda b, g: (b + 2, g + up) if b % 2 == 0 else None)
        passed = sent(visitor, lambda b, g: (b + 1, g + up) if b % 2 == 0 else None)
        return users, visitor, (passed, ahead, even_acc)

    def visit(users, user_acc, visitor, tile, up):
        gap, grad = on_vmem(visit_kernel, "visit", 2, users, visitor, tile)
        grad = sent(grad, lambda b, g: (b + 1, g + up))
        users, user_acc = adagrad(users, user_acc, user_gradient(gap, users, visitor))
        return users, user_acc, grad

    gap = weighted_gap(users, items, tiles[0])
    new_items, new_acc = adagrad(items, item_acc, item_gradient(gap, users, items))
    users, user_acc = adagrad(users, user_acc, user_gradient(gap, users, items))
    users, visitor, state = send_off(users, new_items, new_acc, 0)
    users, user_acc, grad = visit(users, user_acc, visitor, tiles[1], 0)

    items, gap, new_items, new_acc = on_vmem(local_kernel, "local", 4, odd_flag, *state, grad, users, tiles[2])
    users, user_acc = adagrad(users, user_acc, user_gradient(gap, users, items))
    users, visitor, (passed, ahead, even_acc) = send_off(users, new_items, new_acc, 1)
    users, user_acc, grad = visit(users, user_acc, visitor, tiles[3], 1)

    items, item_acc = adagrad(jnp.where(odd, passed, ahead), jnp.where(odd, ahead, even_acc), grad)
    return users, user_acc, items, item_acc


def solution(mesh):
    spec = P(("blk", "group"), None)
    return jax.shard_map(body, mesh=mesh, in_specs=(spec,) * 5, out_specs=(spec,) * 4, check_vma=False)
```

time: 53.2 us -> 50.9 us (0.957)
  waiting for transfers between devices: 27 us -> 19.9 us
  starting transfers between devices: 17.7 us -> 22.5 us
  Pallas kernels: 0 us -> 2.42 us
  matrix products: 6.25 us -> 4.01 us
    ppermute x10, waiting for transfers between devices: 27 us -> 19.9 us  [sent(): return lax.ppermute(value, ('blk', 'group'), pairs)]
    ppermute x10, starting transfers between devices: 17.7 us -> 22.5 us  [sent(): return lax.ppermute(value, ('blk', 'group'), pairs)]
    pallas_call x0 -> x3, Pallas kernels: none -> 2.42 us  [on_vmem(): pl.pallas_call(kernel, out_shape=[jax.ShapeDtypeStruct(shape, jnp.float32...]
    dot_general x4 -> x1, matrix products: 1.61 us -> 0.41 us  [item_gradient(): lax.dot_general(gap, users, (((0,), (0,)), ((), ())), precision=PREC)]
    dot_general x4 -> x1, matrix products: 2.57 us -> 1.52 us  [weighted_gap(): lax.dot_general(users, items, (((1,), (1,)), ((), ())), precision=PREC)]
  transfers between devices with their start and end apart: 10 -> 10, of which waited for: 7 -> 6; matrix products, arithmetic and copies ran while one was open for 7% -> 4% of each run, Pallas kernels for 0% -> 3%
where the time goes in v4:
time: 50.9 us; the launch traced here: 50.7 us
  starting transfers between devices  22.5 us (44%)
  waiting for transfers between devices  19.9 us (39%)
  matrix products  4.01 us (8%)
  Pallas kernels  2.42 us (5%)
  other arithmetic  0.93 us (2%)
  between operations  0.84 us (2%)
    ppermute x10, starting transfers between devices, sent(): return lax.ppermute(value, ('blk', 'group'), pairs)  22.5 us
    ppermute x10, waiting for transfers between devices, sent(): return lax.ppermute(value, ('blk', 'group'), pairs)  19.9 us
    pallas_call x3, Pallas kernels, on_vmem(): pl.pallas_call(kernel, out_shape=[jax.ShapeDtypeStruct(shape, jnp.float32...  2.42 us
    dot_general x4, matrix products, user_gradient(): jnp.dot(gap, items, precision=PREC)  2.08 us
    dot_general x1, matrix products, weighted_gap(): lax.dot_general(users, items, (((1,), (1,)), ((), ())), precision=PREC)  1.52 us
  transfers between devices with their start and end apart: 10, of which 6 were waited for; matrix products, arithmetic and copies ran while one was open for 4% of the time, Pallas kernels for 3%

profile of v4, /device:TPU:0, one launch (start us, length us, event | category | flops | bytes accessed | tf_op | source)
XLA Modules:
  0.0 50.7 jit_solution(455073269572512983)
XLA Ops:
  0.6 0.0 copy-start.1
  0.6 0.0 copy-start
  0.7 0.0 copy-start.4
  0.7 1.5 %fusion.5 = f32[256,256]{1,0:T(8,128)S(1)} fusion(f32[256,256]{1,0:T(8,128)} %param.5, f32[256,256]{1,0:T(8,128)} %param.7, s32[256,1024]{1,0:T(8,128)} %param.9), kind=kOutput, calls=%fused_computation.11 | convolution fusion | flops 101122048 | bytes 1048576 | tf_op jit(solution)/shard_map/dot_general | solution.py:39
  2.2 0.0 copy-done.1
  2.2 0.0 copy-done
  2.2 0.0 copy-done.4
  2.2 0.0 copy-start.3
  2.2 0.4 multiply_subtract_fusion.5
  2.7 0.0 copy-start.2
  2.7 3.0 %collective-permute-start = (f32[256,256]{1,0:T(8,128)S(1)}, f32[256,256]{1,0:T(8,128)S(1)}, u32[]{:S(2)}, u32[]{:S(2)}) collective-permute-start(f32[256,256]{1,0:T(8,128)S(1)} %get-tuple-element.19), channel_id=1, source_target_pairs={{0,4},{1,5},{2,6},{3,7},{4,8},{5,9},{6,10},{7,11},{8,12},{9,13},{1... | collective-permute-start | bytes 786440 | tf_op jit(solution)/shard_map/ppermute | solution.py:23
  5.7 0.0 copy-done.3
  5.7 0.3 multiply_subtract_fusion.4
  6.0 3.5 %collective-permute-start.3 = (f32[256,256]{1,0:T(8,128)S(1)}, f32[256,256]{1,0:T(8,128)S(1)}, u32[]{:S(2)}, u32[]{:S(2)}) collective-permute-start(f32[256,256]{1,0:T(8,128)S(1)} %get-tuple-element.18), channel_id=1, source_target_pairs={{0,8},{1,9},{2,10},{3,11},{8,16},{9,17},{10,18},{11,19},{16,24},{1... | collective-permute-start | bytes 786440 | tf_op jit(solution)/shard_map/ppermute | solution.py:23
  9.5 1.6 %collective-permute-start.2 = (f32[256,256]{1,0:T(8,128)S(1)}, f32[256,256]{1,0:T(8,128)S(1)}, u32[]{:S(2)}, u32[]{:S(2)}) collective-permute-start(f32[256,256]{1,0:T(8,128)S(1)} %broadcast_select_fusion.1), channel_id=1, source_target_pairs={{0,8},{1,9},{2,10},{3,11},{4,12},{5,13},{6,14},{7,15},{8,16},{9,17... | collective-permute-start | bytes 786440 | tf_op jit(solution)/shard_map/ppermute | solution.py:23
  11.2 0.0 copy-done.2
  11.2 0.1 fusion.6
  11.2 4.6 %collective-permute-done.items_ref = f32[256,256]{1,0:T(8,128)S(1)} collective-permute-done((f32[256,256]{1,0:T(8,128)S(1)}, f32[256,256]{1,0:T(8,128)S(1)}, u32[]{:S(2)}, u32[]{:S(2)}) %collective-permute-start) | collective-permute-done | bytes 262176 | tf_op jit(solution)/shard_map/ppermute | solution.py:23
  15.8 0.8 %visit.2 = (f32[256,256]{1,0:T(8,128)S(1)}, f32[256,256]{1,0:T(8,128)S(1)}) custom-call(f32[256,256]{1,0:T(8,128)S(1)} %get-tuple-element.20.users_ref, f32[256,256]{1,0:T(8,128)S(1)} %collective-permute-done.items_ref, s32[256,256]{1,0:T(8,128)S(1)} %get-tuple-element.41.tile_ref), custom_call_target="tpu_custom_call" | custom-call | flops 201326592 | bytes 1310720 | tf_op jit(solution)/shard_map/visit/pallas_call | solution.py:79
  16.6 0.1 collective-permute-start.4
  16.7 3.4 %collective-permute-start.1 = (f32[256,256]{1,0:T(8,128)S(1)}, f32[256,256]{1,0:T(8,128)S(1)}, u32[]{:S(2)}, u32[]{:S(2)}) collective-permute-start(f32[256,256]{1,0:T(8,128)S(1)} %collective-permute-done.items_ref), channel_id=1, source_target_pairs={{0,4},{1,5},{2,6},{3,7},{8,12},{9,13},{10,14},{11,15},{16,20},{17,... | collective-permute-start | bytes 786440 | tf_op jit(solution)/shard_map/ppermute | solution.py:23
  20.0 0.3 multiply_subtract_fusion.3
  20.4 2.8 %collective-permute-done.2.ahead_ref = f32[256,256]{1,0:T(8,128)S(1)} collective-permute-done((f32[256,256]{1,0:T(8,128)S(1)}, f32[256,256]{1,0:T(8,128)S(1)}, u32[]{:S(2)}, u32[]{:S(2)}) %collective-permute-start.2) | collective-permute-done | bytes 262176 | tf_op jit(solution)/shard_map/ppermute | solution.py:23
  23.1 0.0 collective-permute-done.3.even_acc_ref
  23.1 3.6 %collective-permute-done.1.passed_ref = f32[256,256]{1,0:T(8,128)S(1)} collective-permute-done((f32[256,256]{1,0:T(8,128)S(1)}, f32[256,256]{1,0:T(8,128)S(1)}, u32[]{:S(2)}, u32[]{:S(2)}) %collective-permute-start.1) | collective-permute-done | bytes 262176 | tf_op jit(solution)/shard_map/ppermute | solution.py:23
  26.7 0.0 collective-permute-done.4.old_grad_ref
  26.7 0.9 %local.1 = (f32[256,256]{1,0:T(8,128)S(1)}, f32[256,256]{1,0:T(8,128)S(1)}, f32[256,256]{1,0:T(8,128)S(1)}, f32[256,256]{1,0:T(8,128)S(1)}) custom-call(s32[1]{0:T(128)} %bitcast.odd_ref, f32[256,256]{1,0:T(8,128)S(1)} %collective-permute-done.1.passed_ref, f32[256,256]{1,0:T(8,128)S(1)} %collective-permute-done.2.ahead_ref, ...), custom_call_target="tpu_custom_call" | custom-call | flops 201326592 | bytes 1310720 | tf_op jit(solution)/shard_map/local/pallas_call | solution.py:79
  27.7 2.5 %collective-permute-start.5 = (f32[256,256]{1,0:T(8,128)S(1)}, f32[256,256]{1,0:T(8,128)S(1)}, u32[]{:S(2)}, u32[]{:S(2)}) collective-permute-start(f32[256,256]{1,0:T(8,128)S(1)} %get-tuple-element.30), channel_id=1, source_target_pairs={{0,4},{1,5},{2,6},{3,7},{4,8},{5,9},{6,10},{7,11},{8,12},{9,13},{1... | collective-permute-start | bytes 786440 | tf_op jit(solution)/shard_map/ppermute | solution.py:23
  30.2 0.3 multiply_subtract_fusion.2
  30.5 1.9 %collective-permute-start.9 = (f32[256,256]{1,0:T(8,128)S(1)}, f32[256,256]{1,0:T(8,128)S(1)}, u32[]{:S(2)}, u32[]{:S(2)}) collective-permute-start(f32[256,256]{1,0:T(8,128)S(1)} %get-tuple-element.29), channel_id=1, source_target_pairs={{0,9},{1,10},{2,11},{3,8},{8,17},{9,18},{10,19},{11,16},{16,25},{1... | collective-permute-start | bytes 786440 | tf_op jit(solution)/shard_map/ppermute | solution.py:23
  32.5 2.0 %collective-permute-start.7 = (f32[256,256]{1,0:T(8,128)S(1)}, f32[256,256]{1,0:T(8,128)S(1)}, u32[]{:S(2)}, u32[]{:S(2)}) collective-permute-start(f32[256,256]{1,0:T(8,128)S(1)} %broadcast_select_fusion), channel_id=1, source_target_pairs={{0,9},{1,10},{2,11},{3,8},{4,13},{5,14},{6,15},{7,12},{8,17},{9,18... | collective-permute-start | bytes 786440 | tf_op jit(solution)/shard_map/ppermute | solution.py:23
  34.5 2.8 %collective-permute-done.5.items_ref = f32[256,256]{1,0:T(8,128)S(1)} collective-permute-done((f32[256,256]{1,0:T(8,128)S(1)}, f32[256,256]{1,0:T(8,128)S(1)}, u32[]{:S(2)}, u32[]{:S(2)}) %collective-permute-start.5) | collective-permute-done | bytes 262176 | tf_op jit(solution)/shard_map/ppermute | solution.py:23
  37.2 0.8 %visit.3 = (f32[256,256]{1,0:T(8,128)S(1)}, f32[256,256]{1,0:T(8,128)S(1)}) custom-call(f32[256,256]{1,0:T(8,128)S(1)} %get-tuple-element.27.users_ref, f32[256,256]{1,0:T(8,128)S(1)} %collective-permute-done.5.items_ref, s32[256,256]{1,0:T(8,128)S(1)} %get-tuple-element.40.tile_ref), custom_call_target="tpu_custom_call" | custom-call | flops 201326592 | bytes 1310720 | tf_op jit(solution)/shard_map/visit/pallas_call | solution.py:79
  38.0 0.1 collective-permute-start.8
  38.0 4.5 %collective-permute-start.6 = (f32[256,256]{1,0:T(8,128)S(1)}, f32[256,256]{1,0:T(8,128)S(1)}, u32[]{:S(2)}, u32[]{:S(2)}) collective-permute-start(f32[256,256]{1,0:T(8,128)S(1)} %collective-permute-done.5.items_ref), channel_id=1, source_target_pairs={{0,5},{1,6},{2,7},{3,4},{8,13},{9,14},{10,15},{11,12},{16,21},{17,... | collective-permute-start | bytes 786440 | tf_op jit(solution)/shard_map/ppermute | solution.py:23
  42.6 1.1 %multiply_subtract_fusion.1 = (f32[256,256]{1,0:T(8,128)}, f32[256,256]{1,0:T(8,128)}) fusion(f32[256,256]{1,0:T(8,128)S(1)} %get-tuple-element.27.users_ref, f32[256,256]{1,0:T(8,128)S(1)} %get-tuple-element.37, f32[256,256]{1,0:T(8,128)S(1)} %get-tuple-element.46, f32[256,256]{1,0:T(8,128)S(1)} %get-tuple-element.28, ...), kind=kOutput, calls=%fused_computation.14 | convolution fusion | flops 101318656 | bytes 1835008 | tf_op jit(solution)/shard_map/dot_general | solution.py:91
  43.7 5.4 %collective-permute-done.7 = f32[256,256]{1,0:T(8,128)S(1)} collective-permute-done((f32[256,256]{1,0:T(8,128)S(1)}, f32[256,256]{1,0:T(8,128)S(1)}, u32[]{:S(2)}, u32[]{:S(2)}) %collective-permute-start.7) | collective-permute-done | bytes 262176 | tf_op jit(solution)/shard_map/ppermute | solution.py:23
  49.1 0.0 collective-permute-done.9
  49.1 0.8 %collective-permute-done.8 = f32[256,256]{1,0:T(8,128)S(1)} collective-permute-done((f32[256,256]{1,0:T(8,128)S(1)}, f32[256,256]{1,0:T(8,128)S(1)}, u32[]{:S(2)}, u32[]{:S(2)}) %collective-permute-start.8) | collective-permute-done | bytes 262176 | tf_op jit(solution)/shard_map/ppermute | solution.py:23
  49.8 0.0 collective-permute-done.6
  49.9 0.9 %multiply_subtract_fusion = (f32[256,256]{1,0:T(8,128)}, f32[256,256]{1,0:T(8,128)}) fusion(f32[256,256]{1,0:T(8,128)S(1)} %collective-permute-done.8, f32[256,256]{1,0:T(8,128)S(1)} %collective-permute-done.6, f32[256,256]{1,0:T(8,128)S(1)} %collective-permute-done.7, pred[]{:T(512)S(6)} %eq.5, f32[256,256]{1,0:T(8,128)S(1)} %collective-permute-done.9), kind=kLoop, calls=%fused_computation.12 | loop fusion | flops 458752 | bytes 1572865 | tf_op jit(solution)/shard_map/sub | solution.py:96
  (2 shorter events, 0.1 us)
Async XLA Ops:
  0.6 1.6 %copy-start.1 = (f32[256,256]{1,0:T(8,128)S(1)}, f32[256,256]{1,0:T(8,128)}, u32[]{:S(2)}) copy-start(f32[256,256]{1,0:T(8,128)} %param.7) | copy-start | bytes 786436
  0.6 1.6 %copy-start = (f32[256,256]{1,0:T(8,128)S(1)}, f32[256,256]{1,0:T(8,128)}, u32[]{:S(2)}) copy-start(f32[256,256]{1,0:T(8,128)} %param.5) | copy-start | bytes 786436
  0.7 1.6 %copy-start.4 = (f32[256,256]{1,0:T(8,128)S(1)}, f32[256,256]{1,0:T(8,128)}, u32[]{:S(2)}) copy-start(f32[256,256]{1,0:T(8,128)} %param.8) | copy-start | bytes 786436
  2.2 3.4 %copy-start.3 = (f32[256,256]{1,0:T(8,128)S(1)}, f32[256,256]{1,0:T(8,128)}, u32[]{:S(2)}) copy-start(f32[256,256]{1,0:T(8,128)} %param.6) | copy-start | bytes 786436
  2.7 8.5 %copy-start.2 = (s32[256,1024]{1,0:T(8,128)S(1)}, s32[256,1024]{1,0:T(8,128)}, u32[]{:S(2)}) copy-start(s32[256,1024]{1,0:T(8,128)} %param.9) | copy-start | bytes 3145732
  2.7 13.2 %collective-permute-start = (f32[256,256]{1,0:T(8,128)S(1)}, f32[256,256]{1,0:T(8,128)S(1)}, u32[]{:S(2)}, u32[]{:S(2)}) collective-permute-start(f32[256,256]{1,0:T(8,128)S(1)} %get-tuple-element.19), channel_id=1, source_target_pairs={{0,4},{1,5},{2,6},{3,7},{4,8},{5,9},{6,10},{7,11},{8,12},{9,13},{1... | collective-permute-start | bytes 786440 | tf_op jit(solution)/shard_map/ppermute | solution.py:23
  6.0 17.1 %collective-permute-start.3 = (f32[256,256]{1,0:T(8,128)S(1)}, f32[256,256]{1,0:T(8,128)S(1)}, u32[]{:S(2)}, u32[]{:S(2)}) collective-permute-start(f32[256,256]{1,0:T(8,128)S(1)} %get-tuple-element.18), channel_id=1, source_target_pairs={{0,8},{1,9},{2,10},{3,11},{8,16},{9,17},{10,18},{11,19},{16,24},{1... | collective-permute-start | bytes 786440 | tf_op jit(solution)/shard_map/ppermute | solution.py:23
  9.5 13.6 %collective-permute-start.2 = (f32[256,256]{1,0:T(8,128)S(1)}, f32[256,256]{1,0:T(8,128)S(1)}, u32[]{:S(2)}, u32[]{:S(2)}) collective-permute-start(f32[256,256]{1,0:T(8,128)S(1)} %broadcast_select_fusion.1), channel_id=1, source_target_pairs={{0,8},{1,9},{2,10},{3,11},{4,12},{5,13},{6,14},{7,15},{8,16},{9,17... | collective-permute-start | bytes 786440 | tf_op jit(solution)/shard_map/ppermute | solution.py:23
  16.6 10.1 %collective-permute-start.4 = (f32[256,256]{1,0:T(8,128)S(1)}, f32[256,256]{1,0:T(8,128)S(1)}, u32[]{:S(2)}, u32[]{:S(2)}) collective-permute-start(f32[256,256]{1,0:T(8,128)S(1)} %get-tuple-element.21), channel_id=1, source_target_pairs={{0,4},{1,5},{2,6},{3,7},{4,8},{5,9},{6,10},{7,11},{8,12},{9,13},{1... | collective-permute-start | bytes 786440 | tf_op jit(solution)/shard_map/ppermute | solution.py:23
  16.7 10.1 %collective-permute-start.1 = (f32[256,256]{1,0:T(8,128)S(1)}, f32[256,256]{1,0:T(8,128)S(1)}, u32[]{:S(2)}, u32[]{:S(2)}) collective-permute-start(f32[256,256]{1,0:T(8,128)S(1)} %collective-permute-done.items_ref), channel_id=1, source_target_pairs={{0,4},{1,5},{2,6},{3,7},{8,12},{9,13},{10,14},{11,15},{16,20},{17,... | collective-permute-start | bytes 786440 | tf_op jit(solution)/shard_map/ppermute | solution.py:23
  27.7 9.6 %collective-permute-start.5 = (f32[256,256]{1,0:T(8,128)S(1)}, f32[256,256]{1,0:T(8,128)S(1)}, u32[]{:S(2)}, u32[]{:S(2)}) collective-permute-start(f32[256,256]{1,0:T(8,128)S(1)} %get-tuple-element.30), channel_id=1, source_target_pairs={{0,4},{1,5},{2,6},{3,7},{4,8},{5,9},{6,10},{7,11},{8,12},{9,13},{1... | collective-permute-start | bytes 786440 | tf_op jit(solution)/shard_map/ppermute | solution.py:23
  30.5 18.5 %collective-permute-start.9 = (f32[256,256]{1,0:T(8,128)S(1)}, f32[256,256]{1,0:T(8,128)S(1)}, u32[]{:S(2)}, u32[]{:S(2)}) collective-permute-start(f32[256,256]{1,0:T(8,128)S(1)} %get-tuple-element.29), channel_id=1, source_target_pairs={{0,9},{1,10},{2,11},{3,8},{8,17},{9,18},{10,19},{11,16},{16,25},{1... | collective-permute-start | bytes 786440 | tf_op jit(solution)/shard_map/ppermute | solution.py:23
  32.5 16.6 %collective-permute-start.7 = (f32[256,256]{1,0:T(8,128)S(1)}, f32[256,256]{1,0:T(8,128)S(1)}, u32[]{:S(2)}, u32[]{:S(2)}) collective-permute-start(f32[256,256]{1,0:T(8,128)S(1)} %broadcast_select_fusion), channel_id=1, source_target_pairs={{0,9},{1,10},{2,11},{3,8},{4,13},{5,14},{6,15},{7,12},{8,17},{9,18... | collective-permute-start | bytes 786440 | tf_op jit(solution)/shard_map/ppermute | solution.py:23
  38.0 11.9 %collective-permute-start.8 = (f32[256,256]{1,0:T(8,128)S(1)}, f32[256,256]{1,0:T(8,128)S(1)}, u32[]{:S(2)}, u32[]{:S(2)}) collective-permute-start(f32[256,256]{1,0:T(8,128)S(1)} %get-tuple-element.31), channel_id=1, source_target_pairs={{0,5},{1,6},{2,7},{3,4},{4,9},{5,10},{6,11},{7,8},{8,13},{9,14},{1... | collective-permute-start | bytes 786440 | tf_op jit(solution)/shard_map/ppermute | solution.py:23
  38.0 11.8 %collective-permute-start.6 = (f32[256,256]{1,0:T(8,128)S(1)}, f32[256,256]{1,0:T(8,128)S(1)}, u32[]{:S(2)}, u32[]{:S(2)}) collective-permute-start(f32[256,256]{1,0:T(8,128)S(1)} %collective-permute-done.5.items_ref), channel_id=1, source_target_pairs={{0,5},{1,6},{2,7},{3,4},{8,13},{9,14},{10,15},{11,12},{16,21},{17,... | collective-permute-start | bytes 786440 | tf_op jit(solution)/shard_map/ppermute | solution.py:23

commit v5 on v1

--- a/solution.py
+++ b/solution.py
@@ -19,6 +19,10 @@
             if target is not None:
                 pairs.append((b * n_group + g, target[0] % n_blk * n_group + target[1] % n_group))
     return lax.ppermute(value, ("blk", "group"), pairs)
+
+
+def passes_on(b, g, n_blk):
+    return (b % 2 == 1) & ((g % 2 == 1) | (b % n_blk >= n_blk - 2))
 
 
 def weighted_gap(users, items, count_tile):
@@ -45,7 +49,8 @@
 def body(users, user_acc, items, item_acc, counts):
     rows = items.shape[0]
     tiles = [counts[:, s * rows : (s + 1) * rows] for s in range(4)]
-    odd = lax.axis_index("blk") % 2 == 1
+    n_blk, blk, group = lax.axis_size("blk"), lax.axis_index("blk"), lax.axis_index("group")
+    passing = passes_on(blk, group, n_blk)
 
     def two_strata(users, user_acc, items, item_acc, first, up):
         gap = weighted_gap(users, items, tiles[first])
@@ -56,16 +61,17 @@
 
         visitor = sent(items, lambda b, g: (b + 1, g))
         items, item_acc, users = lax.optimization_barrier((items, item_acc, users))
-        ahead = sent(jnp.where(odd, item_acc, items), lambda b, g: (b + 2, g + up))
-        even_acc = sent(item_acc, lambda b, g: (b + 2, g + up) if b % 2 == 0 else None)
-        passed = sent(visitor, lambda b, g: (b + 1, g + up) if b % 2 == 0 else None)
+        ahead = sent(jnp.where(passing, item_acc, items), lambda b, g: (b + 2, g + up))
+        late = sent(item_acc, lambda b, g: None if passes_on(b, g, n_blk) else (b + 2, g + up))
+        passed = sent(visitor, lambda b, g: (b + 1, g + up) if passes_on(b - 1, g, n_blk) else None)
         gap = weighted_gap(users, visitor, tiles[first + 1])
         grad_v = item_gradient(gap, users, visitor)
         grad_u = user_gradient(gap, users, visitor)
         grad_v = sent(grad_v, lambda b, g: (b + 1, g + up))
         users, user_acc = adagrad(users, user_acc, grad_u)
-        items = jnp.where(odd, passed, ahead)
-        item_acc = jnp.where(odd, ahead, even_acc)
+        came_by_visit = passes_on((blk - 2) % n_blk, group - up, n_blk)
+        items = jnp.where(came_by_visit, passed, ahead)
+        item_acc = jnp.where(came_by_visit, ahead, late)
         items, item_acc = adagrad(items, item_acc, grad_v)
         return users, user_acc, items, item_acc
 

time: 50.9 us -> 50.9 us (level)
  transfers between devices with their start and end apart: 10 -> 10, of which waited for: 7 -> 8; matrix products, arithmetic and copies ran while one was open for 7% -> 7% of each run, Pallas kernels for 0% -> 0%
where the time goes in v5:
time: 50.9 us; the launch traced here: 50.7 us
  starting transfers between devices  22.2 us (44%)
  waiting for transfers between devices  20.3 us (40%)
  matrix products  6.28 us (12%)
  other arithmetic  1.01 us (2%)
  between operations  0.88 us (2%)
    ppermute x10, starting transfers between devices, sent(): return lax.ppermute(value, ('blk', 'group'), pairs)  22.2 us
    ppermute x10, waiting for transfers between devices, sent(): return lax.ppermute(value, ('blk', 'group'), pairs)  20.3 us
    dot_general x4, matrix products, weighted_gap(): lax.dot_general(users, items, (((1,), (1,)), ((), ())), precision=PREC)  2.56 us
    dot_general x4, matrix products, user_gradient(): jnp.dot(gap, items, precision=PREC)  2.08 us
    dot_general x4, matrix products, item_gradient(): lax.dot_general(gap, users, (((0,), (0,)), ((), ())), precision=PREC)  1.63 us
  transfers between devices with their start and end apart: 10, of which 8 were waited for; matrix products, arithmetic and copies ran while one was open for 7% of the time, Pallas kernels for 0%

profile of v5, /device:TPU:0, one launch (start us, length us, event | category | flops | bytes accessed | tf_op | source)
XLA Modules:
  0.0 50.7 jit_solution(5936176652616883079)
XLA Ops:
  0.6 0.0 copy-start.1
  0.6 0.0 copy-start
  0.7 0.0 copy-start.4
  0.7 1.5 %fusion.8 = f32[256,256]{1,0:T(8,128)S(1)} fusion(f32[256,256]{1,0:T(8,128)} %param.5, f32[256,256]{1,0:T(8,128)} %param.7, s32[256,1024]{1,0:T(8,128)} %param.9), kind=kOutput, calls=%fused_computation.20 | convolution fusion | flops 101122048 | bytes 1048576 | tf_op jit(solution)/shard_map/dot_general | solution.py:29
  2.2 0.0 copy-done.1
  2.2 0.0 copy-done
  2.2 0.0 copy-done.4
  2.2 0.0 copy-start.2
  2.2 0.4 multiply_subtract_fusion.7
  2.7 0.0 copy-start.3
  2.7 3.0 %collective-permute-start = (f32[256,256]{1,0:T(8,128)S(1)}, f32[256,256]{1,0:T(8,128)S(1)}, u32[]{:S(2)}, u32[]{:S(2)}) collective-permute-start(f32[256,256]{1,0:T(8,128)S(1)} %get-tuple-element.11), channel_id=1, source_target_pairs={{0,4},{1,5},{2,6},{3,7},{4,8},{5,9},{6,10},{7,11},{8,12},{9,13},{1... | collective-permute-start | bytes 786440 | tf_op jit(solution)/shard_map/ppermute | solution.py:21
  5.7 0.0 copy-done.2
  5.7 0.3 multiply_subtract_fusion.6
  6.0 3.5 %collective-permute-start.4 = (f32[256,256]{1,0:T(8,128)S(1)}, f32[256,256]{1,0:T(8,128)S(1)}, u32[]{:S(2)}, u32[]{:S(2)}) collective-permute-start(f32[256,256]{1,0:T(8,128)S(1)} %get-tuple-element.10), channel_id=1, source_target_pairs={{0,8},{1,9},{2,10},{3,11},{4,12},{6,14},{8,16},{9,17},{10,18},{11,... | collective-permute-start | bytes 786440 | tf_op jit(solution)/shard_map/ppermute | solution.py:21
  9.6 1.6 %collective-permute-start.2 = (f32[256,256]{1,0:T(8,128)S(1)}, f32[256,256]{1,0:T(8,128)S(1)}, u32[]{:S(2)}, u32[]{:S(2)}) collective-permute-start(f32[256,256]{1,0:T(8,128)S(1)} %broadcast_select_fusion.1), channel_id=1, source_target_pairs={{0,8},{1,9},{2,10},{3,11},{4,12},{5,13},{6,14},{7,15},{8,16},{9,17... | collective-permute-start | bytes 786440 | tf_op jit(solution)/shard_map/ppermute | solution.py:21
  11.2 4.6 %collective-permute-done = f32[256,256]{1,0:T(8,128)S(1)} collective-permute-done((f32[256,256]{1,0:T(8,128)S(1)}, f32[256,256]{1,0:T(8,128)S(1)}, u32[]{:S(2)}, u32[]{:S(2)}) %collective-permute-start) | collective-permute-done | bytes 262176 | tf_op jit(solution)/shard_map/ppermute | solution.py:21
  15.8 0.0 copy-done.3
  15.8 0.3 fusion.5
  16.2 0.4 multiply_add_fusion.8
  16.6 0.1 collective-permute-start.3
  16.7 3.4 %collective-permute-start.1 = (f32[256,256]{1,0:T(8,128)S(1)}, f32[256,256]{1,0:T(8,128)S(1)}, u32[]{:S(2)}, u32[]{:S(2)}) collective-permute-start(f32[256,256]{1,0:T(8,128)S(1)} %collective-permute-done), channel_id=1, source_target_pairs={{0,4},{1,5},{2,6},{3,7},{9,13},{11,15},{17,21},{19,23},{25,29},{27... | collective-permute-start | bytes 786440 | tf_op jit(solution)/shard_map/ppermute | solution.py:21
  20.0 0.3 multiply_subtract_fusion.4
  20.4 2.8 %collective-permute-done.2 = f32[256,256]{1,0:T(8,128)S(1)} collective-permute-done((f32[256,256]{1,0:T(8,128)S(1)}, f32[256,256]{1,0:T(8,128)S(1)}, u32[]{:S(2)}, u32[]{:S(2)}) %collective-permute-start.2) | collective-permute-done | bytes 262176 | tf_op jit(solution)/shard_map/ppermute | solution.py:21
  23.1 0.0 collective-permute-done.4
  23.1 3.1 %collective-permute-done.3 = f32[256,256]{1,0:T(8,128)S(1)} collective-permute-done((f32[256,256]{1,0:T(8,128)S(1)}, f32[256,256]{1,0:T(8,128)S(1)}, u32[]{:S(2)}, u32[]{:S(2)}) %collective-permute-start.3) | collective-permute-done | bytes 262176 | tf_op jit(solution)/shard_map/ppermute | solution.py:21
  26.2 0.5 collective-permute-done.1
  26.7 0.1 multiply_subtract_fusion.5
  26.8 0.3 fusion.3
  27.2 0.4 multiply_subtract_fusion.3
  27.6 2.5 %collective-permute-start.5 = (f32[256,256]{1,0:T(8,128)S(1)}, f32[256,256]{1,0:T(8,128)S(1)}, u32[]{:S(2)}, u32[]{:S(2)}) collective-permute-start(f32[256,256]{1,0:T(8,128)S(1)} %get-tuple-element.15), channel_id=1, source_target_pairs={{0,4},{1,5},{2,6},{3,7},{4,8},{5,9},{6,10},{7,11},{8,12},{9,13},{1... | collective-permute-start | bytes 786440 | tf_op jit(solution)/shard_map/ppermute | solution.py:21
  30.1 0.3 multiply_subtract_fusion.2
  30.5 1.9 %collective-permute-start.9 = (f32[256,256]{1,0:T(8,128)S(1)}, f32[256,256]{1,0:T(8,128)S(1)}, u32[]{:S(2)}, u32[]{:S(2)}) collective-permute-start(f32[256,256]{1,0:T(8,128)S(1)} %get-tuple-element.14), channel_id=1, source_target_pairs={{0,9},{1,10},{2,11},{3,8},{4,13},{6,15},{8,17},{9,18},{10,19},{11,... | collective-permute-start | bytes 786440 | tf_op jit(solution)/shard_map/ppermute | solution.py:21
  32.4 1.8 %collective-permute-start.7 = (f32[256,256]{1,0:T(8,128)S(1)}, f32[256,256]{1,0:T(8,128)S(1)}, u32[]{:S(2)}, u32[]{:S(2)}) collective-permute-start(f32[256,256]{1,0:T(8,128)S(1)} %broadcast_select_fusion), channel_id=1, source_target_pairs={{0,9},{1,10},{2,11},{3,8},{4,13},{5,14},{6,15},{7,12},{8,17},{9,18... | collective-permute-start | bytes 786440 | tf_op jit(solution)/shard_map/ppermute | solution.py:21
  34.3 2.5 %collective-permute-done.5 = f32[256,256]{1,0:T(8,128)S(1)} collective-permute-done((f32[256,256]{1,0:T(8,128)S(1)}, f32[256,256]{1,0:T(8,128)S(1)}, u32[]{:S(2)}, u32[]{:S(2)}) %collective-permute-start.5) | collective-permute-done | bytes 262176 | tf_op jit(solution)/shard_map/ppermute | solution.py:21
  36.7 0.3 fusion.1
  37.1 0.4 multiply_add_fusion.1
  37.5 0.1 collective-permute-start.8
  37.6 4.3 %collective-permute-start.6 = (f32[256,256]{1,0:T(8,128)S(1)}, f32[256,256]{1,0:T(8,128)S(1)}, u32[]{:S(2)}, u32[]{:S(2)}) collective-permute-start(f32[256,256]{1,0:T(8,128)S(1)} %collective-permute-done.5), channel_id=1, source_target_pairs={{0,5},{1,6},{2,7},{3,4},{9,14},{11,12},{17,22},{19,20},{25,30},{27... | collective-permute-start | bytes 786440 | tf_op jit(solution)/shard_map/ppermute | solution.py:21
  41.9 1.1 %multiply_subtract_fusion.1 = (f32[256,256]{1,0:T(8,128)}, f32[256,256]{1,0:T(8,128)}) fusion(f32[256,256]{1,0:T(8,128)S(1)} %get-tuple-element.13, f32[256,256]{1,0:T(8,128)S(1)} %get-tuple-element.23, f32[256,256]{1,0:T(8,128)S(1)} %get-tuple-element.29, f32[256,256]{1,0:T(8,128)S(1)} %fusion.1, f32[256,256]{1,0:T(8,128)S(1)} %collective-permute-done.5), kind=kOutput, calls=%fused_computation.24 | convolution fusion | flops 101318656 | bytes 1835008 | tf_op jit(solution)/shard_map/dot_general | solution.py:36
  43.0 5.7 %collective-permute-done.7 = f32[256,256]{1,0:T(8,128)S(1)} collective-permute-done((f32[256,256]{1,0:T(8,128)S(1)}, f32[256,256]{1,0:T(8,128)S(1)}, u32[]{:S(2)}, u32[]{:S(2)}) %collective-permute-start.7) | collective-permute-done | bytes 262176 | tf_op jit(solution)/shard_map/ppermute | solution.py:21
  48.7 0.0 collective-permute-done.9
  48.7 0.9 %collective-permute-done.8 = f32[256,256]{1,0:T(8,128)S(1)} collective-permute-done((f32[256,256]{1,0:T(8,128)S(1)}, f32[256,256]{1,0:T(8,128)S(1)}, u32[]{:S(2)}, u32[]{:S(2)}) %collective-permute-start.8) | collective-permute-done | bytes 262176 | tf_op jit(solution)/shard_map/ppermute | solution.py:21
  49.6 0.3 collective-permute-done.6
  49.8 0.9 %multiply_subtract_fusion = (f32[256,256]{1,0:T(8,128)}, f32[256,256]{1,0:T(8,128)}) fusion(f32[256,256]{1,0:T(8,128)S(1)} %collective-permute-done.8, f32[256,256]{1,0:T(8,128)S(1)} %collective-permute-done.6, f32[256,256]{1,0:T(8,128)S(1)} %collective-permute-done.7, pred[]{:T(512)S(6)} %and.53, f32[256,256]{1,0:T(8,128)S(1)} %collective-permute-done.9), kind=kLoop, calls=%fused_computation.21 | loop fusion | flops 458752 | bytes 1572865 | tf_op jit(solution)/shard_map/sub | solution.py:46
  (2 shorter events, 0.1 us)
Async XLA Ops:
  0.6 1.6 %copy-start.1 = (f32[256,256]{1,0:T(8,128)S(1)}, f32[256,256]{1,0:T(8,128)}, u32[]{:S(2)}) copy-start(f32[256,256]{1,0:T(8,128)} %param.7) | copy-start | bytes 786436
  0.6 1.6 %copy-start = (f32[256,256]{1,0:T(8,128)S(1)}, f32[256,256]{1,0:T(8,128)}, u32[]{:S(2)}) copy-start(f32[256,256]{1,0:T(8,128)} %param.5) | copy-start | bytes 786436
  0.7 1.6 %copy-start.4 = (f32[256,256]{1,0:T(8,128)S(1)}, f32[256,256]{1,0:T(8,128)}, u32[]{:S(2)}) copy-start(f32[256,256]{1,0:T(8,128)} %param.8) | copy-start | bytes 786436
  2.2 3.4 %copy-start.2 = (f32[256,256]{1,0:T(8,128)S(1)}, f32[256,256]{1,0:T(8,128)}, u32[]{:S(2)}) copy-start(f32[256,256]{1,0:T(8,128)} %param.6) | copy-start | bytes 786436
  2.7 13.2 %copy-start.3 = (s32[256,1024]{1,0:T(8,128)S(1)}, s32[256,1024]{1,0:T(8,128)}, u32[]{:S(2)}) copy-start(s32[256,1024]{1,0:T(8,128)} %param.9) | copy-start | bytes 3145732
  2.7 13.2 %collective-permute-start = (f32[256,256]{1,0:T(8,128)S(1)}, f32[256,256]{1,0:T(8,128)S(1)}, u32[]{:S(2)}, u32[]{:S(2)}) collective-permute-start(f32[256,256]{1,0:T(8,128)S(1)} %get-tuple-element.11), channel_id=1, source_target_pairs={{0,4},{1,5},{2,6},{3,7},{4,8},{5,9},{6,10},{7,11},{8,12},{9,13},{1... | collective-permute-start | bytes 786440 | tf_op jit(solution)/shard_map/ppermute | solution.py:21
  6.0 17.1 %collective-permute-start.4 = (f32[256,256]{1,0:T(8,128)S(1)}, f32[256,256]{1,0:T(8,128)S(1)}, u32[]{:S(2)}, u32[]{:S(2)}) collective-permute-start(f32[256,256]{1,0:T(8,128)S(1)} %get-tuple-element.10), channel_id=1, source_target_pairs={{0,8},{1,9},{2,10},{3,11},{4,12},{6,14},{8,16},{9,17},{10,18},{11,... | collective-permute-start | bytes 786440 | tf_op jit(solution)/shard_map/ppermute | solution.py:21
  9.6 13.6 %collective-permute-start.2 = (f32[256,256]{1,0:T(8,128)S(1)}, f32[256,256]{1,0:T(8,128)S(1)}, u32[]{:S(2)}, u32[]{:S(2)}) collective-permute-start(f32[256,256]{1,0:T(8,128)S(1)} %broadcast_select_fusion.1), channel_id=1, source_target_pairs={{0,8},{1,9},{2,10},{3,11},{4,12},{5,13},{6,14},{7,15},{8,16},{9,17... | collective-permute-start | bytes 786440 | tf_op jit(solution)/shard_map/ppermute | solution.py:21
  16.6 9.6 %collective-permute-start.3 = (f32[256,256]{1,0:T(8,128)S(1)}, f32[256,256]{1,0:T(8,128)S(1)}, u32[]{:S(2)}, u32[]{:S(2)}) collective-permute-start(f32[256,256]{1,0:T(8,128)S(1)} %multiply_add_fusion.8), channel_id=1, source_target_pairs={{0,4},{1,5},{2,6},{3,7},{4,8},{5,9},{6,10},{7,11},{8,12},{9,13},{1... | collective-permute-start | bytes 786440 | tf_op jit(solution)/shard_map/ppermute | solution.py:21
  16.7 10.1 %collective-permute-start.1 = (f32[256,256]{1,0:T(8,128)S(1)}, f32[256,256]{1,0:T(8,128)S(1)}, u32[]{:S(2)}, u32[]{:S(2)}) collective-permute-start(f32[256,256]{1,0:T(8,128)S(1)} %collective-permute-done), channel_id=1, source_target_pairs={{0,4},{1,5},{2,6},{3,7},{9,13},{11,15},{17,21},{19,23},{25,29},{27... | collective-permute-start | bytes 786440 | tf_op jit(solution)/shard_map/ppermute | solution.py:21
  27.6 9.1 %collective-permute-start.5 = (f32[256,256]{1,0:T(8,128)S(1)}, f32[256,256]{1,0:T(8,128)S(1)}, u32[]{:S(2)}, u32[]{:S(2)}) collective-permute-start(f32[256,256]{1,0:T(8,128)S(1)} %get-tuple-element.15), channel_id=1, source_target_pairs={{0,4},{1,5},{2,6},{3,7},{4,8},{5,9},{6,10},{7,11},{8,12},{9,13},{1... | collective-permute-start | bytes 786440 | tf_op jit(solution)/shard_map/ppermute | solution.py:21
  30.5 18.2 %collective-permute-start.9 = (f32[256,256]{1,0:T(8,128)S(1)}, f32[256,256]{1,0:T(8,128)S(1)}, u32[]{:S(2)}, u32[]{:S(2)}) collective-permute-start(f32[256,256]{1,0:T(8,128)S(1)} %get-tuple-element.14), channel_id=1, source_target_pairs={{0,9},{1,10},{2,11},{3,8},{4,13},{6,15},{8,17},{9,18},{10,19},{11,... | collective-permute-start | bytes 786440 | tf_op jit(solution)/shard_map/ppermute | solution.py:21
  32.4 16.2 %collective-permute-start.7 = (f32[256,256]{1,0:T(8,128)S(1)}, f32[256,256]{1,0:T(8,128)S(1)}, u32[]{:S(2)}, u32[]{:S(2)}) collective-permute-start(f32[256,256]{1,0:T(8,128)S(1)} %broadcast_select_fusion), channel_id=1, source_target_pairs={{0,9},{1,10},{2,11},{3,8},{4,13},{5,14},{6,15},{7,12},{8,17},{9,18... | collective-permute-start | bytes 786440 | tf_op jit(solution)/shard_map/ppermute | solution.py:21
  37.5 12.1 %collective-permute-start.8 = (f32[256,256]{1,0:T(8,128)S(1)}, f32[256,256]{1,0:T(8,128)S(1)}, u32[]{:S(2)}, u32[]{:S(2)}) collective-permute-start(f32[256,256]{1,0:T(8,128)S(1)} %multiply_add_fusion.1), channel_id=1, source_target_pairs={{0,5},{1,6},{2,7},{3,4},{4,9},{5,10},{6,11},{7,8},{8,13},{9,14},{1... | collective-permute-start | bytes 786440 | tf_op jit(solution)/shard_map/ppermute | solution.py:21
  37.6 12.3 %collective-permute-start.6 = (f32[256,256]{1,0:T(8,128)S(1)}, f32[256,256]{1,0:T(8,128)S(1)}, u32[]{:S(2)}, u32[]{:S(2)}) collective-permute-start(f32[256,256]{1,0:T(8,128)S(1)} %collective-permute-done.5), channel_id=1, source_target_pairs={{0,5},{1,6},{2,7},{3,4},{9,14},{11,12},{17,22},{19,20},{25,30},{27... | collective-permute-start | bytes 786440 | tf_op jit(solution)/shard_map/ppermute | solution.py:21

commit v6 on v4

--- a/solution.py
+++ b/solution.py
@@ -29,10 +29,10 @@
 
 
 def product(left, right, dims):
-    def dot(a, b):
-        return lax.dot_general(a, b, (dims, ((), ())), preferred_element_type=jnp.float32)
-
-    return dot(left[0], right[1]) + dot(left[1], right[0]) + dot(left[0], right[0])
+    (left_dim,), (right_dim,) = dims
+    lefts = jnp.concatenate([left[0], left[0], left[1]], axis=left_dim)
+    rights = jnp.concatenate([right[0], right[1], right[0]], axis=right_dim)
+    return lax.dot_general(lefts, rights, (dims, ((), ())), preferred_element_type=jnp.float32)
 
 
 def weighted_gap(users, items, count_tile):

time: 50.9 us -> 50.9 us (level)
  no operation moved by 1% of the time
where the time goes in v6:
time: 50.9 us; the launch traced here: 50.7 us
  starting transfers between devices  22.5 us (44%)
  waiting for transfers between devices  19.9 us (39%)
  matrix products  4.01 us (8%)
  Pallas kernels  2.4 us (5%)
  other arithmetic  0.93 us (2%)
  between operations  0.84 us (2%)
    ppermute x10, starting transfers between devices, sent(): return lax.ppermute(value, ('blk', 'group'), pairs)  22.5 us
    ppermute x10, waiting for transfers between devices, sent(): return lax.ppermute(value, ('blk', 'group'), pairs)  19.9 us
    pallas_call x3, Pallas kernels, on_vmem(): pl.pallas_call(kernel, out_shape=[jax.ShapeDtypeStruct(shape, jnp.float32...  2.4 us
    dot_general x4, matrix products, user_gradient(): jnp.dot(gap, items, precision=PREC)  2.08 us
    dot_general x1, matrix products, weighted_gap(): lax.dot_general(users, items, (((1,), (1,)), ((), ())), precision=PREC)  1.52 us
  transfers between devices with their start and end apart: 10, of which 6 were waited for; matrix products, arithmetic and copies ran while one was open for 4% of the time, Pallas kernels for 3%

profile of v6, /device:TPU:0, one launch (start us, length us, event | category | flops | bytes accessed | tf_op | source)
XLA Modules:
  0.0 50.7 jit_solution(15014597224877633608)
XLA Ops:
  0.6 0.0 copy-start.1
  0.6 0.0 copy-start
  0.7 0.0 copy-start.4
  0.7 1.5 %fusion.5 = f32[256,256]{1,0:T(8,128)S(1)} fusion(f32[256,256]{1,0:T(8,128)} %param.5, f32[256,256]{1,0:T(8,128)} %param.7, s32[256,1024]{1,0:T(8,128)} %param.9), kind=kOutput, calls=%fused_computation.11 | convolution fusion | flops 101122048 | bytes 1048576 | tf_op jit(solution)/shard_map/dot_general | solution.py:39
  2.2 0.0 copy-done.1
  2.2 0.0 copy-done
  2.2 0.0 copy-done.4
  2.2 0.0 copy-start.3
  2.2 0.4 multiply_subtract_fusion.5
  2.7 0.0 copy-start.2
  2.7 3.0 %collective-permute-start = (f32[256,256]{1,0:T(8,128)S(1)}, f32[256,256]{1,0:T(8,128)S(1)}, u32[]{:S(2)}, u32[]{:S(2)}) collective-permute-start(f32[256,256]{1,0:T(8,128)S(1)} %get-tuple-element.19), channel_id=1, source_target_pairs={{0,4},{1,5},{2,6},{3,7},{4,8},{5,9},{6,10},{7,11},{8,12},{9,13},{1... | collective-permute-start | bytes 786440 | tf_op jit(solution)/shard_map/ppermute | solution.py:23
  5.7 0.0 copy-done.3
  5.7 0.3 multiply_subtract_fusion.4
  6.0 3.5 %collective-permute-start.3 = (f32[256,256]{1,0:T(8,128)S(1)}, f32[256,256]{1,0:T(8,128)S(1)}, u32[]{:S(2)}, u32[]{:S(2)}) collective-permute-start(f32[256,256]{1,0:T(8,128)S(1)} %get-tuple-element.18), channel_id=1, source_target_pairs={{0,8},{1,9},{2,10},{3,11},{8,16},{9,17},{10,18},{11,19},{16,24},{1... | collective-permute-start | bytes 786440 | tf_op jit(solution)/shard_map/ppermute | solution.py:23
  9.5 1.6 %collective-permute-start.2 = (f32[256,256]{1,0:T(8,128)S(1)}, f32[256,256]{1,0:T(8,128)S(1)}, u32[]{:S(2)}, u32[]{:S(2)}) collective-permute-start(f32[256,256]{1,0:T(8,128)S(1)} %broadcast_select_fusion.1), channel_id=1, source_target_pairs={{0,8},{1,9},{2,10},{3,11},{4,12},{5,13},{6,14},{7,15},{8,16},{9,17... | collective-permute-start | bytes 786440 | tf_op jit(solution)/shard_map/ppermute | solution.py:23
  11.2 0.0 copy-done.2
  11.2 0.1 fusion.6
  11.2 4.6 %collective-permute-done.items_ref = f32[256,256]{1,0:T(8,128)S(1)} collective-permute-done((f32[256,256]{1,0:T(8,128)S(1)}, f32[256,256]{1,0:T(8,128)S(1)}, u32[]{:S(2)}, u32[]{:S(2)}) %collective-permute-start) | collective-permute-done | bytes 262176 | tf_op jit(solution)/shard_map/ppermute | solution.py:23
  15.8 0.7 %visit.2 = (f32[256,256]{1,0:T(8,128)S(1)}, f32[256,256]{1,0:T(8,128)S(1)}) custom-call(f32[256,256]{1,0:T(8,128)S(1)} %get-tuple-element.20.users_ref, f32[256,256]{1,0:T(8,128)S(1)} %collective-permute-done.items_ref, s32[256,256]{1,0:T(8,128)S(1)} %get-tuple-element.41.tile_ref), custom_call_target="tpu_custom_call" | custom-call | flops 201326592 | bytes 1310720 | tf_op jit(solution)/shard_map/visit/pallas_call | solution.py:79
  16.6 0.1 collective-permute-start.4
  16.6 3.4 %collective-permute-start.1 = (f32[256,256]{1,0:T(8,128)S(1)}, f32[256,256]{1,0:T(8,128)S(1)}, u32[]{:S(2)}, u32[]{:S(2)}) collective-permute-start(f32[256,256]{1,0:T(8,128)S(1)} %collective-permute-done.items_ref), channel_id=1, source_target_pairs={{0,4},{1,5},{2,6},{3,7},{8,12},{9,13},{10,14},{11,15},{16,20},{17,... | collective-permute-start | bytes 786440 | tf_op jit(solution)/shard_map/ppermute | solution.py:23
  20.0 0.3 multiply_subtract_fusion.3
  20.3 2.8 %collective-permute-done.2.ahead_ref = f32[256,256]{1,0:T(8,128)S(1)} collective-permute-done((f32[256,256]{1,0:T(8,128)S(1)}, f32[256,256]{1,0:T(8,128)S(1)}, u32[]{:S(2)}, u32[]{:S(2)}) %collective-permute-start.2) | collective-permute-done | bytes 262176 | tf_op jit(solution)/shard_map/ppermute | solution.py:23
  23.1 0.0 collective-permute-done.3.even_acc_ref
  23.1 3.6 %collective-permute-done.1.passed_ref = f32[256,256]{1,0:T(8,128)S(1)} collective-permute-done((f32[256,256]{1,0:T(8,128)S(1)}, f32[256,256]{1,0:T(8,128)S(1)}, u32[]{:S(2)}, u32[]{:S(2)}) %collective-permute-start.1) | collective-permute-done | bytes 262176 | tf_op jit(solution)/shard_map/ppermute | solution.py:23
  26.7 0.0 collective-permute-done.4.old_grad_ref
  26.7 0.9 %local.1 = (f32[256,256]{1,0:T(8,128)S(1)}, f32[256,256]{1,0:T(8,128)S(1)}, f32[256,256]{1,0:T(8,128)S(1)}, f32[256,256]{1,0:T(8,128)S(1)}) custom-call(s32[1]{0:T(128)} %bitcast.odd_ref, f32[256,256]{1,0:T(8,128)S(1)} %collective-permute-done.1.passed_ref, f32[256,256]{1,0:T(8,128)S(1)} %collective-permute-done.2.ahead_ref, ...), custom_call_target="tpu_custom_call" | custom-call | flops 201326592 | bytes 1310720 | tf_op jit(solution)/shard_map/local/pallas_call | solution.py:79
  27.6 2.5 %collective-permute-start.5 = (f32[256,256]{1,0:T(8,128)S(1)}, f32[256,256]{1,0:T(8,128)S(1)}, u32[]{:S(2)}, u32[]{:S(2)}) collective-permute-start(f32[256,256]{1,0:T(8,128)S(1)} %get-tuple-element.30), channel_id=1, source_target_pairs={{0,4},{1,5},{2,6},{3,7},{4,8},{5,9},{6,10},{7,11},{8,12},{9,13},{1... | collective-permute-start | bytes 786440 | tf_op jit(solution)/shard_map/ppermute | solution.py:23
  30.2 0.3 multiply_subtract_fusion.2
  30.5 1.9 %collective-permute-start.9 = (f32[256,256]{1,0:T(8,128)S(1)}, f32[256,256]{1,0:T(8,128)S(1)}, u32[]{:S(2)}, u32[]{:S(2)}) collective-permute-start(f32[256,256]{1,0:T(8,128)S(1)} %get-tuple-element.29), channel_id=1, source_target_pairs={{0,9},{1,10},{2,11},{3,8},{8,17},{9,18},{10,19},{11,16},{16,25},{1... | collective-permute-start | bytes 786440 | tf_op jit(solution)/shard_map/ppermute | solution.py:23
  32.5 2.0 %collective-permute-start.7 = (f32[256,256]{1,0:T(8,128)S(1)}, f32[256,256]{1,0:T(8,128)S(1)}, u32[]{:S(2)}, u32[]{:S(2)}) collective-permute-start(f32[256,256]{1,0:T(8,128)S(1)} %broadcast_select_fusion), channel_id=1, source_target_pairs={{0,9},{1,10},{2,11},{3,8},{4,13},{5,14},{6,15},{7,12},{8,17},{9,18... | collective-permute-start | bytes 786440 | tf_op jit(solution)/shard_map/ppermute | solution.py:23
  34.4 2.8 %collective-permute-done.5.items_ref = f32[256,256]{1,0:T(8,128)S(1)} collective-permute-done((f32[256,256]{1,0:T(8,128)S(1)}, f32[256,256]{1,0:T(8,128)S(1)}, u32[]{:S(2)}, u32[]{:S(2)}) %collective-permute-start.5) | collective-permute-done | bytes 262176 | tf_op jit(solution)/shard_map/ppermute | solution.py:23
  37.2 0.7 %visit.3 = (f32[256,256]{1,0:T(8,128)S(1)}, f32[256,256]{1,0:T(8,128)S(1)}) custom-call(f32[256,256]{1,0:T(8,128)S(1)} %get-tuple-element.27.users_ref, f32[256,256]{1,0:T(8,128)S(1)} %collective-permute-done.5.items_ref, s32[256,256]{1,0:T(8,128)S(1)} %get-tuple-element.40.tile_ref), custom_call_target="tpu_custom_call" | custom-call | flops 201326592 | bytes 1310720 | tf_op jit(solution)/shard_map/visit/pallas_call | solution.py:79
  38.0 0.1 collective-permute-start.8
  38.0 4.5 %collective-permute-start.6 = (f32[256,256]{1,0:T(8,128)S(1)}, f32[256,256]{1,0:T(8,128)S(1)}, u32[]{:S(2)}, u32[]{:S(2)}) collective-permute-start(f32[256,256]{1,0:T(8,128)S(1)} %collective-permute-done.5.items_ref), channel_id=1, source_target_pairs={{0,5},{1,6},{2,7},{3,4},{8,13},{9,14},{10,15},{11,12},{16,21},{17,... | collective-permute-start | bytes 786440 | tf_op jit(solution)/shard_map/ppermute | solution.py:23
  42.6 1.1 %multiply_subtract_fusion.1 = (f32[256,256]{1,0:T(8,128)}, f32[256,256]{1,0:T(8,128)}) fusion(f32[256,256]{1,0:T(8,128)S(1)} %get-tuple-element.27.users_ref, f32[256,256]{1,0:T(8,128)S(1)} %get-tuple-element.37, f32[256,256]{1,0:T(8,128)S(1)} %get-tuple-element.46, f32[256,256]{1,0:T(8,128)S(1)} %get-tuple-element.28, ...), kind=kOutput, calls=%fused_computation.14 | convolution fusion | flops 101318656 | bytes 1835008 | tf_op jit(solution)/shard_map/dot_general | solution.py:91
  43.7 5.4 %collective-permute-done.7 = f32[256,256]{1,0:T(8,128)S(1)} collective-permute-done((f32[256,256]{1,0:T(8,128)S(1)}, f32[256,256]{1,0:T(8,128)S(1)}, u32[]{:S(2)}, u32[]{:S(2)}) %collective-permute-start.7) | collective-permute-done | bytes 262176 | tf_op jit(solution)/shard_map/ppermute | solution.py:23
  49.0 0.0 collective-permute-done.9
  49.0 0.8 %collective-permute-done.8 = f32[256,256]{1,0:T(8,128)S(1)} collective-permute-done((f32[256,256]{1,0:T(8,128)S(1)}, f32[256,256]{1,0:T(8,128)S(1)}, u32[]{:S(2)}, u32[]{:S(2)}) %collective-permute-start.8) | collective-permute-done | bytes 262176 | tf_op jit(solution)/shard_map/ppermute | solution.py:23
  49.8 0.0 collective-permute-done.6
  49.8 0.9 %multiply_subtract_fusion = (f32[256,256]{1,0:T(8,128)}, f32[256,256]{1,0:T(8,128)}) fusion(f32[256,256]{1,0:T(8,128)S(1)} %collective-permute-done.8, f32[256,256]{1,0:T(8,128)S(1)} %collective-permute-done.6, f32[256,256]{1,0:T(8,128)S(1)} %collective-permute-done.7, pred[]{:T(512)S(6)} %eq.5, f32[256,256]{1,0:T(8,128)S(1)} %collective-permute-done.9), kind=kLoop, calls=%fused_computation.12 | loop fusion | flops 458752 | bytes 1572865 | tf_op jit(solution)/shard_map/sub | solution.py:96
  (2 shorter events, 0.1 us)
Async XLA Ops:
  0.6 1.6 %copy-start.1 = (f32[256,256]{1,0:T(8,128)S(1)}, f32[256,256]{1,0:T(8,128)}, u32[]{:S(2)}) copy-start(f32[256,256]{1,0:T(8,128)} %param.7) | copy-start | bytes 786436
  0.6 1.6 %copy-start = (f32[256,256]{1,0:T(8,128)S(1)}, f32[256,256]{1,0:T(8,128)}, u32[]{:S(2)}) copy-start(f32[256,256]{1,0:T(8,128)} %param.5) | copy-start | bytes 786436
  0.7 1.6 %copy-start.4 = (f32[256,256]{1,0:T(8,128)S(1)}, f32[256,256]{1,0:T(8,128)}, u32[]{:S(2)}) copy-start(f32[256,256]{1,0:T(8,128)} %param.8) | copy-start | bytes 786436
  2.2 3.4 %copy-start.3 = (f32[256,256]{1,0:T(8,128)S(1)}, f32[256,256]{1,0:T(8,128)}, u32[]{:S(2)}) copy-start(f32[256,256]{1,0:T(8,128)} %param.6) | copy-start | bytes 786436
  2.7 8.5 %copy-start.2 = (s32[256,1024]{1,0:T(8,128)S(1)}, s32[256,1024]{1,0:T(8,128)}, u32[]{:S(2)}) copy-start(s32[256,1024]{1,0:T(8,128)} %param.9) | copy-start | bytes 3145732
  2.7 13.2 %collective-permute-start = (f32[256,256]{1,0:T(8,128)S(1)}, f32[256,256]{1,0:T(8,128)S(1)}, u32[]{:S(2)}, u32[]{:S(2)}) collective-permute-start(f32[256,256]{1,0:T(8,128)S(1)} %get-tuple-element.19), channel_id=1, source_target_pairs={{0,4},{1,5},{2,6},{3,7},{4,8},{5,9},{6,10},{7,11},{8,12},{9,13},{1... | collective-permute-start | bytes 786440 | tf_op jit(solution)/shard_map/ppermute | solution.py:23
  6.0 17.1 %collective-permute-start.3 = (f32[256,256]{1,0:T(8,128)S(1)}, f32[256,256]{1,0:T(8,128)S(1)}, u32[]{:S(2)}, u32[]{:S(2)}) collective-permute-start(f32[256,256]{1,0:T(8,128)S(1)} %get-tuple-element.18), channel_id=1, source_target_pairs={{0,8},{1,9},{2,10},{3,11},{8,16},{9,17},{10,18},{11,19},{16,24},{1... | collective-permute-start | bytes 786440 | tf_op jit(solution)/shard_map/ppermute | solution.py:23
  9.5 13.6 %collective-permute-start.2 = (f32[256,256]{1,0:T(8,128)S(1)}, f32[256,256]{1,0:T(8,128)S(1)}, u32[]{:S(2)}, u32[]{:S(2)}) collective-permute-start(f32[256,256]{1,0:T(8,128)S(1)} %broadcast_select_fusion.1), channel_id=1, source_target_pairs={{0,8},{1,9},{2,10},{3,11},{4,12},{5,13},{6,14},{7,15},{8,16},{9,17... | collective-permute-start | bytes 786440 | tf_op jit(solution)/shard_map/ppermute | solution.py:23
  16.6 10.1 %collective-permute-start.4 = (f32[256,256]{1,0:T(8,128)S(1)}, f32[256,256]{1,0:T(8,128)S(1)}, u32[]{:S(2)}, u32[]{:S(2)}) collective-permute-start(f32[256,256]{1,0:T(8,128)S(1)} %get-tuple-element.21), channel_id=1, source_target_pairs={{0,4},{1,5},{2,6},{3,7},{4,8},{5,9},{6,10},{7,11},{8,12},{9,13},{1... | collective-permute-start | bytes 786440 | tf_op jit(solution)/shard_map/ppermute | solution.py:23
  16.6 10.1 %collective-permute-start.1 = (f32[256,256]{1,0:T(8,128)S(1)}, f32[256,256]{1,0:T(8,128)S(1)}, u32[]{:S(2)}, u32[]{:S(2)}) collective-permute-start(f32[256,256]{1,0:T(8,128)S(1)} %collective-permute-done.items_ref), channel_id=1, source_target_pairs={{0,4},{1,5},{2,6},{3,7},{8,12},{9,13},{10,14},{11,15},{16,20},{17,... | collective-permute-start | bytes 786440 | tf_op jit(solution)/shard_map/ppermute | solution.py:23
  27.6 9.6 %collective-permute-start.5 = (f32[256,256]{1,0:T(8,128)S(1)}, f32[256,256]{1,0:T(8,128)S(1)}, u32[]{:S(2)}, u32[]{:S(2)}) collective-permute-start(f32[256,256]{1,0:T(8,128)S(1)} %get-tuple-element.30), channel_id=1, source_target_pairs={{0,4},{1,5},{2,6},{3,7},{4,8},{5,9},{6,10},{7,11},{8,12},{9,13},{1... | collective-permute-start | bytes 786440 | tf_op jit(solution)/shard_map/ppermute | solution.py:23
  30.5 18.5 %collective-permute-start.9 = (f32[256,256]{1,0:T(8,128)S(1)}, f32[256,256]{1,0:T(8,128)S(1)}, u32[]{:S(2)}, u32[]{:S(2)}) collective-permute-start(f32[256,256]{1,0:T(8,128)S(1)} %get-tuple-element.29), channel_id=1, source_target_pairs={{0,9},{1,10},{2,11},{3,8},{8,17},{9,18},{10,19},{11,16},{16,25},{1... | collective-permute-start | bytes 786440 | tf_op jit(solution)/shard_map/ppermute | solution.py:23
  32.5 16.6 %collective-permute-start.7 = (f32[256,256]{1,0:T(8,128)S(1)}, f32[256,256]{1,0:T(8,128)S(1)}, u32[]{:S(2)}, u32[]{:S(2)}) collective-permute-start(f32[256,256]{1,0:T(8,128)S(1)} %broadcast_select_fusion), channel_id=1, source_target_pairs={{0,9},{1,10},{2,11},{3,8},{4,13},{5,14},{6,15},{7,12},{8,17},{9,18... | collective-permute-start | bytes 786440 | tf_op jit(solution)/shard_map/ppermute | solution.py:23
  38.0 11.9 %collective-permute-start.8 = (f32[256,256]{1,0:T(8,128)S(1)}, f32[256,256]{1,0:T(8,128)S(1)}, u32[]{:S(2)}, u32[]{:S(2)}) collective-permute-start(f32[256,256]{1,0:T(8,128)S(1)} %get-tuple-element.31), channel_id=1, source_target_pairs={{0,5},{1,6},{2,7},{3,4},{4,9},{5,10},{6,11},{7,8},{8,13},{9,14},{1... | collective-permute-start | bytes 786440 | tf_op jit(solution)/shard_map/ppermute | solution.py:23
  38.0 11.8 %collective-permute-start.6 = (f32[256,256]{1,0:T(8,128)S(1)}, f32[256,256]{1,0:T(8,128)S(1)}, u32[]{:S(2)}, u32[]{:S(2)}) collective-permute-start(f32[256,256]{1,0:T(8,128)S(1)} %collective-permute-done.5.items_ref), channel_id=1, source_target_pairs={{0,5},{1,6},{2,7},{3,4},{8,13},{9,14},{10,15},{11,12},{16,21},{17,... | collective-permute-start | bytes 786440 | tf_op jit(solution)/shard_map/ppermute | solution.py:23

commit v7 on v1

--- a/solution.py
+++ b/solution.py
@@ -1,6 +1,8 @@
 import jax
 import jax.numpy as jnp
 from jax import lax
+from jax.experimental import pallas as pl
+from jax.experimental.pallas import tpu as pltpu
 from jax.sharding import PartitionSpec as P
 
 conf_scale = 0.5
@@ -42,16 +44,85 @@
     return factors - step_rate * gradient / jnp.sqrt(sums), sums
 
 
+def halves(value):
+    high = value.astype(jnp.bfloat16)
+    return high, (value - high.astype(jnp.float32)).astype(jnp.bfloat16)
+
+
+def product(left, right, dims):
+    def dot(a, b):
+        return lax.dot_general(a, b, (dims, ((), ())), preferred_element_type=jnp.float32)
+
+    return dot(left[0], right[1]) + dot(left[1], right[0]) + dot(left[0], right[0])
+
+
+def first_kernel(
+    users_hbm, items_hbm, counts_hbm, acc_hbm, gap_ref, new_items_ref, new_acc_ref, users_ref, items_ref, tile_ref, acc_ref, done
+):
+    rows = items_ref.shape[0]
+    copies = [
+        pltpu.make_async_copy(source, target, done.at[index])
+        for index, (source, target) in enumerate(
+            [
+                (users_hbm, users_ref),
+                (items_hbm, items_ref),
+                (counts_hbm.at[:, pl.ds(0, rows)], tile_ref),
+                (acc_hbm, acc_ref),
+            ]
+        )
+    ]
+    for copy in copies:
+        copy.start()
+    copies[0].wait()
+    copies[1].wait()
+    items = items_ref[...]
+    users_parts = halves(users_ref[...])
+    predicted = product(users_parts, halves(items), ((1,), (1,)))
+    copies[2].wait()
+    tile = tile_ref[...]
+    prefer = (tile > 0).astype(jnp.float32)
+    gap = (1.0 + conf_scale * tile.astype(jnp.float32)) * (predicted - prefer)
+    gap_ref[...] = gap
+    grad = 2.0 * product(halves(gap), users_parts, ((0,), (0,))) + 2.0 * ridge_weight * items
+    copies[3].wait()
+    new_items_ref[...], new_acc_ref[...] = adagrad(items, acc_ref[...], grad)
+
+
+def first_stratum(*operands):
+    users, items, counts, item_acc = operands
+    shape, rows = items.shape, items.shape[0]
+    here, there = pl.BlockSpec(memory_space=pltpu.VMEM), pl.BlockSpec(memory_space=pltpu.HBM)
+    return pl.pallas_call(
+        first_kernel,
+        out_shape=[jax.ShapeDtypeStruct((users.shape[0], rows), jnp.float32)] + [jax.ShapeDtypeStruct(shape, jnp.float32)] * 2,
+        in_specs=[there] * 4,
+        out_specs=[here] * 3,
+        scratch_shapes=[
+            pltpu.VMEM(users.shape, jnp.float32),
+            pltpu.VMEM(shape, jnp.float32),
+            pltpu.VMEM((users.shape[0], rows), jnp.int32),
+            pltpu.VMEM(shape, jnp.float32),
+            pltpu.SemaphoreType.DMA((4,)),
+        ],
+        compiler_params=pltpu.CompilerParams(vmem_limit_bytes=16 * 2**20),
+        cost_estimate=pl.CostEstimate(flops=12 * rows**3, bytes_accessed=7 * 4 * rows**2, transcendentals=0),
+        name="first_stratum",
+    )(*[pltpu.with_memory_space_constraint(operand, pltpu.HBM) for operand in operands])
+
+
 def body(users, user_acc, items, item_acc, counts):
     rows = items.shape[0]
     tiles = [counts[:, s * rows : (s + 1) * rows] for s in range(4)]
     odd = lax.axis_index("blk") % 2 == 1
 
     def two_strata(users, user_acc, items, item_acc, first, up):
-        gap = weighted_gap(users, items, tiles[first])
-        grad_v = item_gradient(gap, users, items)
+        if first == 0:
+            gap, new_items, item_acc = first_stratum(users, items, counts, item_acc)
+        else:
+            gap = weighted_gap(users, items, tiles[first])
+            new_items, item_acc = adagrad(items, item_acc, item_gradient(gap, users, items))
         grad_u = user_gradient(gap, users, items)
-        items, item_acc = adagrad(items, item_acc, grad_v)
+        items = new_items
         users, user_acc = adagrad(users, user_acc, grad_u)
 
         visitor = sent(items, lambda b, g: (b + 1, g))

time: 50.9 us -> 50.9 us (level)
  Pallas kernels: 0 us -> 2.05 us
  matrix products: 6.26 us -> 4.33 us
    pallas_call x0 -> x1, Pallas kernels: none -> 2.05 us  [first_stratum(): pl.pallas_call(first_kernel, out_shape=[jax.ShapeDtypeStruct((users.shape...]
    dot_general x4 -> x3, matrix products: 2.56 us -> 1.04 us  [weighted_gap(): lax.dot_general(users, items, (((1,), (1,)), ((), ())), precision=PREC)]
    dot_general x4 -> x3, matrix products: 1.62 us -> 1.21 us  [item_gradient(): lax.dot_general(gap, users, (((0,), (0,)), ((), ())), precision=PREC)]
  transfers between devices with their start and end apart: 10 -> 10, of which waited for: 7 -> 6; matrix products, arithmetic and copies ran while one was open for 7% -> 7% of each run, Pallas kernels for 0% -> 0%
where the time goes in v7:
time: 50.9 us; the launch traced here: 50.7 us
  starting transfers between devices  22.5 us (44%)
  waiting for transfers between devices  20 us (39%)
  matrix products  4.33 us (9%)
  Pallas kernels  2.05 us (4%)
  other arithmetic  1.02 us (2%)
  between operations  0.82 us (2%)
    ppermute x10, starting transfers between devices, sent(): return lax.ppermute(value, ('blk', 'group'), pairs)  22.5 us
    ppermute x10, waiting for transfers between devices, sent(): return lax.ppermute(value, ('blk', 'group'), pairs)  20 us
    dot_general x4, matrix products, user_gradient(): jnp.dot(gap, items, precision=PREC)  2.08 us
    pallas_call x1, Pallas kernels, first_stratum(): pl.pallas_call(first_kernel, out_shape=[jax.ShapeDtypeStruct((users.shape...  2.05 us
    dot_general x3, matrix products, item_gradient(): lax.dot_general(gap, users, (((0,), (0,)), ((), ())), precision=PREC)  1.21 us
    dot_general x3, matrix products, weighted_gap(): lax.dot_general(users, items, (((1,), (1,)), ((), ())), precision=PREC)  1.04 us
  transfers between devices with their start and end apart: 10, of which 6 were waited for; matrix products, arithmetic and copies ran while one was open for 7% of the time, Pallas kernels for 0%

profile of v7, /device:TPU:0, one launch (start us, length us, event | category | flops | bytes accessed | tf_op | source)
XLA Modules:
  0.0 50.7 jit_solution(14149013048695246313)
XLA Ops:
  0.6 0.0 copy-start.2
  0.6 0.0 copy-start.1
  0.7 0.0 copy-start.3
  0.7 2.1 %first_stratum.1 = (f32[256,256]{1,0:T(8,128)S(1)}, f32[256,256]{1,0:T(8,128)S(1)}, f32[256,256]{1,0:T(8,128)S(1)}) custom-call(f32[256,256]{1,0:T(8,128)} %users_hbm.1, f32[256,256]{1,0:T(8,128)} %items_hbm.1, s32[256,1024]{1,0:T(8,128)} %counts_hbm.1, f32[256,256]{1,0:T(8,128)} %acc_hbm.1), custom_call_target="tpu_custom_call" | custom-call | flops 201326592 | bytes 1835008 | tf_op jit(solution)/shard_map/first_stratum/pallas_call | solution.py:95
  2.7 3.0 %collective-permute-start = (f32[256,256]{1,0:T(8,128)S(1)}, f32[256,256]{1,0:T(8,128)S(1)}, u32[]{:S(2)}, u32[]{:S(2)}) collective-permute-start(f32[256,256]{1,0:T(8,128)S(1)} %get-tuple-element.17), channel_id=1, source_target_pairs={{0,4},{1,5},{2,6},{3,7},{4,8},{5,9},{6,10},{7,11},{8,12},{9,13},{1... | collective-permute-start | bytes 786440 | tf_op jit(solution)/shard_map/ppermute | solution.py:23
  5.7 0.0 copy-done.2
  5.7 0.0 copy-done.1
  5.7 0.0 copy-done.3
  5.7 0.0 copy-start
  5.7 0.3 multiply_subtract_fusion.6
  6.1 3.5 %collective-permute-start.4 = (f32[256,256]{1,0:T(8,128)S(1)}, f32[256,256]{1,0:T(8,128)S(1)}, u32[]{:S(2)}, u32[]{:S(2)}) collective-permute-start(f32[256,256]{1,0:T(8,128)S(1)} %get-tuple-element.16), channel_id=1, source_target_pairs={{0,8},{1,9},{2,10},{3,11},{8,16},{9,17},{10,18},{11,19},{16,24},{1... | collective-permute-start | bytes 786440 | tf_op jit(solution)/shard_map/ppermute | solution.py:23
  9.6 1.6 %collective-permute-start.2 = (f32[256,256]{1,0:T(8,128)S(1)}, f32[256,256]{1,0:T(8,128)S(1)}, u32[]{:S(2)}, u32[]{:S(2)}) collective-permute-start(f32[256,256]{1,0:T(8,128)S(1)} %broadcast_select_fusion.1), channel_id=1, source_target_pairs={{0,8},{1,9},{2,10},{3,11},{4,12},{5,13},{6,14},{7,15},{8,16},{9,17... | collective-permute-start | bytes 786440 | tf_op jit(solution)/shard_map/ppermute | solution.py:23
  11.2 4.7 %collective-permute-done = f32[256,256]{1,0:T(8,128)S(1)} collective-permute-done((f32[256,256]{1,0:T(8,128)S(1)}, f32[256,256]{1,0:T(8,128)S(1)}, u32[]{:S(2)}, u32[]{:S(2)}) %collective-permute-start) | collective-permute-done | bytes 262176 | tf_op jit(solution)/shard_map/ppermute | solution.py:23
  15.9 0.0 copy-done
  15.9 0.3 fusion.5
  16.2 0.4 multiply_add_fusion.8
  16.6 0.1 collective-permute-start.3
  16.7 3.4 %collective-permute-start.1 = (f32[256,256]{1,0:T(8,128)S(1)}, f32[256,256]{1,0:T(8,128)S(1)}, u32[]{:S(2)}, u32[]{:S(2)}) collective-permute-start(f32[256,256]{1,0:T(8,128)S(1)} %collective-permute-done), channel_id=1, source_target_pairs={{0,4},{1,5},{2,6},{3,7},{8,12},{9,13},{10,14},{11,15},{16,20},{17,... | collective-permute-start | bytes 786440 | tf_op jit(solution)/shard_map/ppermute | solution.py:23
  20.1 0.3 multiply_subtract_fusion.4
  20.4 2.8 %collective-permute-done.2 = f32[256,256]{1,0:T(8,128)S(1)} collective-permute-done((f32[256,256]{1,0:T(8,128)S(1)}, f32[256,256]{1,0:T(8,128)S(1)}, u32[]{:S(2)}, u32[]{:S(2)}) %collective-permute-start.2) | collective-permute-done | bytes 262176 | tf_op jit(solution)/shard_map/ppermute | solution.py:23
  23.2 0.0 collective-permute-done.4
  23.2 3.6 %collective-permute-done.1 = f32[256,256]{1,0:T(8,128)S(1)} collective-permute-done((f32[256,256]{1,0:T(8,128)S(1)}, f32[256,256]{1,0:T(8,128)S(1)}, u32[]{:S(2)}, u32[]{:S(2)}) %collective-permute-start.1) | collective-permute-done | bytes 262176 | tf_op jit(solution)/shard_map/ppermute | solution.py:23
  26.8 0.0 collective-permute-done.3
  26.8 0.1 multiply_subtract_fusion.5
  26.9 0.3 fusion.3
  27.2 0.4 multiply_subtract_fusion.3
  27.7 2.5 %collective-permute-start.5 = (f32[256,256]{1,0:T(8,128)S(1)}, f32[256,256]{1,0:T(8,128)S(1)}, u32[]{:S(2)}, u32[]{:S(2)}) collective-permute-start(f32[256,256]{1,0:T(8,128)S(1)} %get-tuple-element.21), channel_id=1, source_target_pairs={{0,4},{1,5},{2,6},{3,7},{4,8},{5,9},{6,10},{7,11},{8,12},{9,13},{1... | collective-permute-start | bytes 786440 | tf_op jit(solution)/shard_map/ppermute | solution.py:23
  30.2 0.3 multiply_subtract_fusion.2
  30.5 1.9 %collective-permute-start.9 = (f32[256,256]{1,0:T(8,128)S(1)}, f32[256,256]{1,0:T(8,128)S(1)}, u32[]{:S(2)}, u32[]{:S(2)}) collective-permute-start(f32[256,256]{1,0:T(8,128)S(1)} %get-tuple-element.20), channel_id=1, source_target_pairs={{0,9},{1,10},{2,11},{3,8},{8,17},{9,18},{10,19},{11,16},{16,25},{1... | collective-permute-start | bytes 786440 | tf_op jit(solution)/shard_map/ppermute | solution.py:23
  32.5 2.0 %collective-permute-start.7 = (f32[256,256]{1,0:T(8,128)S(1)}, f32[256,256]{1,0:T(8,128)S(1)}, u32[]{:S(2)}, u32[]{:S(2)}) collective-permute-start(f32[256,256]{1,0:T(8,128)S(1)} %broadcast_select_fusion), channel_id=1, source_target_pairs={{0,9},{1,10},{2,11},{3,8},{4,13},{5,14},{6,15},{7,12},{8,17},{9,18... | collective-permute-start | bytes 786440 | tf_op jit(solution)/shard_map/ppermute | solution.py:23
  34.5 2.8 %collective-permute-done.5 = f32[256,256]{1,0:T(8,128)S(1)} collective-permute-done((f32[256,256]{1,0:T(8,128)S(1)}, f32[256,256]{1,0:T(8,128)S(1)}, u32[]{:S(2)}, u32[]{:S(2)}) %collective-permute-start.5) | collective-permute-done | bytes 262176 | tf_op jit(solution)/shard_map/ppermute | solution.py:23
  37.2 0.3 fusion.1
  37.6 0.4 multiply_add_fusion.1
  38.0 0.1 collective-permute-start.8
  38.0 4.5 %collective-permute-start.6 = (f32[256,256]{1,0:T(8,128)S(1)}, f32[256,256]{1,0:T(8,128)S(1)}, u32[]{:S(2)}, u32[]{:S(2)}) collective-permute-start(f32[256,256]{1,0:T(8,128)S(1)} %collective-permute-done.5), channel_id=1, source_target_pairs={{0,5},{1,6},{2,7},{3,4},{8,13},{9,14},{10,15},{11,12},{16,21},{17,... | collective-permute-start | bytes 786440 | tf_op jit(solution)/shard_map/ppermute | solution.py:23
  42.6 1.1 %multiply_subtract_fusion.1 = (f32[256,256]{1,0:T(8,128)}, f32[256,256]{1,0:T(8,128)}) fusion(f32[256,256]{1,0:T(8,128)S(1)} %get-tuple-element.19, f32[256,256]{1,0:T(8,128)S(1)} %get-tuple-element.29, f32[256,256]{1,0:T(8,128)S(1)} %get-tuple-element.33, f32[256,256]{1,0:T(8,128)S(1)} %fusion.1, f32[256,256]{1,0:T(8,128)S(1)} %collective-permute-done.5), kind=kOutput, calls=%fused_computation.20 | convolution fusion | flops 101318656 | bytes 1835008 | tf_op jit(solution)/shard_map/dot_general | solution.py:34
  43.7 5.4 %collective-permute-done.7 = f32[256,256]{1,0:T(8,128)S(1)} collective-permute-done((f32[256,256]{1,0:T(8,128)S(1)}, f32[256,256]{1,0:T(8,128)S(1)}, u32[]{:S(2)}, u32[]{:S(2)}) %collective-permute-start.7) | collective-permute-done | bytes 262176 | tf_op jit(solution)/shard_map/ppermute | solution.py:23
  49.1 0.0 collective-permute-done.9
  49.1 0.8 %collective-permute-done.8 = f32[256,256]{1,0:T(8,128)S(1)} collective-permute-done((f32[256,256]{1,0:T(8,128)S(1)}, f32[256,256]{1,0:T(8,128)S(1)}, u32[]{:S(2)}, u32[]{:S(2)}) %collective-permute-start.8) | collective-permute-done | bytes 262176 | tf_op jit(solution)/shard_map/ppermute | solution.py:23
  49.8 0.0 collective-permute-done.6
  49.9 0.9 %multiply_subtract_fusion = (f32[256,256]{1,0:T(8,128)}, f32[256,256]{1,0:T(8,128)}) fusion(f32[256,256]{1,0:T(8,128)S(1)} %collective-permute-done.8, f32[256,256]{1,0:T(8,128)S(1)} %collective-permute-done.6, f32[256,256]{1,0:T(8,128)S(1)} %collective-permute-done.7, pred[]{:T(512)S(6)} %eq.5, f32[256,256]{1,0:T(8,128)S(1)} %collective-permute-done.9), kind=kLoop, calls=%fused_computation.17 | loop fusion | flops 458752 | bytes 1572865 | tf_op jit(solution)/shard_map/sub | solution.py:44
  (2 shorter events, 0.1 us)
Async XLA Ops:
  0.6 5.1 %copy-start.2 = (f32[256,256]{1,0:T(8,128)S(1)}, f32[256,256]{1,0:T(8,128)}, u32[]{:S(2)}) copy-start(f32[256,256]{1,0:T(8,128)} %items_hbm.1) | copy-start | bytes 786436
  0.6 5.1 %copy-start.1 = (f32[256,256]{1,0:T(8,128)S(1)}, f32[256,256]{1,0:T(8,128)}, u32[]{:S(2)}) copy-start(f32[256,256]{1,0:T(8,128)} %users_hbm.1) | copy-start | bytes 786436
  0.7 5.1 %copy-start.3 = (f32[256,256]{1,0:T(8,128)S(1)}, f32[256,256]{1,0:T(8,128)}, u32[]{:S(2)}) copy-start(f32[256,256]{1,0:T(8,128)} %param.6) | copy-start | bytes 786436
  2.7 13.2 %collective-permute-start = (f32[256,256]{1,0:T(8,128)S(1)}, f32[256,256]{1,0:T(8,128)S(1)}, u32[]{:S(2)}, u32[]{:S(2)}) collective-permute-start(f32[256,256]{1,0:T(8,128)S(1)} %get-tuple-element.17), channel_id=1, source_target_pairs={{0,4},{1,5},{2,6},{3,7},{4,8},{5,9},{6,10},{7,11},{8,12},{9,13},{1... | collective-permute-start | bytes 786440 | tf_op jit(solution)/shard_map/ppermute | solution.py:23
  5.7 10.2 %copy-start = (s32[256,1024]{1,0:T(8,128)S(1)}, s32[256,1024]{1,0:T(8,128)}, u32[]{:S(2)}) copy-start(s32[256,1024]{1,0:T(8,128)} %counts_hbm.1) | copy-start | bytes 3145732
  6.1 17.1 %collective-permute-start.4 = (f32[256,256]{1,0:T(8,128)S(1)}, f32[256,256]{1,0:T(8,128)S(1)}, u32[]{:S(2)}, u32[]{:S(2)}) collective-permute-start(f32[256,256]{1,0:T(8,128)S(1)} %get-tuple-element.16), channel_id=1, source_target_pairs={{0,8},{1,9},{2,10},{3,11},{8,16},{9,17},{10,18},{11,19},{16,24},{1... | collective-permute-start | bytes 786440 | tf_op jit(solution)/shard_map/ppermute | solution.py:23
  9.6 13.6 %collective-permute-start.2 = (f32[256,256]{1,0:T(8,128)S(1)}, f32[256,256]{1,0:T(8,128)S(1)}, u32[]{:S(2)}, u32[]{:S(2)}) collective-permute-start(f32[256,256]{1,0:T(8,128)S(1)} %broadcast_select_fusion.1), channel_id=1, source_target_pairs={{0,8},{1,9},{2,10},{3,11},{4,12},{5,13},{6,14},{7,15},{8,16},{9,17... | collective-permute-start | bytes 786440 | tf_op jit(solution)/shard_map/ppermute | solution.py:23
  16.6 10.1 %collective-permute-start.3 = (f32[256,256]{1,0:T(8,128)S(1)}, f32[256,256]{1,0:T(8,128)S(1)}, u32[]{:S(2)}, u32[]{:S(2)}) collective-permute-start(f32[256,256]{1,0:T(8,128)S(1)} %multiply_add_fusion.8), channel_id=1, source_target_pairs={{0,4},{1,5},{2,6},{3,7},{4,8},{5,9},{6,10},{7,11},{8,12},{9,13},{1... | collective-permute-start | bytes 786440 | tf_op jit(solution)/shard_map/ppermute | solution.py:23
  16.7 10.1 %collective-permute-start.1 = (f32[256,256]{1,0:T(8,128)S(1)}, f32[256,256]{1,0:T(8,128)S(1)}, u32[]{:S(2)}, u32[]{:S(2)}) collective-permute-start(f32[256,256]{1,0:T(8,128)S(1)} %collective-permute-done), channel_id=1, source_target_pairs={{0,4},{1,5},{2,6},{3,7},{8,12},{9,13},{10,14},{11,15},{16,20},{17,... | collective-permute-start | bytes 786440 | tf_op jit(solution)/shard_map/ppermute | solution.py:23
  27.7 9.6 %collective-permute-start.5 = (f32[256,256]{1,0:T(8,128)S(1)}, f32[256,256]{1,0:T(8,128)S(1)}, u32[]{:S(2)}, u32[]{:S(2)}) collective-permute-start(f32[256,256]{1,0:T(8,128)S(1)} %get-tuple-element.21), channel_id=1, source_target_pairs={{0,4},{1,5},{2,6},{3,7},{4,8},{5,9},{6,10},{7,11},{8,12},{9,13},{1... | collective-permute-start | bytes 786440 | tf_op jit(solution)/shard_map/ppermute | solution.py:23
  30.5 18.5 %collective-permute-start.9 = (f32[256,256]{1,0:T(8,128)S(1)}, f32[256,256]{1,0:T(8,128)S(1)}, u32[]{:S(2)}, u32[]{:S(2)}) collective-permute-start(f32[256,256]{1,0:T(8,128)S(1)} %get-tuple-element.20), channel_id=1, source_target_pairs={{0,9},{1,10},{2,11},{3,8},{8,17},{9,18},{10,19},{11,16},{16,25},{1... | collective-permute-start | bytes 786440 | tf_op jit(solution)/shard_map/ppermute | solution.py:23
  32.5 16.6 %collective-permute-start.7 = (f32[256,256]{1,0:T(8,128)S(1)}, f32[256,256]{1,0:T(8,128)S(1)}, u32[]{:S(2)}, u32[]{:S(2)}) collective-permute-start(f32[256,256]{1,0:T(8,128)S(1)} %broadcast_select_fusion), channel_id=1, source_target_pairs={{0,9},{1,10},{2,11},{3,8},{4,13},{5,14},{6,15},{7,12},{8,17},{9,18... | collective-permute-start | bytes 786440 | tf_op jit(solution)/shard_map/ppermute | solution.py:23
  38.0 11.9 %collective-permute-start.8 = (f32[256,256]{1,0:T(8,128)S(1)}, f32[256,256]{1,0:T(8,128)S(1)}, u32[]{:S(2)}, u32[]{:S(2)}) collective-permute-start(f32[256,256]{1,0:T(8,128)S(1)} %multiply_add_fusion.1), channel_id=1, source_target_pairs={{0,5},{1,6},{2,7},{3,4},{4,9},{5,10},{6,11},{7,8},{8,13},{9,14},{1... | collective-permute-start | bytes 786440 | tf_op jit(solution)/shard_map/ppermute | solution.py:23
  38.0 11.8 %collective-permute-start.6 = (f32[256,256]{1,0:T(8,128)S(1)}, f32[256,256]{1,0:T(8,128)S(1)}, u32[]{:S(2)}, u32[]{:S(2)}) collective-permute-start(f32[256,256]{1,0:T(8,128)S(1)} %collective-permute-done.5), channel_id=1, source_target_pairs={{0,5},{1,6},{2,7},{3,4},{8,13},{9,14},{10,15},{11,12},{16,21},{17,... | collective-permute-start | bytes 786440 | tf_op jit(solution)/shard_map/ppermute | solution.py:23

commit v8 on v5

--- a/solution.py
+++ b/solution.py
@@ -21,8 +21,8 @@
     return lax.ppermute(value, ("blk", "group"), pairs)
 
 
-def passes_on(b, g, n_blk):
-    return (b % 2 == 1) & ((g % 2 == 1) | (b % n_blk >= n_blk - 2))
+def passes_on(b, g, n_blk, up):
+    return (b % 2 == 1) & ((up == 0) | (g % 2 == 1) | (b % n_blk >= n_blk - 2))
 
 
 def weighted_gap(users, items, count_tile):
@@ -50,7 +50,6 @@
     rows = items.shape[0]
     tiles = [counts[:, s * rows : (s + 1) * rows] for s in range(4)]
     n_blk, blk, group = lax.axis_size("blk"), lax.axis_index("blk"), lax.axis_index("group")
-    passing = passes_on(blk, group, n_blk)
 
     def two_strata(users, user_acc, items, item_acc, first, up):
         gap = weighted_gap(users, items, tiles[first])
@@ -61,15 +60,16 @@
 
         visitor = sent(items, lambda b, g: (b + 1, g))
         items, item_acc, users = lax.optimization_barrier((items, item_acc, users))
+        passing = passes_on(blk, group, n_blk, up)
         ahead = sent(jnp.where(passing, item_acc, items), lambda b, g: (b + 2, g + up))
-        late = sent(item_acc, lambda b, g: None if passes_on(b, g, n_blk) else (b + 2, g + up))
-        passed = sent(visitor, lambda b, g: (b + 1, g + up) if passes_on(b - 1, g, n_blk) else None)
+        late = sent(item_acc, lambda b, g: None if passes_on(b, g, n_blk, up) else (b + 2, g + up))
+        passed = sent(visitor, lambda b, g: (b + 1, g + up) if passes_on(b - 1, g, n_blk, up) else None)
         gap = weighted_gap(users, visitor, tiles[first + 1])
         grad_v = item_gradient(gap, users, visitor)
         grad_u = user_gradient(gap, users, visitor)
         grad_v = sent(grad_v, lambda b, g: (b + 1, g + up))
         users, user_acc = adagrad(users, user_acc, grad_u)
-        came_by_visit = passes_on((blk - 2) % n_blk, group - up, n_blk)
+        came_by_visit = passes_on((blk - 2) % n_blk, group - up, n_blk, up)
         items = jnp.where(came_by_visit, passed, ahead)
         item_acc = jnp.where(came_by_visit, ahead, late)
         items, item_acc = adagrad(items, item_acc, grad_v)

time: 50.9 us -> 50.9 us (level)
  no operation moved by 1% of the time
where the time goes in v8:
time: 50.9 us; the launch traced here: 50.7 us
  starting transfers between devices  22.2 us (44%)
  waiting for transfers between devices  20.3 us (40%)
  matrix products  6.27 us (12%)
  other arithmetic  1.01 us (2%)
  between operations  0.86 us (2%)
    ppermute x10, starting transfers between devices, sent(): return lax.ppermute(value, ('blk', 'group'), pairs)  22.2 us
    ppermute x10, waiting for transfers between devices, sent(): return lax.ppermute(value, ('blk', 'group'), pairs)  20.3 us
    dot_general x4, matrix products, weighted_gap(): lax.dot_general(users, items, (((1,), (1,)), ((), ())), precision=PREC)  2.56 us
    dot_general x4, matrix products, user_gradient(): jnp.dot(gap, items, precision=PREC)  2.08 us
    dot_general x4, matrix products, item_gradient(): lax.dot_general(gap, users, (((0,), (0,)), ((), ())), precision=PREC)  1.63 us
  transfers between devices with their start and end apart: 10, of which 8 were waited for; matrix products, arithmetic and copies ran while one was open for 7% of the time, Pallas kernels for 0%

profile of v8, /device:TPU:0, one launch (start us, length us, event | category | flops | bytes accessed | tf_op | source)
XLA Modules:
  0.0 50.7 jit_solution(7236224798031882204)
XLA Ops:
  0.6 0.0 copy-start.1
  0.6 0.0 copy-start
  0.7 0.0 copy-start.4
  0.7 1.5 %fusion.8 = f32[256,256]{1,0:T(8,128)S(1)} fusion(f32[256,256]{1,0:T(8,128)} %param.5, f32[256,256]{1,0:T(8,128)} %param.7, s32[256,1024]{1,0:T(8,128)} %param.9), kind=kOutput, calls=%fused_computation.20 | convolution fusion | flops 101122048 | bytes 1048576 | tf_op jit(solution)/shard_map/dot_general | solution.py:29
  2.2 0.0 copy-done.1
  2.2 0.0 copy-done
  2.2 0.0 copy-done.4
  2.2 0.0 copy-start.2
  2.2 0.4 multiply_subtract_fusion.7
  2.7 0.0 copy-start.3
  2.7 3.0 %collective-permute-start = (f32[256,256]{1,0:T(8,128)S(1)}, f32[256,256]{1,0:T(8,128)S(1)}, u32[]{:S(2)}, u32[]{:S(2)}) collective-permute-start(f32[256,256]{1,0:T(8,128)S(1)} %get-tuple-element.11), channel_id=1, source_target_pairs={{0,4},{1,5},{2,6},{3,7},{4,8},{5,9},{6,10},{7,11},{8,12},{9,13},{1... | collective-permute-start | bytes 786440 | tf_op jit(solution)/shard_map/ppermute | solution.py:21
  5.7 0.0 copy-done.2
  5.7 0.3 multiply_subtract_fusion.6
  6.0 3.5 %collective-permute-start.4 = (f32[256,256]{1,0:T(8,128)S(1)}, f32[256,256]{1,0:T(8,128)S(1)}, u32[]{:S(2)}, u32[]{:S(2)}) collective-permute-start(f32[256,256]{1,0:T(8,128)S(1)} %get-tuple-element.10), channel_id=1, source_target_pairs={{0,8},{1,9},{2,10},{3,11},{8,16},{9,17},{10,18},{11,19},{16,24},{1... | collective-permute-start | bytes 786440 | tf_op jit(solution)/shard_map/ppermute | solution.py:21
  9.5 1.6 %collective-permute-start.2 = (f32[256,256]{1,0:T(8,128)S(1)}, f32[256,256]{1,0:T(8,128)S(1)}, u32[]{:S(2)}, u32[]{:S(2)}) collective-permute-start(f32[256,256]{1,0:T(8,128)S(1)} %broadcast_select_fusion.1), channel_id=1, source_target_pairs={{0,8},{1,9},{2,10},{3,11},{4,12},{5,13},{6,14},{7,15},{8,16},{9,17... | collective-permute-start | bytes 786440 | tf_op jit(solution)/shard_map/ppermute | solution.py:21
  11.2 4.7 %collective-permute-done = f32[256,256]{1,0:T(8,128)S(1)} collective-permute-done((f32[256,256]{1,0:T(8,128)S(1)}, f32[256,256]{1,0:T(8,128)S(1)}, u32[]{:S(2)}, u32[]{:S(2)}) %collective-permute-start) | collective-permute-done | bytes 262176 | tf_op jit(solution)/shard_map/ppermute | solution.py:21
  15.8 0.0 copy-done.3
  15.8 0.3 fusion.5
  16.2 0.4 multiply_add_fusion.8
  16.6 0.1 collective-permute-start.3
  16.7 3.4 %collective-permute-start.1 = (f32[256,256]{1,0:T(8,128)S(1)}, f32[256,256]{1,0:T(8,128)S(1)}, u32[]{:S(2)}, u32[]{:S(2)}) collective-permute-start(f32[256,256]{1,0:T(8,128)S(1)} %collective-permute-done), channel_id=1, source_target_pairs={{0,4},{1,5},{2,6},{3,7},{8,12},{9,13},{10,14},{11,15},{16,20},{17,... | collective-permute-start | bytes 786440 | tf_op jit(solution)/shard_map/ppermute | solution.py:21
  20.0 0.3 multiply_subtract_fusion.4
  20.4 2.8 %collective-permute-done.2 = f32[256,256]{1,0:T(8,128)S(1)} collective-permute-done((f32[256,256]{1,0:T(8,128)S(1)}, f32[256,256]{1,0:T(8,128)S(1)}, u32[]{:S(2)}, u32[]{:S(2)}) %collective-permute-start.2) | collective-permute-done | bytes 262176 | tf_op jit(solution)/shard_map/ppermute | solution.py:21
  23.1 0.0 collective-permute-done.4
  23.1 3.1 %collective-permute-done.3 = f32[256,256]{1,0:T(8,128)S(1)} collective-permute-done((f32[256,256]{1,0:T(8,128)S(1)}, f32[256,256]{1,0:T(8,128)S(1)}, u32[]{:S(2)}, u32[]{:S(2)}) %collective-permute-start.3) | collective-permute-done | bytes 262176 | tf_op jit(solution)/shard_map/ppermute | solution.py:21
  26.2 0.5 collective-permute-done.1
  26.7 0.1 multiply_subtract_fusion.5
  26.8 0.3 fusion.3
  27.2 0.4 multiply_subtract_fusion.3
  27.6 2.5 %collective-permute-start.5 = (f32[256,256]{1,0:T(8,128)S(1)}, f32[256,256]{1,0:T(8,128)S(1)}, u32[]{:S(2)}, u32[]{:S(2)}) collective-permute-start(f32[256,256]{1,0:T(8,128)S(1)} %get-tuple-element.15), channel_id=1, source_target_pairs={{0,4},{1,5},{2,6},{3,7},{4,8},{5,9},{6,10},{7,11},{8,12},{9,13},{1... | collective-permute-start | bytes 786440 | tf_op jit(solution)/shard_map/ppermute | solution.py:21
  30.1 0.3 multiply_subtract_fusion.2
  30.5 1.9 %collective-permute-start.9 = (f32[256,256]{1,0:T(8,128)S(1)}, f32[256,256]{1,0:T(8,128)S(1)}, u32[]{:S(2)}, u32[]{:S(2)}) collective-permute-start(f32[256,256]{1,0:T(8,128)S(1)} %get-tuple-element.14), channel_id=1, source_target_pairs={{0,9},{1,10},{2,11},{3,8},{4,13},{6,15},{8,17},{9,18},{10,19},{11,... | collective-permute-start | bytes 786440 | tf_op jit(solution)/shard_map/ppermute | solution.py:21
  32.4 2.0 %collective-permute-start.7 = (f32[256,256]{1,0:T(8,128)S(1)}, f32[256,256]{1,0:T(8,128)S(1)}, u32[]{:S(2)}, u32[]{:S(2)}) collective-permute-start(f32[256,256]{1,0:T(8,128)S(1)} %broadcast_select_fusion), channel_id=1, source_target_pairs={{0,9},{1,10},{2,11},{3,8},{4,13},{5,14},{6,15},{7,12},{8,17},{9,18... | collective-permute-start | bytes 786440 | tf_op jit(solution)/shard_map/ppermute | solution.py:21
  34.4 2.3 %collective-permute-done.5 = f32[256,256]{1,0:T(8,128)S(1)} collective-permute-done((f32[256,256]{1,0:T(8,128)S(1)}, f32[256,256]{1,0:T(8,128)S(1)}, u32[]{:S(2)}, u32[]{:S(2)}) %collective-permute-start.5) | collective-permute-done | bytes 262176 | tf_op jit(solution)/shard_map/ppermute | solution.py:21
  36.7 0.3 fusion.1
  37.1 0.4 multiply_add_fusion.1
  37.5 0.1 collective-permute-start.8
  37.5 4.2 %collective-permute-start.6 = (f32[256,256]{1,0:T(8,128)S(1)}, f32[256,256]{1,0:T(8,128)S(1)}, u32[]{:S(2)}, u32[]{:S(2)}) collective-permute-start(f32[256,256]{1,0:T(8,128)S(1)} %collective-permute-done.5), channel_id=1, source_target_pairs={{0,5},{1,6},{2,7},{3,4},{9,14},{11,12},{17,22},{19,20},{25,30},{27... | collective-permute-start | bytes 786440 | tf_op jit(solution)/shard_map/ppermute | solution.py:21
  41.8 1.1 %multiply_subtract_fusion.1 = (f32[256,256]{1,0:T(8,128)}, f32[256,256]{1,0:T(8,128)}) fusion(f32[256,256]{1,0:T(8,128)S(1)} %get-tuple-element.13, f32[256,256]{1,0:T(8,128)S(1)} %get-tuple-element.23, f32[256,256]{1,0:T(8,128)S(1)} %get-tuple-element.29, f32[256,256]{1,0:T(8,128)S(1)} %fusion.1, f32[256,256]{1,0:T(8,128)S(1)} %collective-permute-done.5), kind=kOutput, calls=%fused_computation.24 | convolution fusion | flops 101318656 | bytes 1835008 | tf_op jit(solution)/shard_map/dot_general | solution.py:36
  42.9 5.9 %collective-permute-done.7 = f32[256,256]{1,0:T(8,128)S(1)} collective-permute-done((f32[256,256]{1,0:T(8,128)S(1)}, f32[256,256]{1,0:T(8,128)S(1)}, u32[]{:S(2)}, u32[]{:S(2)}) %collective-permute-start.7) | collective-permute-done | bytes 262176 | tf_op jit(solution)/shard_map/ppermute | solution.py:21
  48.8 0.0 collective-permute-done.9
  48.8 0.8 %collective-permute-done.8 = f32[256,256]{1,0:T(8,128)S(1)} collective-permute-done((f32[256,256]{1,0:T(8,128)S(1)}, f32[256,256]{1,0:T(8,128)S(1)}, u32[]{:S(2)}, u32[]{:S(2)}) %collective-permute-start.8) | collective-permute-done | bytes 262176 | tf_op jit(solution)/shard_map/ppermute | solution.py:21
  49.6 0.3 collective-permute-done.6
  49.8 0.9 %multiply_subtract_fusion = (f32[256,256]{1,0:T(8,128)}, f32[256,256]{1,0:T(8,128)}) fusion(f32[256,256]{1,0:T(8,128)S(1)} %collective-permute-done.8, f32[256,256]{1,0:T(8,128)S(1)} %collective-permute-done.6, f32[256,256]{1,0:T(8,128)S(1)} %collective-permute-done.7, pred[]{:T(512)S(6)} %and.45, f32[256,256]{1,0:T(8,128)S(1)} %collective-permute-done.9), kind=kLoop, calls=%fused_computation.21 | loop fusion | flops 458752 | bytes 1572865 | tf_op jit(solution)/shard_map/sub | solution.py:46
  (2 shorter events, 0.1 us)
Async XLA Ops:
  0.6 1.6 %copy-start.1 = (f32[256,256]{1,0:T(8,128)S(1)}, f32[256,256]{1,0:T(8,128)}, u32[]{:S(2)}) copy-start(f32[256,256]{1,0:T(8,128)} %param.7) | copy-start | bytes 786436
  0.6 1.6 %copy-start = (f32[256,256]{1,0:T(8,128)S(1)}, f32[256,256]{1,0:T(8,128)}, u32[]{:S(2)}) copy-start(f32[256,256]{1,0:T(8,128)} %param.5) | copy-start | bytes 786436
  0.7 1.6 %copy-start.4 = (f32[256,256]{1,0:T(8,128)S(1)}, f32[256,256]{1,0:T(8,128)}, u32[]{:S(2)}) copy-start(f32[256,256]{1,0:T(8,128)} %param.8) | copy-start | bytes 786436
  2.2 3.4 %copy-start.2 = (f32[256,256]{1,0:T(8,128)S(1)}, f32[256,256]{1,0:T(8,128)}, u32[]{:S(2)}) copy-start(f32[256,256]{1,0:T(8,128)} %param.6) | copy-start | bytes 786436
  2.7 13.2 %copy-start.3 = (s32[256,1024]{1,0:T(8,128)S(1)}, s32[256,1024]{1,0:T(8,128)}, u32[]{:S(2)}) copy-start(s32[256,1024]{1,0:T(8,128)} %param.9) | copy-start | bytes 3145732
  2.7 13.2 %collective-permute-start = (f32[256,256]{1,0:T(8,128)S(1)}, f32[256,256]{1,0:T(8,128)S(1)}, u32[]{:S(2)}, u32[]{:S(2)}) collective-permute-start(f32[256,256]{1,0:T(8,128)S(1)} %get-tuple-element.11), channel_id=1, source_target_pairs={{0,4},{1,5},{2,6},{3,7},{4,8},{5,9},{6,10},{7,11},{8,12},{9,13},{1... | collective-permute-start | bytes 786440 | tf_op jit(solution)/shard_map/ppermute | solution.py:21
  6.0 17.1 %collective-permute-start.4 = (f32[256,256]{1,0:T(8,128)S(1)}, f32[256,256]{1,0:T(8,128)S(1)}, u32[]{:S(2)}, u32[]{:S(2)}) collective-permute-start(f32[256,256]{1,0:T(8,128)S(1)} %get-tuple-element.10), channel_id=1, source_target_pairs={{0,8},{1,9},{2,10},{3,11},{8,16},{9,17},{10,18},{11,19},{16,24},{1... | collective-permute-start | bytes 786440 | tf_op jit(solution)/shard_map/ppermute | solution.py:21
  9.5 13.6 %collective-permute-start.2 = (f32[256,256]{1,0:T(8,128)S(1)}, f32[256,256]{1,0:T(8,128)S(1)}, u32[]{:S(2)}, u32[]{:S(2)}) collective-permute-start(f32[256,256]{1,0:T(8,128)S(1)} %broadcast_select_fusion.1), channel_id=1, source_target_pairs={{0,8},{1,9},{2,10},{3,11},{4,12},{5,13},{6,14},{7,15},{8,16},{9,17... | collective-permute-start | bytes 786440 | tf_op jit(solution)/shard_map/ppermute | solution.py:21
  16.6 9.6 %collective-permute-start.3 = (f32[256,256]{1,0:T(8,128)S(1)}, f32[256,256]{1,0:T(8,128)S(1)}, u32[]{:S(2)}, u32[]{:S(2)}) collective-permute-start(f32[256,256]{1,0:T(8,128)S(1)} %multiply_add_fusion.8), channel_id=1, source_target_pairs={{0,4},{1,5},{2,6},{3,7},{4,8},{5,9},{6,10},{7,11},{8,12},{9,13},{1... | collective-permute-start | bytes 786440 | tf_op jit(solution)/shard_map/ppermute | solution.py:21
  16.7 10.1 %collective-permute-start.1 = (f32[256,256]{1,0:T(8,128)S(1)}, f32[256,256]{1,0:T(8,128)S(1)}, u32[]{:S(2)}, u32[]{:S(2)}) collective-permute-start(f32[256,256]{1,0:T(8,128)S(1)} %collective-permute-done), channel_id=1, source_target_pairs={{0,4},{1,5},{2,6},{3,7},{8,12},{9,13},{10,14},{11,15},{16,20},{17,... | collective-permute-start | bytes 786440 | tf_op jit(solution)/shard_map/ppermute | solution.py:21
  27.6 9.1 %collective-permute-start.5 = (f32[256,256]{1,0:T(8,128)S(1)}, f32[256,256]{1,0:T(8,128)S(1)}, u32[]{:S(2)}, u32[]{:S(2)}) collective-permute-start(f32[256,256]{1,0:T(8,128)S(1)} %get-tuple-element.15), channel_id=1, source_target_pairs={{0,4},{1,5},{2,6},{3,7},{4,8},{5,9},{6,10},{7,11},{8,12},{9,13},{1... | collective-permute-start | bytes 786440 | tf_op jit(solution)/shard_map/ppermute | solution.py:21
  30.5 18.3 %collective-permute-start.9 = (f32[256,256]{1,0:T(8,128)S(1)}, f32[256,256]{1,0:T(8,128)S(1)}, u32[]{:S(2)}, u32[]{:S(2)}) collective-permute-start(f32[256,256]{1,0:T(8,128)S(1)} %get-tuple-element.14), channel_id=1, source_target_pairs={{0,9},{1,10},{2,11},{3,8},{4,13},{6,15},{8,17},{9,18},{10,19},{11,... | collective-permute-start | bytes 786440 | tf_op jit(solution)/shard_map/ppermute | solution.py:21
  32.4 16.3 %collective-permute-start.7 = (f32[256,256]{1,0:T(8,128)S(1)}, f32[256,256]{1,0:T(8,128)S(1)}, u32[]{:S(2)}, u32[]{:S(2)}) collective-permute-start(f32[256,256]{1,0:T(8,128)S(1)} %broadcast_select_fusion), channel_id=1, source_target_pairs={{0,9},{1,10},{2,11},{3,8},{4,13},{5,14},{6,15},{7,12},{8,17},{9,18... | collective-permute-start | bytes 786440 | tf_op jit(solution)/shard_map/ppermute | solution.py:21
  37.5 12.1 %collective-permute-start.8 = (f32[256,256]{1,0:T(8,128)S(1)}, f32[256,256]{1,0:T(8,128)S(1)}, u32[]{:S(2)}, u32[]{:S(2)}) collective-permute-start(f32[256,256]{1,0:T(8,128)S(1)} %multiply_add_fusion.1), channel_id=1, source_target_pairs={{0,5},{1,6},{2,7},{3,4},{4,9},{5,10},{6,11},{7,8},{8,13},{9,14},{1... | collective-permute-start | bytes 786440 | tf_op jit(solution)/shard_map/ppermute | solution.py:21
  37.5 12.3 %collective-permute-start.6 = (f32[256,256]{1,0:T(8,128)S(1)}, f32[256,256]{1,0:T(8,128)S(1)}, u32[]{:S(2)}, u32[]{:S(2)}) collective-permute-start(f32[256,256]{1,0:T(8,128)S(1)} %collective-permute-done.5), channel_id=1, source_target_pairs={{0,5},{1,6},{2,7},{3,4},{9,14},{11,12},{17,22},{19,20},{25,30},{27... | collective-permute-start | bytes 786440 | tf_op jit(solution)/shard_map/ppermute | solution.py:21

commit v9 on v6

--- a/solution.py
+++ b/solution.py
@@ -72,6 +72,40 @@
     new_items_ref[...], new_acc_ref[...] = adagrad(items, acc, grad)
 
 
+def last_kernel(odd_ref, passed_ref, ahead_ref, even_acc_ref, grad_ref, items_hbm, acc_hbm, items_ref, acc_ref, done):
+    odd = odd_ref[0] == 1
+    parts = done.shape[0]
+    size = grad_ref.shape[0] // parts
+    copies = []
+    for part in range(parts):
+        at = pl.ds(part * size, size)
+        ahead = ahead_ref[at, :]
+        items_ref[at, :], acc_ref[at, :] = adagrad(
+            jnp.where(odd, passed_ref[at, :], ahead), jnp.where(odd, ahead, even_acc_ref[at, :]), grad_ref[at, :]
+        )
+        for index, (source, target) in enumerate([(items_ref, items_hbm), (acc_ref, acc_hbm)]):
+            copy = pltpu.make_async_copy(source.at[at, :], target.at[at, :], done.at[part, index])
+            copy.start()
+            copies.append(copy)
+    for copy in copies:
+        copy.wait()
+
+
+def last_update(odd_flag, passed, ahead, even_acc, grad):
+    here, there = pl.BlockSpec(memory_space=pltpu.VMEM), pl.BlockSpec(memory_space=pltpu.HBM)
+    shape = jax.ShapeDtypeStruct(grad.shape, jnp.float32)
+    return pl.pallas_call(
+        last_kernel,
+        out_shape=[shape] * 2,
+        in_specs=[pl.BlockSpec(memory_space=pltpu.SMEM)] + [here] * 4,
+        out_specs=[there] * 2,
+        scratch_shapes=[pltpu.VMEM(grad.shape, jnp.float32)] * 2 + [pltpu.SemaphoreType.DMA((4, 2))],
+        compiler_params=pltpu.CompilerParams(vmem_limit_bytes=8 * 2**20),
+        cost_estimate=pl.CostEstimate(flops=8 * grad.size, bytes_accessed=24 * grad.size, transcendentals=grad.size),
+        name="last_update",
+    )(odd_flag, passed, ahead, even_acc, grad)
+
+
 def on_vmem(kernel, name, outputs, *operands):
     here = pl.BlockSpec(memory_space=pltpu.VMEM)
     scalars = pl.BlockSpec(memory_space=pltpu.SMEM)
@@ -93,7 +127,7 @@
 
 def adagrad(factors, sums, gradient):
     sums = sums + gradient * gradient
-    return factors - step_rate * gradient / jnp.sqrt(sums), sums
+    return factors - step_rate * gradient * lax.rsqrt(sums), sums
 
 
 def body(users, user_acc, items, item_acc, counts):
@@ -127,7 +161,7 @@
     users, visitor, (passed, ahead, even_acc) = send_off(users, new_items, new_acc, 1)
     users, user_acc, grad = visit(users, user_acc, visitor, tiles[3], 1)
 
-    items, item_acc = adagrad(jnp.where(odd, passed, ahead), jnp.where(odd, ahead, even_acc), grad)
+    items, item_acc = last_update(odd_flag, passed, ahead, even_acc, grad)
     return users, user_acc, items, item_acc
 
 

time: 50.9 us -> 50.8 us (level)
  other arithmetic: 0.93 us -> 0.07 us
  Pallas kernels: 2.4 us -> 3.16 us
    pallas_call x0 -> x1, Pallas kernels: none -> 0.87 us  [last_update(): pl.pallas_call(last_kernel, out_shape=[shape] * 2, in_specs=[pl.BlockSpec...]
    sub x1 -> x0, other arithmetic: 0.86 us -> none  [adagrad(): return (factors - step_rate * gradient / jnp.sqrt(sums), sums)]
where the time goes in v9:
time: 50.8 us; the launch traced here: 50.6 us
  starting transfers between devices  22.5 us (44%)
  waiting for transfers between devices  19.9 us (39%)
  matrix products  4.01 us (8%)
  Pallas kernels  3.16 us (6%)
  between operations  0.84 us (2%)
    ppermute x10, starting transfers between devices, sent(): return lax.ppermute(value, ('blk', 'group'), pairs)  22.5 us
    ppermute x10, waiting for transfers between devices, sent(): return lax.ppermute(value, ('blk', 'group'), pairs)  19.9 us
    pallas_call x3, Pallas kernels, on_vmem(): pl.pallas_call(kernel, out_shape=[jax.ShapeDtypeStruct(shape, jnp.float32...  2.28 us
    dot_general x4, matrix products, user_gradient(): jnp.dot(gap, items, precision=PREC)  2.08 us
    dot_general x1, matrix products, weighted_gap(): lax.dot_general(users, items, (((1,), (1,)), ((), ())), precision=PREC)  1.52 us
  transfers between devices with their start and end apart: 10, of which 6 were waited for; matrix products, arithmetic and copies ran while one was open for 4% of the time, Pallas kernels for 3%

profile of v9, /device:TPU:0, one launch (start us, length us, event | category | flops | bytes accessed | tf_op | source)
XLA Modules:
  0.0 50.6 jit_solution(6285965560824252177)
XLA Ops:
  0.6 0.0 copy-start.1
  0.6 0.0 copy-start
  0.7 0.0 copy-start.4
  0.7 1.5 %fusion.5 = f32[256,256]{1,0:T(8,128)S(1)} fusion(f32[256,256]{1,0:T(8,128)} %param.5, f32[256,256]{1,0:T(8,128)} %param.7, s32[256,1024]{1,0:T(8,128)} %param.9), kind=kOutput, calls=%fused_computation.11 | convolution fusion | flops 101122048 | bytes 1048576 | tf_op jit(solution)/shard_map/dot_general | solution.py:39
  2.2 0.0 copy-done.1
  2.2 0.0 copy-done
  2.2 0.0 copy-done.4
  2.2 0.0 copy-start.3
  2.2 0.4 multiply_subtract_fusion.4
  2.7 0.0 copy-start.2
  2.7 3.0 %collective-permute-start = (f32[256,256]{1,0:T(8,128)S(1)}, f32[256,256]{1,0:T(8,128)S(1)}, u32[]{:S(2)}, u32[]{:S(2)}) collective-permute-start(f32[256,256]{1,0:T(8,128)S(1)} %get-tuple-element.21), channel_id=1, source_target_pairs={{0,4},{1,5},{2,6},{3,7},{4,8},{5,9},{6,10},{7,11},{8,12},{9,13},{1... | collective-permute-start | bytes 786440 | tf_op jit(solution)/shard_map/ppermute | solution.py:23
  5.7 0.0 copy-done.3
  5.7 0.3 multiply_subtract_fusion.3
  6.0 3.5 %collective-permute-start.3 = (f32[256,256]{1,0:T(8,128)S(1)}, f32[256,256]{1,0:T(8,128)S(1)}, u32[]{:S(2)}, u32[]{:S(2)}) collective-permute-start(f32[256,256]{1,0:T(8,128)S(1)} %get-tuple-element.20), channel_id=1, source_target_pairs={{0,8},{1,9},{2,10},{3,11},{8,16},{9,17},{10,18},{11,19},{16,24},{1... | collective-permute-start | bytes 786440 | tf_op jit(solution)/shard_map/ppermute | solution.py:23
  9.5 1.6 %collective-permute-start.2 = (f32[256,256]{1,0:T(8,128)S(1)}, f32[256,256]{1,0:T(8,128)S(1)}, u32[]{:S(2)}, u32[]{:S(2)}) collective-permute-start(f32[256,256]{1,0:T(8,128)S(1)} %broadcast_select_fusion.1), channel_id=1, source_target_pairs={{0,8},{1,9},{2,10},{3,11},{4,12},{5,13},{6,14},{7,15},{8,16},{9,17... | collective-permute-start | bytes 786440 | tf_op jit(solution)/shard_map/ppermute | solution.py:23
  11.2 0.0 copy-done.2
  11.2 0.1 fusion.6
  11.2 4.6 %collective-permute-done.items_ref = f32[256,256]{1,0:T(8,128)S(1)} collective-permute-done((f32[256,256]{1,0:T(8,128)S(1)}, f32[256,256]{1,0:T(8,128)S(1)}, u32[]{:S(2)}, u32[]{:S(2)}) %collective-permute-start) | collective-permute-done | bytes 262176 | tf_op jit(solution)/shard_map/ppermute | solution.py:23
  15.8 0.7 %visit.2 = (f32[256,256]{1,0:T(8,128)S(1)}, f32[256,256]{1,0:T(8,128)S(1)}) custom-call(f32[256,256]{1,0:T(8,128)S(1)} %get-tuple-element.22.users_ref, f32[256,256]{1,0:T(8,128)S(1)} %collective-permute-done.items_ref, s32[256,256]{1,0:T(8,128)S(1)} %get-tuple-element.43.tile_ref), custom_call_target="tpu_custom_call" | custom-call | flops 201326592 | bytes 1310720 | tf_op jit(solution)/shard_map/visit/pallas_call | solution.py:113
  16.6 0.1 collective-permute-start.4
  16.6 3.4 %collective-permute-start.1 = (f32[256,256]{1,0:T(8,128)S(1)}, f32[256,256]{1,0:T(8,128)S(1)}, u32[]{:S(2)}, u32[]{:S(2)}) collective-permute-start(f32[256,256]{1,0:T(8,128)S(1)} %collective-permute-done.items_ref), channel_id=1, source_target_pairs={{0,4},{1,5},{2,6},{3,7},{8,12},{9,13},{10,14},{11,15},{16,20},{17,... | collective-permute-start | bytes 786440 | tf_op jit(solution)/shard_map/ppermute | solution.py:23
  20.0 0.3 multiply_subtract_fusion.2
  20.3 2.8 %collective-permute-done.2.ahead_ref = f32[256,256]{1,0:T(8,128)S(1)} collective-permute-done((f32[256,256]{1,0:T(8,128)S(1)}, f32[256,256]{1,0:T(8,128)S(1)}, u32[]{:S(2)}, u32[]{:S(2)}) %collective-permute-start.2) | collective-permute-done | bytes 262176 | tf_op jit(solution)/shard_map/ppermute | solution.py:23
  23.1 0.0 collective-permute-done.3.even_acc_ref
  23.1 3.6 %collective-permute-done.1.passed_ref = f32[256,256]{1,0:T(8,128)S(1)} collective-permute-done((f32[256,256]{1,0:T(8,128)S(1)}, f32[256,256]{1,0:T(8,128)S(1)}, u32[]{:S(2)}, u32[]{:S(2)}) %collective-permute-start.1) | collective-permute-done | bytes 262176 | tf_op jit(solution)/shard_map/ppermute | solution.py:23
  26.7 0.0 collective-permute-done.4.old_grad_ref
  26.7 0.8 %local.1 = (f32[256,256]{1,0:T(8,128)S(1)}, f32[256,256]{1,0:T(8,128)S(1)}, f32[256,256]{1,0:T(8,128)S(1)}, f32[256,256]{1,0:T(8,128)S(1)}) custom-call(s32[1]{0:T(128)} %bitcast.odd_ref, f32[256,256]{1,0:T(8,128)S(1)} %collective-permute-done.1.passed_ref, f32[256,256]{1,0:T(8,128)S(1)} %collective-permute-done.2.ahead_ref, ...), custom_call_target="tpu_custom_call" | custom-call | flops 201326592 | bytes 1310720 | tf_op jit(solution)/shard_map/local/pallas_call | solution.py:113
  27.5 2.5 %collective-permute-start.5 = (f32[256,256]{1,0:T(8,128)S(1)}, f32[256,256]{1,0:T(8,128)S(1)}, u32[]{:S(2)}, u32[]{:S(2)}) collective-permute-start(f32[256,256]{1,0:T(8,128)S(1)} %get-tuple-element.32), channel_id=1, source_target_pairs={{0,4},{1,5},{2,6},{3,7},{4,8},{5,9},{6,10},{7,11},{8,12},{9,13},{1... | collective-permute-start | bytes 786440 | tf_op jit(solution)/shard_map/ppermute | solution.py:23
  30.1 0.3 multiply_subtract_fusion.1
  30.4 1.9 %collective-permute-start.8 = (f32[256,256]{1,0:T(8,128)S(1)}, f32[256,256]{1,0:T(8,128)S(1)}, u32[]{:S(2)}, u32[]{:S(2)}) collective-permute-start(f32[256,256]{1,0:T(8,128)S(1)} %get-tuple-element.31), channel_id=1, source_target_pairs={{0,9},{1,10},{2,11},{3,8},{8,17},{9,18},{10,19},{11,16},{16,25},{1... | collective-permute-start | bytes 786440 | tf_op jit(solution)/shard_map/ppermute | solution.py:23
  32.4 2.0 %collective-permute-start.7 = (f32[256,256]{1,0:T(8,128)S(1)}, f32[256,256]{1,0:T(8,128)S(1)}, u32[]{:S(2)}, u32[]{:S(2)}) collective-permute-start(f32[256,256]{1,0:T(8,128)S(1)} %broadcast_select_fusion), channel_id=1, source_target_pairs={{0,9},{1,10},{2,11},{3,8},{4,13},{5,14},{6,15},{7,12},{8,17},{9,18... | collective-permute-start | bytes 786440 | tf_op jit(solution)/shard_map/ppermute | solution.py:23
  34.3 2.8 %collective-permute-done.5.items_ref = f32[256,256]{1,0:T(8,128)S(1)} collective-permute-done((f32[256,256]{1,0:T(8,128)S(1)}, f32[256,256]{1,0:T(8,128)S(1)}, u32[]{:S(2)}, u32[]{:S(2)}) %collective-permute-start.5) | collective-permute-done | bytes 262176 | tf_op jit(solution)/shard_map/ppermute | solution.py:23
  37.1 0.7 %visit.3 = (f32[256,256]{1,0:T(8,128)S(1)}, f32[256,256]{1,0:T(8,128)S(1)}) custom-call(f32[256,256]{1,0:T(8,128)S(1)} %get-tuple-element.29.users_ref, f32[256,256]{1,0:T(8,128)S(1)} %collective-permute-done.5.items_ref, s32[256,256]{1,0:T(8,128)S(1)} %get-tuple-element.42.tile_ref), custom_call_target="tpu_custom_call" | custom-call | flops 201326592 | bytes 1310720 | tf_op jit(solution)/shard_map/visit/pallas_call | solution.py:113
  37.8 0.1 collective-permute-start.9
  37.9 4.5 %collective-permute-start.6 = (f32[256,256]{1,0:T(8,128)S(1)}, f32[256,256]{1,0:T(8,128)S(1)}, u32[]{:S(2)}, u32[]{:S(2)}) collective-permute-start(f32[256,256]{1,0:T(8,128)S(1)} %collective-permute-done.5.items_ref), channel_id=1, source_target_pairs={{0,5},{1,6},{2,7},{3,4},{8,13},{9,14},{10,15},{11,12},{16,21},{17,... | collective-permute-start | bytes 786440 | tf_op jit(solution)/shard_map/ppermute | solution.py:23
  42.4 1.1 %multiply_subtract_fusion = (f32[256,256]{1,0:T(8,128)}, f32[256,256]{1,0:T(8,128)}) fusion(f32[256,256]{1,0:T(8,128)S(1)} %get-tuple-element.29.users_ref, f32[256,256]{1,0:T(8,128)S(1)} %get-tuple-element.39, f32[256,256]{1,0:T(8,128)S(1)} %get-tuple-element.48, f32[256,256]{1,0:T(8,128)S(1)} %get-tuple-element.30, ...), kind=kOutput, calls=%fused_computation.12 | convolution fusion | flops 101318656 | bytes 1835008 | tf_op jit(solution)/shard_map/dot_general | solution.py:125
  43.5 5.4 %collective-permute-done.7.ahead_ref = f32[256,256]{1,0:T(8,128)S(1)} collective-permute-done((f32[256,256]{1,0:T(8,128)S(1)}, f32[256,256]{1,0:T(8,128)S(1)}, u32[]{:S(2)}, u32[]{:S(2)}) %collective-permute-start.7) | collective-permute-done | bytes 262176 | tf_op jit(solution)/shard_map/ppermute | solution.py:23
  48.9 0.0 collective-permute-done.8.even_acc_ref
  48.9 0.8 %collective-permute-done.9.grad_ref = f32[256,256]{1,0:T(8,128)S(1)} collective-permute-done((f32[256,256]{1,0:T(8,128)S(1)}, f32[256,256]{1,0:T(8,128)S(1)}, u32[]{:S(2)}, u32[]{:S(2)}) %collective-permute-start.9) | collective-permute-done | bytes 262176 | tf_op jit(solution)/shard_map/ppermute | solution.py:23
  49.7 0.0 collective-permute-done.6.passed_ref
  49.7 0.9 %last_update.1 = (f32[256,256]{1,0:T(8,128)}, f32[256,256]{1,0:T(8,128)}) custom-call(s32[1]{0:T(128)} %bitcast.odd_ref, f32[256,256]{1,0:T(8,128)S(1)} %collective-permute-done.6.passed_ref, f32[256,256]{1,0:T(8,128)S(1)} %collective-permute-done.7.ahead_ref, f32[256,256]{1,0:T(8,128)S(1)} %collective-permute-done.8.even_acc_ref, ...), custom_call_target="tpu_custom_call" | custom-call | flops 524288 | bytes 1572864 | tf_op jit(solution)/shard_map/last_update/pallas_call | solution.py:97
  (2 shorter events, 0.1 us)
Async XLA Ops:
  0.6 1.6 %copy-start.1 = (f32[256,256]{1,0:T(8,128)S(1)}, f32[256,256]{1,0:T(8,128)}, u32[]{:S(2)}) copy-start(f32[256,256]{1,0:T(8,128)} %param.7) | copy-start | bytes 786436
  0.6 1.6 %copy-start = (f32[256,256]{1,0:T(8,128)S(1)}, f32[256,256]{1,0:T(8,128)}, u32[]{:S(2)}) copy-start(f32[256,256]{1,0:T(8,128)} %param.5) | copy-start | bytes 786436
  0.7 1.6 %copy-start.4 = (f32[256,256]{1,0:T(8,128)S(1)}, f32[256,256]{1,0:T(8,128)}, u32[]{:S(2)}) copy-start(f32[256,256]{1,0:T(8,128)} %param.8) | copy-start | bytes 786436
  2.2 3.4 %copy-start.3 = (f32[256,256]{1,0:T(8,128)S(1)}, f32[256,256]{1,0:T(8,128)}, u32[]{:S(2)}) copy-start(f32[256,256]{1,0:T(8,128)} %param.6) | copy-start | bytes 786436
  2.7 8.5 %copy-start.2 = (s32[256,1024]{1,0:T(8,128)S(1)}, s32[256,1024]{1,0:T(8,128)}, u32[]{:S(2)}) copy-start(s32[256,1024]{1,0:T(8,128)} %param.9) | copy-start | bytes 3145732
  2.7 13.2 %collective-permute-start = (f32[256,256]{1,0:T(8,128)S(1)}, f32[256,256]{1,0:T(8,128)S(1)}, u32[]{:S(2)}, u32[]{:S(2)}) collective-permute-start(f32[256,256]{1,0:T(8,128)S(1)} %get-tuple-element.21), channel_id=1, source_target_pairs={{0,4},{1,5},{2,6},{3,7},{4,8},{5,9},{6,10},{7,11},{8,12},{9,13},{1... | collective-permute-start | bytes 786440 | tf_op jit(solution)/shard_map/ppermute | solution.py:23
  6.0 17.1 %collective-permute-start.3 = (f32[256,256]{1,0:T(8,128)S(1)}, f32[256,256]{1,0:T(8,128)S(1)}, u32[]{:S(2)}, u32[]{:S(2)}) collective-permute-start(f32[256,256]{1,0:T(8,128)S(1)} %get-tuple-element.20), channel_id=1, source_target_pairs={{0,8},{1,9},{2,10},{3,11},{8,16},{9,17},{10,18},{11,19},{16,24},{1... | collective-permute-start | bytes 786440 | tf_op jit(solution)/shard_map/ppermute | solution.py:23
  9.5 13.6 %collective-permute-start.2 = (f32[256,256]{1,0:T(8,128)S(1)}, f32[256,256]{1,0:T(8,128)S(1)}, u32[]{:S(2)}, u32[]{:S(2)}) collective-permute-start(f32[256,256]{1,0:T(8,128)S(1)} %broadcast_select_fusion.1), channel_id=1, source_target_pairs={{0,8},{1,9},{2,10},{3,11},{4,12},{5,13},{6,14},{7,15},{8,16},{9,17... | collective-permute-start | bytes 786440 | tf_op jit(solution)/shard_map/ppermute | solution.py:23
  16.6 10.1 %collective-permute-start.4 = (f32[256,256]{1,0:T(8,128)S(1)}, f32[256,256]{1,0:T(8,128)S(1)}, u32[]{:S(2)}, u32[]{:S(2)}) collective-permute-start(f32[256,256]{1,0:T(8,128)S(1)} %get-tuple-element.23), channel_id=1, source_target_pairs={{0,4},{1,5},{2,6},{3,7},{4,8},{5,9},{6,10},{7,11},{8,12},{9,13},{1... | collective-permute-start | bytes 786440 | tf_op jit(solution)/shard_map/ppermute | solution.py:23
  16.6 10.1 %collective-permute-start.1 = (f32[256,256]{1,0:T(8,128)S(1)}, f32[256,256]{1,0:T(8,128)S(1)}, u32[]{:S(2)}, u32[]{:S(2)}) collective-permute-start(f32[256,256]{1,0:T(8,128)S(1)} %collective-permute-done.items_ref), channel_id=1, source_target_pairs={{0,4},{1,5},{2,6},{3,7},{8,12},{9,13},{10,14},{11,15},{16,20},{17,... | collective-permute-start | bytes 786440 | tf_op jit(solution)/shard_map/ppermute | solution.py:23
  27.5 9.6 %collective-permute-start.5 = (f32[256,256]{1,0:T(8,128)S(1)}, f32[256,256]{1,0:T(8,128)S(1)}, u32[]{:S(2)}, u32[]{:S(2)}) collective-permute-start(f32[256,256]{1,0:T(8,128)S(1)} %get-tuple-element.32), channel_id=1, source_target_pairs={{0,4},{1,5},{2,6},{3,7},{4,8},{5,9},{6,10},{7,11},{8,12},{9,13},{1... | collective-permute-start | bytes 786440 | tf_op jit(solution)/shard_map/ppermute | solution.py:23
  30.4 18.5 %collective-permute-start.8 = (f32[256,256]{1,0:T(8,128)S(1)}, f32[256,256]{1,0:T(8,128)S(1)}, u32[]{:S(2)}, u32[]{:S(2)}) collective-permute-start(f32[256,256]{1,0:T(8,128)S(1)} %get-tuple-element.31), channel_id=1, source_target_pairs={{0,9},{1,10},{2,11},{3,8},{8,17},{9,18},{10,19},{11,16},{16,25},{1... | collective-permute-start | bytes 786440 | tf_op jit(solution)/shard_map/ppermute | solution.py:23
  32.4 16.6 %collective-permute-start.7 = (f32[256,256]{1,0:T(8,128)S(1)}, f32[256,256]{1,0:T(8,128)S(1)}, u32[]{:S(2)}, u32[]{:S(2)}) collective-permute-start(f32[256,256]{1,0:T(8,128)S(1)} %broadcast_select_fusion), channel_id=1, source_target_pairs={{0,9},{1,10},{2,11},{3,8},{4,13},{5,14},{6,15},{7,12},{8,17},{9,18... | collective-permute-start | bytes 786440 | tf_op jit(solution)/shard_map/ppermute | solution.py:23
  37.8 11.9 %collective-permute-start.9 = (f32[256,256]{1,0:T(8,128)S(1)}, f32[256,256]{1,0:T(8,128)S(1)}, u32[]{:S(2)}, u32[]{:S(2)}) collective-permute-start(f32[256,256]{1,0:T(8,128)S(1)} %get-tuple-element.33), channel_id=1, source_target_pairs={{0,5},{1,6},{2,7},{3,4},{4,9},{5,10},{6,11},{7,8},{8,13},{9,14},{1... | collective-permute-start | bytes 786440 | tf_op jit(solution)/shard_map/ppermute | solution.py:23
  37.9 11.8 %collective-permute-start.6 = (f32[256,256]{1,0:T(8,128)S(1)}, f32[256,256]{1,0:T(8,128)S(1)}, u32[]{:S(2)}, u32[]{:S(2)}) collective-permute-start(f32[256,256]{1,0:T(8,128)S(1)} %collective-permute-done.5.items_ref), channel_id=1, source_target_pairs={{0,5},{1,6},{2,7},{3,4},{8,13},{9,14},{10,15},{11,12},{16,21},{17,... | collective-permute-start | bytes 786440 | tf_op jit(solution)/shard_map/ppermute | solution.py:23

commit v10 on v9

--- a/solution.py
+++ b/solution.py
@@ -21,6 +21,10 @@
             if target is not None:
                 pairs.append((b * n_group + g, target[0] % n_blk * n_group + target[1] % n_group))
     return lax.ppermute(value, ("blk", "group"), pairs)
+
+
+def passes_on(b, g, n_blk, up):
+    return (b % 2 == 1) & ((up == 0) | (g % 2 == 1) | (b % n_blk >= n_blk - 2))
 
 
 def halves(value):
@@ -60,20 +64,20 @@
 
 
 def local_kernel(
-    odd_ref, passed_ref, ahead_ref, even_acc_ref, old_grad_ref, users_ref, tile_ref, items_ref, gap_ref, new_items_ref, new_acc_ref
+    by_visit_ref, passed_ref, ahead_ref, late_ref, old_grad_ref, users_ref, tile_ref, items_ref, gap_ref, new_items_ref, new_acc_ref
 ):
-    odd = odd_ref[0] == 1
+    by_visit = by_visit_ref[0] == 1
     ahead = ahead_ref[...]
     items, acc = adagrad(
-        jnp.where(odd, passed_ref[...], ahead), jnp.where(odd, ahead, even_acc_ref[...]), old_grad_ref[...]
+        jnp.where(by_visit, passed_ref[...], ahead), jnp.where(by_visit, ahead, late_ref[...]), old_grad_ref[...]
     )
     gap, grad = pair_products(users_ref[...], items, tile_ref[...])
     items_ref[...], gap_ref[...] = items, gap
     new_items_ref[...], new_acc_ref[...] = adagrad(items, acc, grad)
 
 
-def last_kernel(odd_ref, passed_ref, ahead_ref, even_acc_ref, grad_ref, items_hbm, acc_hbm, items_ref, acc_ref, done):
-    odd = odd_ref[0] == 1
+def last_kernel(by_visit_ref, passed_ref, ahead_ref, late_ref, grad_ref, items_hbm, acc_hbm, items_ref, acc_ref, done):
+    by_visit = by_visit_ref[0] == 1
     parts = done.shape[0]
     size = grad_ref.shape[0] // parts
     copies = []
@@ -81,7 +85,7 @@
         at = pl.ds(part * size, size)
         ahead = ahead_ref[at, :]
         items_ref[at, :], acc_ref[at, :] = adagrad(
-            jnp.where(odd, passed_ref[at, :], ahead), jnp.where(odd, ahead, even_acc_ref[at, :]), grad_ref[at, :]
+            jnp.where(by_visit, passed_ref[at, :], ahead), jnp.where(by_visit, ahead, late_ref[at, :]), grad_ref[at, :]
         )
         for index, (source, target) in enumerate([(items_ref, items_hbm), (acc_ref, acc_hbm)]):
             copy = pltpu.make_async_copy(source.at[at, :], target.at[at, :], done.at[part, index])
@@ -91,7 +95,7 @@
         copy.wait()
 
 
-def last_update(odd_flag, passed, ahead, even_acc, grad):
+def last_update(by_visit, passed, ahead, late, grad):
     here, there = pl.BlockSpec(memory_space=pltpu.VMEM), pl.BlockSpec(memory_space=pltpu.HBM)
     shape = jax.ShapeDtypeStruct(grad.shape, jnp.float32)
     return pl.pallas_call(
@@ -103,7 +107,7 @@
         compiler_params=pltpu.CompilerParams(vmem_limit_bytes=8 * 2**20),
         cost_estimate=pl.CostEstimate(flops=8 * grad.size, bytes_accessed=24 * grad.size, transcendentals=grad.size),
         name="last_update",
-    )(odd_flag, passed, ahead, even_acc, grad)
+    )(by_visit, passed, ahead, late, grad)
 
 
 def on_vmem(kernel, name, outputs, *operands):
@@ -133,16 +137,17 @@
 def body(users, user_acc, items, item_acc, counts):
     rows = items.shape[0]
     tiles = [counts[:, s * rows : (s + 1) * rows] for s in range(4)]
-    odd = lax.axis_index("blk") % 2 == 1
-    odd_flag = odd.astype(jnp.int32).reshape(1)
+    n_blk, blk, group = lax.axis_size("blk"), lax.axis_index("blk"), lax.axis_index("group")
 
     def send_off(users, items, item_acc, up):
         visitor = sent(items, lambda b, g: (b + 1, g))
         items, item_acc, users = lax.optimization_barrier((items, item_acc, users))
-        ahead = sent(jnp.where(odd, item_acc, items), lambda b, g: (b + 2, g + up))
-        even_acc = sent(item_acc, lambda b, g: (b + 2, g + up) if b % 2 == 0 else None)
-        passed = sent(visitor, lambda b, g: (b + 1, g + up) if b % 2 == 0 else None)
-        return users, visitor, (passed, ahead, even_acc)
+        passing = passes_on(blk, group, n_blk, up)
+        ahead = sent(jnp.where(passing, item_acc, items), lambda b, g: (b + 2, g + up))
+        late = sent(item_acc, lambda b, g: None if passes_on(b, g, n_blk, up) else (b + 2, g + up))
+        passed = sent(visitor, lambda b, g: (b + 1, g + up) if passes_on(b - 1, g, n_blk, up) else None)
+        came_by_visit = passes_on((blk - 2) % n_blk, group - up, n_blk, up)
+        return users, visitor, (came_by_visit.astype(jnp.int32).reshape(1), passed, ahead, late)
 
     def visit(users, user_acc, visitor, tile, up):
         gap, grad = on_vmem(visit_kernel, "visit", 2, users, visitor, tile)
@@ -156,12 +161,12 @@
     users, visitor, state = send_off(users, new_items, new_acc, 0)
     users, user_acc, grad = visit(users, user_acc, visitor, tiles[1], 0)
 
-    items, gap, new_items, new_acc = on_vmem(local_kernel, "local", 4, odd_flag, *state, grad, users, tiles[2])
+    items, gap, new_items, new_acc = on_vmem(local_kernel, "local", 4, *state, grad, users, tiles[2])
     users, user_acc = adagrad(users, user_acc, user_gradient(gap, users, items))
-    users, visitor, (passed, ahead, even_acc) = send_off(users, new_items, new_acc, 1)
+    users, visitor, state = send_off(users, new_items, new_acc, 1)
     users, user_acc, grad = visit(users, user_acc, visitor, tiles[3], 1)
 
-    items, item_acc = last_update(odd_flag, passed, ahead, even_acc, grad)
+    items, item_acc = last_update(*state, grad)
     return users, user_acc, items, item_acc
 
 

time: 50.8 us -> 50.8 us (level)
  transfers between devices with their start and end apart: 10 -> 10, of which waited for: 6 -> 7; matrix products, arithmetic and copies ran while one was open for 4% -> 4% of each run, Pallas kernels for 3% -> 3%
where the time goes in v10:
time: 50.8 us; the launch traced here: 50.6 us
  starting transfers between devices  22.2 us (44%)
  waiting for transfers between devices  20.2 us (40%)
  matrix products  4.01 us (8%)
  Pallas kernels  3.16 us (6%)
  between operations  0.85 us (2%)
    ppermute x10, starting transfers between devices, sent(): return lax.ppermute(value, ('blk', 'group'), pairs)  22.2 us
    ppermute x10, waiting for transfers between devices, sent(): return lax.ppermute(value, ('blk', 'group'), pairs)  20.2 us
    pallas_call x3, Pallas kernels, on_vmem(): pl.pallas_call(kernel, out_shape=[jax.ShapeDtypeStruct(shape, jnp.float32...  2.29 us
    dot_general x4, matrix products, user_gradient(): jnp.dot(gap, items, precision=PREC)  2.08 us
    dot_general x1, matrix products, weighted_gap(): lax.dot_general(users, items, (((1,), (1,)), ((), ())), precision=PREC)  1.52 us
  transfers between devices with their start and end apart: 10, of which 7 were waited for; matrix products, arithmetic and copies ran while one was open for 4% of the time, Pallas kernels for 3%

profile of v10, /device:TPU:0, one launch (start us, length us, event | category | flops | bytes accessed | tf_op | source)
XLA Modules:
  0.0 50.6 jit_solution(2855103408155303260)
XLA Ops:
  0.6 0.0 copy-start.1
  0.6 0.0 copy-start
  0.7 0.0 copy-start.4
  0.7 1.5 %fusion.5 = f32[256,256]{1,0:T(8,128)S(1)} fusion(f32[256,256]{1,0:T(8,128)} %param.5, f32[256,256]{1,0:T(8,128)} %param.7, s32[256,1024]{1,0:T(8,128)} %param.9), kind=kOutput, calls=%fused_computation.11 | convolution fusion | flops 101122048 | bytes 1048576 | tf_op jit(solution)/shard_map/dot_general | solution.py:43
  2.2 0.0 copy-done.1
  2.2 0.0 copy-done
  2.2 0.0 copy-done.4
  2.2 0.0 copy-start.3
  2.2 0.4 multiply_subtract_fusion.4
  2.7 0.0 copy-start.2
  2.7 3.0 %collective-permute-start = (f32[256,256]{1,0:T(8,128)S(1)}, f32[256,256]{1,0:T(8,128)S(1)}, u32[]{:S(2)}, u32[]{:S(2)}) collective-permute-start(f32[256,256]{1,0:T(8,128)S(1)} %get-tuple-element.21), channel_id=1, source_target_pairs={{0,4},{1,5},{2,6},{3,7},{4,8},{5,9},{6,10},{7,11},{8,12},{9,13},{1... | collective-permute-start | bytes 786440 | tf_op jit(solution)/shard_map/ppermute | solution.py:23
  5.7 0.0 copy-done.3
  5.7 0.3 multiply_subtract_fusion.3
  6.0 3.5 %collective-permute-start.3 = (f32[256,256]{1,0:T(8,128)S(1)}, f32[256,256]{1,0:T(8,128)S(1)}, u32[]{:S(2)}, u32[]{:S(2)}) collective-permute-start(f32[256,256]{1,0:T(8,128)S(1)} %get-tuple-element.20), channel_id=1, source_target_pairs={{0,8},{1,9},{2,10},{3,11},{8,16},{9,17},{10,18},{11,19},{16,24},{1... | collective-permute-start | bytes 786440 | tf_op jit(solution)/shard_map/ppermute | solution.py:23
  9.5 1.6 %collective-permute-start.2 = (f32[256,256]{1,0:T(8,128)S(1)}, f32[256,256]{1,0:T(8,128)S(1)}, u32[]{:S(2)}, u32[]{:S(2)}) collective-permute-start(f32[256,256]{1,0:T(8,128)S(1)} %broadcast_select_fusion.1), channel_id=1, source_target_pairs={{0,8},{1,9},{2,10},{3,11},{4,12},{5,13},{6,14},{7,15},{8,16},{9,17... | collective-permute-start | bytes 786440 | tf_op jit(solution)/shard_map/ppermute | solution.py:23
  11.2 0.0 copy-done.2
  11.2 0.1 fusion.6
  11.2 4.6 %collective-permute-done.items_ref = f32[256,256]{1,0:T(8,128)S(1)} collective-permute-done((f32[256,256]{1,0:T(8,128)S(1)}, f32[256,256]{1,0:T(8,128)S(1)}, u32[]{:S(2)}, u32[]{:S(2)}) %collective-permute-start) | collective-permute-done | bytes 262176 | tf_op jit(solution)/shard_map/ppermute | solution.py:23
  15.8 0.7 %visit.2 = (f32[256,256]{1,0:T(8,128)S(1)}, f32[256,256]{1,0:T(8,128)S(1)}) custom-call(f32[256,256]{1,0:T(8,128)S(1)} %get-tuple-element.22.users_ref, f32[256,256]{1,0:T(8,128)S(1)} %collective-permute-done.items_ref, s32[256,256]{1,0:T(8,128)S(1)} %get-tuple-element.43.tile_ref), custom_call_target="tpu_custom_call" | custom-call | flops 201326592 | bytes 1310720 | tf_op jit(solution)/shard_map/visit/pallas_call | solution.py:117
  16.6 0.1 collective-permute-start.4
  16.6 3.4 %collective-permute-start.1 = (f32[256,256]{1,0:T(8,128)S(1)}, f32[256,256]{1,0:T(8,128)S(1)}, u32[]{:S(2)}, u32[]{:S(2)}) collective-permute-start(f32[256,256]{1,0:T(8,128)S(1)} %collective-permute-done.items_ref), channel_id=1, source_target_pairs={{0,4},{1,5},{2,6},{3,7},{8,12},{9,13},{10,14},{11,15},{16,20},{17,... | collective-permute-start | bytes 786440 | tf_op jit(solution)/shard_map/ppermute | solution.py:23
  20.0 0.3 multiply_subtract_fusion.2
  20.3 2.8 %collective-permute-done.2.ahead_ref = f32[256,256]{1,0:T(8,128)S(1)} collective-permute-done((f32[256,256]{1,0:T(8,128)S(1)}, f32[256,256]{1,0:T(8,128)S(1)}, u32[]{:S(2)}, u32[]{:S(2)}) %collective-permute-start.2) | collective-permute-done | bytes 262176 | tf_op jit(solution)/shard_map/ppermute | solution.py:23
  23.1 0.0 collective-permute-done.3.late_ref
  23.1 3.6 %collective-permute-done.1.passed_ref = f32[256,256]{1,0:T(8,128)S(1)} collective-permute-done((f32[256,256]{1,0:T(8,128)S(1)}, f32[256,256]{1,0:T(8,128)S(1)}, u32[]{:S(2)}, u32[]{:S(2)}) %collective-permute-start.1) | collective-permute-done | bytes 262176 | tf_op jit(solution)/shard_map/ppermute | solution.py:23
  26.7 0.0 collective-permute-done.4.old_grad_ref
  26.7 0.8 %local.1 = (f32[256,256]{1,0:T(8,128)S(1)}, f32[256,256]{1,0:T(8,128)S(1)}, f32[256,256]{1,0:T(8,128)S(1)}, f32[256,256]{1,0:T(8,128)S(1)}) custom-call(s32[1]{0:T(128)} %bitcast.by_visit_ref, f32[256,256]{1,0:T(8,128)S(1)} %collective-permute-done.1.passed_ref, f32[256,256]{1,0:T(8,128)S(1)} %collective-permute-done.2.ahead_ref, ...), custom_call_target="tpu_custom_call" | custom-call | flops 201326592 | bytes 1310720 | tf_op jit(solution)/shard_map/local/pallas_call | solution.py:117
  27.5 2.5 %collective-permute-start.5 = (f32[256,256]{1,0:T(8,128)S(1)}, f32[256,256]{1,0:T(8,128)S(1)}, u32[]{:S(2)}, u32[]{:S(2)}) collective-permute-start(f32[256,256]{1,0:T(8,128)S(1)} %get-tuple-element.32), channel_id=1, source_target_pairs={{0,4},{1,5},{2,6},{3,7},{4,8},{5,9},{6,10},{7,11},{8,12},{9,13},{1... | collective-permute-start | bytes 786440 | tf_op jit(solution)/shard_map/ppermute | solution.py:23
  30.1 0.3 multiply_subtract_fusion.1
  30.4 1.9 %collective-permute-start.8 = (f32[256,256]{1,0:T(8,128)S(1)}, f32[256,256]{1,0:T(8,128)S(1)}, u32[]{:S(2)}, u32[]{:S(2)}) collective-permute-start(f32[256,256]{1,0:T(8,128)S(1)} %get-tuple-element.31), channel_id=1, source_target_pairs={{0,9},{1,10},{2,11},{3,8},{4,13},{6,15},{8,17},{9,18},{10,19},{11,... | collective-permute-start | bytes 786440 | tf_op jit(solution)/shard_map/ppermute | solution.py:23
  32.4 2.0 %collective-permute-start.7 = (f32[256,256]{1,0:T(8,128)S(1)}, f32[256,256]{1,0:T(8,128)S(1)}, u32[]{:S(2)}, u32[]{:S(2)}) collective-permute-start(f32[256,256]{1,0:T(8,128)S(1)} %broadcast_select_fusion), channel_id=1, source_target_pairs={{0,9},{1,10},{2,11},{3,8},{4,13},{5,14},{6,15},{7,12},{8,17},{9,18... | collective-permute-start | bytes 786440 | tf_op jit(solution)/shard_map/ppermute | solution.py:23
  34.3 2.3 %collective-permute-done.5.items_ref = f32[256,256]{1,0:T(8,128)S(1)} collective-permute-done((f32[256,256]{1,0:T(8,128)S(1)}, f32[256,256]{1,0:T(8,128)S(1)}, u32[]{:S(2)}, u32[]{:S(2)}) %collective-permute-start.5) | collective-permute-done | bytes 262176 | tf_op jit(solution)/shard_map/ppermute | solution.py:23
  36.6 0.7 %visit.3 = (f32[256,256]{1,0:T(8,128)S(1)}, f32[256,256]{1,0:T(8,128)S(1)}) custom-call(f32[256,256]{1,0:T(8,128)S(1)} %get-tuple-element.29.users_ref, f32[256,256]{1,0:T(8,128)S(1)} %collective-permute-done.5.items_ref, s32[256,256]{1,0:T(8,128)S(1)} %get-tuple-element.42.tile_ref), custom_call_target="tpu_custom_call" | custom-call | flops 201326592 | bytes 1310720 | tf_op jit(solution)/shard_map/visit/pallas_call | solution.py:117
  37.4 0.1 collective-permute-start.9
  37.5 4.2 %collective-permute-start.6 = (f32[256,256]{1,0:T(8,128)S(1)}, f32[256,256]{1,0:T(8,128)S(1)}, u32[]{:S(2)}, u32[]{:S(2)}) collective-permute-start(f32[256,256]{1,0:T(8,128)S(1)} %collective-permute-done.5.items_ref), channel_id=1, source_target_pairs={{0,5},{1,6},{2,7},{3,4},{9,14},{11,12},{17,22},{19,20},{25,30},{27... | collective-permute-start | bytes 786440 | tf_op jit(solution)/shard_map/ppermute | solution.py:23
  41.7 1.1 %multiply_subtract_fusion = (f32[256,256]{1,0:T(8,128)}, f32[256,256]{1,0:T(8,128)}) fusion(f32[256,256]{1,0:T(8,128)S(1)} %get-tuple-element.29.users_ref, f32[256,256]{1,0:T(8,128)S(1)} %get-tuple-element.39, f32[256,256]{1,0:T(8,128)S(1)} %get-tuple-element.48, f32[256,256]{1,0:T(8,128)S(1)} %get-tuple-element.30, ...), kind=kOutput, calls=%fused_computation.12 | convolution fusion | flops 101318656 | bytes 1835008 | tf_op jit(solution)/shard_map/dot_general | solution.py:129
  42.8 5.9 %collective-permute-done.7.ahead_ref = f32[256,256]{1,0:T(8,128)S(1)} collective-permute-done((f32[256,256]{1,0:T(8,128)S(1)}, f32[256,256]{1,0:T(8,128)S(1)}, u32[]{:S(2)}, u32[]{:S(2)}) %collective-permute-start.7) | collective-permute-done | bytes 262176 | tf_op jit(solution)/shard_map/ppermute | solution.py:23
  48.7 0.0 collective-permute-done.8.late_ref
  48.7 0.8 %collective-permute-done.9.grad_ref = f32[256,256]{1,0:T(8,128)S(1)} collective-permute-done((f32[256,256]{1,0:T(8,128)S(1)}, f32[256,256]{1,0:T(8,128)S(1)}, u32[]{:S(2)}, u32[]{:S(2)}) %collective-permute-start.9) | collective-permute-done | bytes 262176 | tf_op jit(solution)/shard_map/ppermute | solution.py:23
  49.5 0.3 collective-permute-done.6.passed_ref
  49.7 0.9 %last_update.1 = (f32[256,256]{1,0:T(8,128)}, f32[256,256]{1,0:T(8,128)}) custom-call(s32[1]{0:T(128)} %bitcast.1.by_visit_ref, f32[256,256]{1,0:T(8,128)S(1)} %collective-permute-done.6.passed_ref, f32[256,256]{1,0:T(8,128)S(1)} %collective-permute-done.7.ahead_ref, f32[256,256]{1,0:T(8,128)S(1)} %collective-permute-done.8.late_ref, ...), custom_call_target="tpu_custom_call" | custom-call | flops 524288 | bytes 1572864 | tf_op jit(solution)/shard_map/last_update/pallas_call | solution.py:101
  (2 shorter events, 0.1 us)
Async XLA Ops:
  0.6 1.6 %copy-start.1 = (f32[256,256]{1,0:T(8,128)S(1)}, f32[256,256]{1,0:T(8,128)}, u32[]{:S(2)}) copy-start(f32[256,256]{1,0:T(8,128)} %param.7) | copy-start | bytes 786436
  0.6 1.6 %copy-start = (f32[256,256]{1,0:T(8,128)S(1)}, f32[256,256]{1,0:T(8,128)}, u32[]{:S(2)}) copy-start(f32[256,256]{1,0:T(8,128)} %param.5) | copy-start | bytes 786436
  0.7 1.6 %copy-start.4 = (f32[256,256]{1,0:T(8,128)S(1)}, f32[256,256]{1,0:T(8,128)}, u32[]{:S(2)}) copy-start(f32[256,256]{1,0:T(8,128)} %param.8) | copy-start | bytes 786436
  2.2 3.4 %copy-start.3 = (f32[256,256]{1,0:T(8,128)S(1)}, f32[256,256]{1,0:T(8,128)}, u32[]{:S(2)}) copy-start(f32[256,256]{1,0:T(8,128)} %param.6) | copy-start | bytes 786436
  2.7 8.5 %copy-start.2 = (s32[256,1024]{1,0:T(8,128)S(1)}, s32[256,1024]{1,0:T(8,128)}, u32[]{:S(2)}) copy-start(s32[256,1024]{1,0:T(8,128)} %param.9) | copy-start | bytes 3145732
  2.7 13.2 %collective-permute-start = (f32[256,256]{1,0:T(8,128)S(1)}, f32[256,256]{1,0:T(8,128)S(1)}, u32[]{:S(2)}, u32[]{:S(2)}) collective-permute-start(f32[256,256]{1,0:T(8,128)S(1)} %get-tuple-element.21), channel_id=1, source_target_pairs={{0,4},{1,5},{2,6},{3,7},{4,8},{5,9},{6,10},{7,11},{8,12},{9,13},{1... | collective-permute-start | bytes 786440 | tf_op jit(solution)/shard_map/ppermute | solution.py:23
  6.0 17.1 %collective-permute-start.3 = (f32[256,256]{1,0:T(8,128)S(1)}, f32[256,256]{1,0:T(8,128)S(1)}, u32[]{:S(2)}, u32[]{:S(2)}) collective-permute-start(f32[256,256]{1,0:T(8,128)S(1)} %get-tuple-element.20), channel_id=1, source_target_pairs={{0,8},{1,9},{2,10},{3,11},{8,16},{9,17},{10,18},{11,19},{16,24},{1... | collective-permute-start | bytes 786440 | tf_op jit(solution)/shard_map/ppermute | solution.py:23
  9.5 13.6 %collective-permute-start.2 = (f32[256,256]{1,0:T(8,128)S(1)}, f32[256,256]{1,0:T(8,128)S(1)}, u32[]{:S(2)}, u32[]{:S(2)}) collective-permute-start(f32[256,256]{1,0:T(8,128)S(1)} %broadcast_select_fusion.1), channel_id=1, source_target_pairs={{0,8},{1,9},{2,10},{3,11},{4,12},{5,13},{6,14},{7,15},{8,16},{9,17... | collective-permute-start | bytes 786440 | tf_op jit(solution)/shard_map/ppermute | solution.py:23
  16.6 10.1 %collective-permute-start.4 = (f32[256,256]{1,0:T(8,128)S(1)}, f32[256,256]{1,0:T(8,128)S(1)}, u32[]{:S(2)}, u32[]{:S(2)}) collective-permute-start(f32[256,256]{1,0:T(8,128)S(1)} %get-tuple-element.23), channel_id=1, source_target_pairs={{0,4},{1,5},{2,6},{3,7},{4,8},{5,9},{6,10},{7,11},{8,12},{9,13},{1... | collective-permute-start | bytes 786440 | tf_op jit(solution)/shard_map/ppermute | solution.py:23
  16.6 10.1 %collective-permute-start.1 = (f32[256,256]{1,0:T(8,128)S(1)}, f32[256,256]{1,0:T(8,128)S(1)}, u32[]{:S(2)}, u32[]{:S(2)}) collective-permute-start(f32[256,256]{1,0:T(8,128)S(1)} %collective-permute-done.items_ref), channel_id=1, source_target_pairs={{0,4},{1,5},{2,6},{3,7},{8,12},{9,13},{10,14},{11,15},{16,20},{17,... | collective-permute-start | bytes 786440 | tf_op jit(solution)/shard_map/ppermute | solution.py:23
  27.5 9.1 %collective-permute-start.5 = (f32[256,256]{1,0:T(8,128)S(1)}, f32[256,256]{1,0:T(8,128)S(1)}, u32[]{:S(2)}, u32[]{:S(2)}) collective-permute-start(f32[256,256]{1,0:T(8,128)S(1)} %get-tuple-element.32), channel_id=1, source_target_pairs={{0,4},{1,5},{2,6},{3,7},{4,8},{5,9},{6,10},{7,11},{8,12},{9,13},{1... | collective-permute-start | bytes 786440 | tf_op jit(solution)/shard_map/ppermute | solution.py:23
  30.4 18.3 %collective-permute-start.8 = (f32[256,256]{1,0:T(8,128)S(1)}, f32[256,256]{1,0:T(8,128)S(1)}, u32[]{:S(2)}, u32[]{:S(2)}) collective-permute-start(f32[256,256]{1,0:T(8,128)S(1)} %get-tuple-element.31), channel_id=1, source_target_pairs={{0,9},{1,10},{2,11},{3,8},{4,13},{6,15},{8,17},{9,18},{10,19},{11,... | collective-permute-start | bytes 786440 | tf_op jit(solution)/shard_map/ppermute | solution.py:23
  32.4 16.3 %collective-permute-start.7 = (f32[256,256]{1,0:T(8,128)S(1)}, f32[256,256]{1,0:T(8,128)S(1)}, u32[]{:S(2)}, u32[]{:S(2)}) collective-permute-start(f32[256,256]{1,0:T(8,128)S(1)} %broadcast_select_fusion), channel_id=1, source_target_pairs={{0,9},{1,10},{2,11},{3,8},{4,13},{5,14},{6,15},{7,12},{8,17},{9,18... | collective-permute-start | bytes 786440 | tf_op jit(solution)/shard_map/ppermute | solution.py:23
  37.4 12.1 %collective-permute-start.9 = (f32[256,256]{1,0:T(8,128)S(1)}, f32[256,256]{1,0:T(8,128)S(1)}, u32[]{:S(2)}, u32[]{:S(2)}) collective-permute-start(f32[256,256]{1,0:T(8,128)S(1)} %get-tuple-element.33), channel_id=1, source_target_pairs={{0,5},{1,6},{2,7},{3,4},{4,9},{5,10},{6,11},{7,8},{8,13},{9,14},{1... | collective-permute-start | bytes 786440 | tf_op jit(solution)/shard_map/ppermute | solution.py:23
  37.5 12.3 %collective-permute-start.6 = (f32[256,256]{1,0:T(8,128)S(1)}, f32[256,256]{1,0:T(8,128)S(1)}, u32[]{:S(2)}, u32[]{:S(2)}) collective-permute-start(f32[256,256]{1,0:T(8,128)S(1)} %collective-permute-done.5.items_ref), channel_id=1, source_target_pairs={{0,5},{1,6},{2,7},{3,4},{9,14},{11,12},{17,22},{19,20},{25,30},{27... | collective-permute-start | bytes 786440 | tf_op jit(solution)/shard_map/ppermute | solution.py:23

commit v11 on v10

--- a/solution.py
+++ b/solution.py
@@ -23,8 +23,8 @@
     return lax.ppermute(value, ("blk", "group"), pairs)
 
 
-def passes_on(b, g, n_blk, up):
-    return (b % 2 == 1) & ((up == 0) | (g % 2 == 1) | (b % n_blk >= n_blk - 2))
+def passes_on(b, g, up):
+    return (b % 2 == 1) & ((up == 0) | (g % 2 == 1))
 
 
 def halves(value):
@@ -137,16 +137,16 @@
 def body(users, user_acc, items, item_acc, counts):
     rows = items.shape[0]
     tiles = [counts[:, s * rows : (s + 1) * rows] for s in range(4)]
-    n_blk, blk, group = lax.axis_size("blk"), lax.axis_index("blk"), lax.axis_index("group")
+    blk, group = lax.axis_index("blk"), lax.axis_index("group")
 
     def send_off(users, items, item_acc, up):
         visitor = sent(items, lambda b, g: (b + 1, g))
         items, item_acc, users = lax.optimization_barrier((items, item_acc, users))
-        passing = passes_on(blk, group, n_blk, up)
+        passing = passes_on(blk, group, up)
         ahead = sent(jnp.where(passing, item_acc, items), lambda b, g: (b + 2, g + up))
-        late = sent(item_acc, lambda b, g: None if passes_on(b, g, n_blk, up) else (b + 2, g + up))
-        passed = sent(visitor, lambda b, g: (b + 1, g + up) if passes_on(b - 1, g, n_blk, up) else None)
-        came_by_visit = passes_on((blk - 2) % n_blk, group - up, n_blk, up)
+        late = sent(item_acc, lambda b, g: None if passes_on(b, g, up) else (b + 2, g + up))
+        passed = sent(visitor, lambda b, g: (b + 1, g + up) if passes_on(b - 1, g, up) else None)
+        came_by_visit = passes_on(blk, group - up, up)
         return users, visitor, (came_by_visit.astype(jnp.int32).reshape(1), passed, ahead, late)
 
     def visit(users, user_acc, visitor, tile, up):

time: 50.8 us -> 51.2 us (level)
  starting transfers between devices: 22.2 us -> 18.7 us
  waiting for transfers between devices: 20.2 us -> 23.7 us
    ppermute x10, starting transfers between devices: 22.2 us -> 18.7 us  [sent(): return lax.ppermute(value, ('blk', 'group'), pairs)]
    ppermute x10, waiting for transfers between devices: 20.2 us -> 23.7 us  [sent(): return lax.ppermute(value, ('blk', 'group'), pairs)]
  transfers between devices with their start and end apart: 10 -> 10, of which waited for: 7 -> 6; matrix products, arithmetic and copies ran while one was open for 4% -> 4% of each run, Pallas kernels for 3% -> 3%
where the time goes in v11:
time: 51.2 us; the launch traced here: 50.6 us
  waiting for transfers between devices  23.7 us (46%)
  starting transfers between devices  18.7 us (37%)
  matrix products  4.01 us (8%)
  Pallas kernels  3.16 us (6%)
  between operations  0.84 us (2%)
    ppermute x10, waiting for transfers between devices, sent(): return lax.ppermute(value, ('blk', 'group'), pairs)  23.7 us
    ppermute x10, starting transfers between devices, sent(): return lax.ppermute(value, ('blk', 'group'), pairs)  18.7 us
    pallas_call x3, Pallas kernels, on_vmem(): pl.pallas_call(kernel, out_shape=[jax.ShapeDtypeStruct(shape, jnp.float32...  2.29 us
    dot_general x4, matrix products, user_gradient(): jnp.dot(gap, items, precision=PREC)  2.08 us
    dot_general x1, matrix products, weighted_gap(): lax.dot_general(users, items, (((1,), (1,)), ((), ())), precision=PREC)  1.52 us
  transfers between devices with their start and end apart: 10, of which 6 were waited for; matrix products, arithmetic and copies ran while one was open for 4% of the time, Pallas kernels for 3%

profile of v11, /device:TPU:0, one launch (start us, length us, event | category | flops | bytes accessed | tf_op | source)
XLA Modules:
  0.0 50.6 jit_solution(14576842514906480802)
XLA Ops:
  0.6 0.0 copy-start.1
  0.6 0.0 copy-start
  0.7 0.0 copy-start.4
  0.7 1.5 %fusion.5 = f32[256,256]{1,0:T(8,128)S(1)} fusion(f32[256,256]{1,0:T(8,128)} %param.5, f32[256,256]{1,0:T(8,128)} %param.7, s32[256,1024]{1,0:T(8,128)} %param.9), kind=kOutput, calls=%fused_computation.11 | convolution fusion | flops 101122048 | bytes 1048576 | tf_op jit(solution)/shard_map/dot_general | solution.py:43
  2.2 0.0 copy-done.1
  2.2 0.0 copy-done
  2.2 0.0 copy-done.4
  2.2 0.0 copy-start.3
  2.2 0.4 multiply_subtract_fusion.4
  2.7 0.0 copy-start.2
  2.7 3.0 %collective-permute-start = (f32[256,256]{1,0:T(8,128)S(1)}, f32[256,256]{1,0:T(8,128)S(1)}, u32[]{:S(2)}, u32[]{:S(2)}) collective-permute-start(f32[256,256]{1,0:T(8,128)S(1)} %get-tuple-element.21), channel_id=1, source_target_pairs={{0,4},{1,5},{2,6},{3,7},{4,8},{5,9},{6,10},{7,11},{8,12},{9,13},{1... | collective-permute-start | bytes 786440 | tf_op jit(solution)/shard_map/ppermute | solution.py:23
  5.7 0.0 copy-done.3
  5.7 0.3 multiply_subtract_fusion.3
  6.0 3.5 %collective-permute-start.3 = (f32[256,256]{1,0:T(8,128)S(1)}, f32[256,256]{1,0:T(8,128)S(1)}, u32[]{:S(2)}, u32[]{:S(2)}) collective-permute-start(f32[256,256]{1,0:T(8,128)S(1)} %get-tuple-element.20), channel_id=1, source_target_pairs={{0,8},{1,9},{2,10},{3,11},{8,16},{9,17},{10,18},{11,19},{16,24},{1... | collective-permute-start | bytes 786440 | tf_op jit(solution)/shard_map/ppermute | solution.py:23
  9.5 1.6 %collective-permute-start.2 = (f32[256,256]{1,0:T(8,128)S(1)}, f32[256,256]{1,0:T(8,128)S(1)}, u32[]{:S(2)}, u32[]{:S(2)}) collective-permute-start(f32[256,256]{1,0:T(8,128)S(1)} %broadcast_select_fusion.1), channel_id=1, source_target_pairs={{0,8},{1,9},{2,10},{3,11},{4,12},{5,13},{6,14},{7,15},{8,16},{9,17... | collective-permute-start | bytes 786440 | tf_op jit(solution)/shard_map/ppermute | solution.py:23
  11.2 0.0 copy-done.2
  11.2 0.1 fusion.6
  11.2 4.6 %collective-permute-done.items_ref = f32[256,256]{1,0:T(8,128)S(1)} collective-permute-done((f32[256,256]{1,0:T(8,128)S(1)}, f32[256,256]{1,0:T(8,128)S(1)}, u32[]{:S(2)}, u32[]{:S(2)}) %collective-permute-start) | collective-permute-done | bytes 262176 | tf_op jit(solution)/shard_map/ppermute | solution.py:23
  15.8 0.7 %visit.2 = (f32[256,256]{1,0:T(8,128)S(1)}, f32[256,256]{1,0:T(8,128)S(1)}) custom-call(f32[256,256]{1,0:T(8,128)S(1)} %get-tuple-element.22.users_ref, f32[256,256]{1,0:T(8,128)S(1)} %collective-permute-done.items_ref, s32[256,256]{1,0:T(8,128)S(1)} %get-tuple-element.43.tile_ref), custom_call_target="tpu_custom_call" | custom-call | flops 201326592 | bytes 1310720 | tf_op jit(solution)/shard_map/visit/pallas_call | solution.py:117
  16.6 0.1 collective-permute-start.4
  16.6 3.4 %collective-permute-start.1 = (f32[256,256]{1,0:T(8,128)S(1)}, f32[256,256]{1,0:T(8,128)S(1)}, u32[]{:S(2)}, u32[]{:S(2)}) collective-permute-start(f32[256,256]{1,0:T(8,128)S(1)} %collective-permute-done.items_ref), channel_id=1, source_target_pairs={{0,4},{1,5},{2,6},{3,7},{8,12},{9,13},{10,14},{11,15},{16,20},{17,... | collective-permute-start | bytes 786440 | tf_op jit(solution)/shard_map/ppermute | solution.py:23
  20.0 0.3 multiply_subtract_fusion.2
  20.3 2.8 %collective-permute-done.2.ahead_ref = f32[256,256]{1,0:T(8,128)S(1)} collective-permute-done((f32[256,256]{1,0:T(8,128)S(1)}, f32[256,256]{1,0:T(8,128)S(1)}, u32[]{:S(2)}, u32[]{:S(2)}) %collective-permute-start.2) | collective-permute-done | bytes 262176 | tf_op jit(solution)/shard_map/ppermute | solution.py:23
  23.1 0.0 collective-permute-done.3.late_ref
  23.1 3.6 %collective-permute-done.1.passed_ref = f32[256,256]{1,0:T(8,128)S(1)} collective-permute-done((f32[256,256]{1,0:T(8,128)S(1)}, f32[256,256]{1,0:T(8,128)S(1)}, u32[]{:S(2)}, u32[]{:S(2)}) %collective-permute-start.1) | collective-permute-done | bytes 262176 | tf_op jit(solution)/shard_map/ppermute | solution.py:23
  26.7 0.0 collective-permute-done.4.old_grad_ref
  26.7 0.8 %local.1 = (f32[256,256]{1,0:T(8,128)S(1)}, f32[256,256]{1,0:T(8,128)S(1)}, f32[256,256]{1,0:T(8,128)S(1)}, f32[256,256]{1,0:T(8,128)S(1)}) custom-call(s32[1]{0:T(128)} %bitcast.by_visit_ref, f32[256,256]{1,0:T(8,128)S(1)} %collective-permute-done.1.passed_ref, f32[256,256]{1,0:T(8,128)S(1)} %collective-permute-done.2.ahead_ref, ...), custom_call_target="tpu_custom_call" | custom-call | flops 201326592 | bytes 1310720 | tf_op jit(solution)/shard_map/local/pallas_call | solution.py:117
  27.5 2.5 %collective-permute-start.5 = (f32[256,256]{1,0:T(8,128)S(1)}, f32[256,256]{1,0:T(8,128)S(1)}, u32[]{:S(2)}, u32[]{:S(2)}) collective-permute-start(f32[256,256]{1,0:T(8,128)S(1)} %get-tuple-element.32), channel_id=1, source_target_pairs={{0,4},{1,5},{2,6},{3,7},{4,8},{5,9},{6,10},{7,11},{8,12},{9,13},{1... | collective-permute-start | bytes 786440 | tf_op jit(solution)/shard_map/ppermute | solution.py:23
  30.1 0.3 multiply_subtract_fusion.1
  30.4 1.9 %collective-permute-start.8 = (f32[256,256]{1,0:T(8,128)S(1)}, f32[256,256]{1,0:T(8,128)S(1)}, u32[]{:S(2)}, u32[]{:S(2)}) collective-permute-start(f32[256,256]{1,0:T(8,128)S(1)} %get-tuple-element.31), channel_id=1, source_target_pairs={{0,9},{1,10},{2,11},{3,8},{4,13},{6,15},{8,17},{9,18},{10,19},{11,... | collective-permute-start | bytes 786440 | tf_op jit(solution)/shard_map/ppermute | solution.py:23
  32.4 2.0 %collective-permute-start.7 = (f32[256,256]{1,0:T(8,128)S(1)}, f32[256,256]{1,0:T(8,128)S(1)}, u32[]{:S(2)}, u32[]{:S(2)}) collective-permute-start(f32[256,256]{1,0:T(8,128)S(1)} %broadcast_select_fusion), channel_id=1, source_target_pairs={{0,9},{1,10},{2,11},{3,8},{4,13},{5,14},{6,15},{7,12},{8,17},{9,18... | collective-permute-start | bytes 786440 | tf_op jit(solution)/shard_map/ppermute | solution.py:23
  34.3 2.3 %collective-permute-done.5.items_ref = f32[256,256]{1,0:T(8,128)S(1)} collective-permute-done((f32[256,256]{1,0:T(8,128)S(1)}, f32[256,256]{1,0:T(8,128)S(1)}, u32[]{:S(2)}, u32[]{:S(2)}) %collective-permute-start.5) | collective-permute-done | bytes 262176 | tf_op jit(solution)/shard_map/ppermute | solution.py:23
  36.6 0.7 %visit.3 = (f32[256,256]{1,0:T(8,128)S(1)}, f32[256,256]{1,0:T(8,128)S(1)}) custom-call(f32[256,256]{1,0:T(8,128)S(1)} %get-tuple-element.29.users_ref, f32[256,256]{1,0:T(8,128)S(1)} %collective-permute-done.5.items_ref, s32[256,256]{1,0:T(8,128)S(1)} %get-tuple-element.42.tile_ref), custom_call_target="tpu_custom_call" | custom-call | flops 201326592 | bytes 1310720 | tf_op jit(solution)/shard_map/visit/pallas_call | solution.py:117
  37.4 0.1 collective-permute-start.9
  37.5 0.7 %collective-permute-start.6 = (f32[256,256]{1,0:T(8,128)S(1)}, f32[256,256]{1,0:T(8,128)S(1)}, u32[]{:S(2)}, u32[]{:S(2)}) collective-permute-start(f32[256,256]{1,0:T(8,128)S(1)} %collective-permute-done.5.items_ref), channel_id=1, source_target_pairs={{1,6},{3,4},{9,14},{11,12},{17,22},{19,20},{25,30},{27,28}} | collective-permute-start | bytes 786440 | tf_op jit(solution)/shard_map/ppermute | solution.py:23
  38.2 1.1 %multiply_subtract_fusion = (f32[256,256]{1,0:T(8,128)}, f32[256,256]{1,0:T(8,128)}) fusion(f32[256,256]{1,0:T(8,128)S(1)} %get-tuple-element.29.users_ref, f32[256,256]{1,0:T(8,128)S(1)} %get-tuple-element.39, f32[256,256]{1,0:T(8,128)S(1)} %get-tuple-element.48, f32[256,256]{1,0:T(8,128)S(1)} %get-tuple-element.30, ...), kind=kOutput, calls=%fused_computation.12 | convolution fusion | flops 101318656 | bytes 1835008 | tf_op jit(solution)/shard_map/dot_general | solution.py:129
  39.3 9.3 %collective-permute-done.7.ahead_ref = f32[256,256]{1,0:T(8,128)S(1)} collective-permute-done((f32[256,256]{1,0:T(8,128)S(1)}, f32[256,256]{1,0:T(8,128)S(1)}, u32[]{:S(2)}, u32[]{:S(2)}) %collective-permute-start.7) | collective-permute-done | bytes 262176 | tf_op jit(solution)/shard_map/ppermute | solution.py:23
  48.5 0.0 collective-permute-done.8.late_ref
  48.6 1.2 %collective-permute-done.9.grad_ref = f32[256,256]{1,0:T(8,128)S(1)} collective-permute-done((f32[256,256]{1,0:T(8,128)S(1)}, f32[256,256]{1,0:T(8,128)S(1)}, u32[]{:S(2)}, u32[]{:S(2)}) %collective-permute-start.9) | collective-permute-done | bytes 262176 | tf_op jit(solution)/shard_map/ppermute | solution.py:23
  49.7 0.0 collective-permute-done.6.passed_ref
  49.7 0.9 %last_update.1 = (f32[256,256]{1,0:T(8,128)}, f32[256,256]{1,0:T(8,128)}) custom-call(s32[1]{0:T(128)} %bitcast.1.by_visit_ref, f32[256,256]{1,0:T(8,128)S(1)} %collective-permute-done.6.passed_ref, f32[256,256]{1,0:T(8,128)S(1)} %collective-permute-done.7.ahead_ref, f32[256,256]{1,0:T(8,128)S(1)} %collective-permute-done.8.late_ref, ...), custom_call_target="tpu_custom_call" | custom-call | flops 524288 | bytes 1572864 | tf_op jit(solution)/shard_map/last_update/pallas_call | solution.py:101
  (2 shorter events, 0.1 us)
Async XLA Ops:
  0.6 1.6 %copy-start.1 = (f32[256,256]{1,0:T(8,128)S(1)}, f32[256,256]{1,0:T(8,128)}, u32[]{:S(2)}) copy-start(f32[256,256]{1,0:T(8,128)} %param.7) | copy-start | bytes 786436
  0.6 1.6 %copy-start = (f32[256,256]{1,0:T(8,128)S(1)}, f32[256,256]{1,0:T(8,128)}, u32[]{:S(2)}) copy-start(f32[256,256]{1,0:T(8,128)} %param.5) | copy-start | bytes 786436
  0.7 1.6 %copy-start.4 = (f32[256,256]{1,0:T(8,128)S(1)}, f32[256,256]{1,0:T(8,128)}, u32[]{:S(2)}) copy-start(f32[256,256]{1,0:T(8,128)} %param.8) | copy-start | bytes 786436
  2.2 3.4 %copy-start.3 = (f32[256,256]{1,0:T(8,128)S(1)}, f32[256,256]{1,0:T(8,128)}, u32[]{:S(2)}) copy-start(f32[256,256]{1,0:T(8,128)} %param.6) | copy-start | bytes 786436
  2.7 8.5 %copy-start.2 = (s32[256,1024]{1,0:T(8,128)S(1)}, s32[256,1024]{1,0:T(8,128)}, u32[]{:S(2)}) copy-start(s32[256,1024]{1,0:T(8,128)} %param.9) | copy-start | bytes 3145732
  2.7 13.2 %collective-permute-start = (f32[256,256]{1,0:T(8,128)S(1)}, f32[256,256]{1,0:T(8,128)S(1)}, u32[]{:S(2)}, u32[]{:S(2)}) collective-permute-start(f32[256,256]{1,0:T(8,128)S(1)} %get-tuple-element.21), channel_id=1, source_target_pairs={{0,4},{1,5},{2,6},{3,7},{4,8},{5,9},{6,10},{7,11},{8,12},{9,13},{1... | collective-permute-start | bytes 786440 | tf_op jit(solution)/shard_map/ppermute | solution.py:23
  6.0 17.1 %collective-permute-start.3 = (f32[256,256]{1,0:T(8,128)S(1)}, f32[256,256]{1,0:T(8,128)S(1)}, u32[]{:S(2)}, u32[]{:S(2)}) collective-permute-start(f32[256,256]{1,0:T(8,128)S(1)} %get-tuple-element.20), channel_id=1, source_target_pairs={{0,8},{1,9},{2,10},{3,11},{8,16},{9,17},{10,18},{11,19},{16,24},{1... | collective-permute-start | bytes 786440 | tf_op jit(solution)/shard_map/ppermute | solution.py:23
  9.5 13.6 %collective-permute-start.2 = (f32[256,256]{1,0:T(8,128)S(1)}, f32[256,256]{1,0:T(8,128)S(1)}, u32[]{:S(2)}, u32[]{:S(2)}) collective-permute-start(f32[256,256]{1,0:T(8,128)S(1)} %broadcast_select_fusion.1), channel_id=1, source_target_pairs={{0,8},{1,9},{2,10},{3,11},{4,12},{5,13},{6,14},{7,15},{8,16},{9,17... | collective-permute-start | bytes 786440 | tf_op jit(solution)/shard_map/ppermute | solution.py:23
  16.6 10.1 %collective-permute-start.4 = (f32[256,256]{1,0:T(8,128)S(1)}, f32[256,256]{1,0:T(8,128)S(1)}, u32[]{:S(2)}, u32[]{:S(2)}) collective-permute-start(f32[256,256]{1,0:T(8,128)S(1)} %get-tuple-element.23), channel_id=1, source_target_pairs={{0,4},{1,5},{2,6},{3,7},{4,8},{5,9},{6,10},{7,11},{8,12},{9,13},{1... | collective-permute-start | bytes 786440 | tf_op jit(solution)/shard_map/ppermute | solution.py:23
  16.6 10.1 %collective-permute-start.1 = (f32[256,256]{1,0:T(8,128)S(1)}, f32[256,256]{1,0:T(8,128)S(1)}, u32[]{:S(2)}, u32[]{:S(2)}) collective-permute-start(f32[256,256]{1,0:T(8,128)S(1)} %collective-permute-done.items_ref), channel_id=1, source_target_pairs={{0,4},{1,5},{2,6},{3,7},{8,12},{9,13},{10,14},{11,15},{16,20},{17,... | collective-permute-start | bytes 786440 | tf_op jit(solution)/shard_map/ppermute | solution.py:23
  27.5 9.1 %collective-permute-start.5 = (f32[256,256]{1,0:T(8,128)S(1)}, f32[256,256]{1,0:T(8,128)S(1)}, u32[]{:S(2)}, u32[]{:S(2)}) collective-permute-start(f32[256,256]{1,0:T(8,128)S(1)} %get-tuple-element.32), channel_id=1, source_target_pairs={{0,4},{1,5},{2,6},{3,7},{4,8},{5,9},{6,10},{7,11},{8,12},{9,13},{1... | collective-permute-start | bytes 786440 | tf_op jit(solution)/shard_map/ppermute | solution.py:23
  30.4 18.2 %collective-permute-start.8 = (f32[256,256]{1,0:T(8,128)S(1)}, f32[256,256]{1,0:T(8,128)S(1)}, u32[]{:S(2)}, u32[]{:S(2)}) collective-permute-start(f32[256,256]{1,0:T(8,128)S(1)} %get-tuple-element.31), channel_id=1, source_target_pairs={{0,9},{1,10},{2,11},{3,8},{4,13},{6,15},{8,17},{9,18},{10,19},{11,... | collective-permute-start | bytes 786440 | tf_op jit(solution)/shard_map/ppermute | solution.py:23
  32.4 16.2 %collective-permute-start.7 = (f32[256,256]{1,0:T(8,128)S(1)}, f32[256,256]{1,0:T(8,128)S(1)}, u32[]{:S(2)}, u32[]{:S(2)}) collective-permute-start(f32[256,256]{1,0:T(8,128)S(1)} %broadcast_select_fusion), channel_id=1, source_target_pairs={{0,9},{1,10},{2,11},{3,8},{4,13},{5,14},{6,15},{7,12},{8,17},{9,18... | collective-permute-start | bytes 786440 | tf_op jit(solution)/shard_map/ppermute | solution.py:23
  37.4 12.3 %collective-permute-start.9 = (f32[256,256]{1,0:T(8,128)S(1)}, f32[256,256]{1,0:T(8,128)S(1)}, u32[]{:S(2)}, u32[]{:S(2)}) collective-permute-start(f32[256,256]{1,0:T(8,128)S(1)} %get-tuple-element.33), channel_id=1, source_target_pairs={{0,5},{1,6},{2,7},{3,4},{4,9},{5,10},{6,11},{7,8},{8,13},{9,14},{1... | collective-permute-start | bytes 786440 | tf_op jit(solution)/shard_map/ppermute | solution.py:23
  37.5 12.3 %collective-permute-start.6 = (f32[256,256]{1,0:T(8,128)S(1)}, f32[256,256]{1,0:T(8,128)S(1)}, u32[]{:S(2)}, u32[]{:S(2)}) collective-permute-start(f32[256,256]{1,0:T(8,128)S(1)} %collective-permute-done.5.items_ref), channel_id=1, source_target_pairs={{1,6},{3,4},{9,14},{11,12},{17,22},{19,20},{25,30},{27,28}} | collective-permute-start | bytes 786440 | tf_op jit(solution)/shard_map/ppermute | solution.py:23

commit v12 on v10

--- a/solution.py
+++ b/solution.py
@@ -24,7 +24,7 @@
 
 
 def passes_on(b, g, n_blk, up):
-    return (b % 2 == 1) & ((up == 0) | (g % 2 == 1) | (b % n_blk >= n_blk - 2))
+    return (b % 2 == 1) & ((up == 0) | ((g % 2 == 1) ^ (b % n_blk >= n_blk - 2)))
 
 
 def halves(value):

time: 50.8 us -> 52.5 us (1.033)
  waiting for transfers between devices: 20.2 us -> 21.9 us
    ppermute x10, waiting for transfers between devices: 20.2 us -> 21.9 us  [sent(): return lax.ppermute(value, ('blk', 'group'), pairs)]
  transfers between devices with their start and end apart: 10 -> 10, of which waited for: 7 -> 6; matrix products, arithmetic and copies ran while one was open for 4% -> 4% of each run, Pallas kernels for 3% -> 3%
where the time goes in v12:
time: 52.5 us; the launch traced here: 52.3 us
  starting transfers between devices  22.2 us (42%)
  waiting for transfers between devices  21.9 us (42%)
  matrix products  4.01 us (8%)
  Pallas kernels  3.16 us (6%)
  between operations  0.85 us (2%)
    ppermute x10, starting transfers between devices, sent(): return lax.ppermute(value, ('blk', 'group'), pairs)  22.2 us
    ppermute x10, waiting for transfers between devices, sent(): return lax.ppermute(value, ('blk', 'group'), pairs)  21.9 us
    pallas_call x3, Pallas kernels, on_vmem(): pl.pallas_call(kernel, out_shape=[jax.ShapeDtypeStruct(shape, jnp.float32...  2.29 us
    dot_general x4, matrix products, user_gradient(): jnp.dot(gap, items, precision=PREC)  2.08 us
    dot_general x1, matrix products, weighted_gap(): lax.dot_general(users, items, (((1,), (1,)), ((), ())), precision=PREC)  1.52 us
  transfers between devices with their start and end apart: 10, of which 6 were waited for; matrix products, arithmetic and copies ran while one was open for 4% of the time, Pallas kernels for 3%

profile of v12, /device:TPU:0, one launch (start us, length us, event | category | flops | bytes accessed | tf_op | source)
XLA Modules:
  0.0 52.3 jit_solution(11090555227777734953)
XLA Ops:
  0.6 0.0 copy-start.1
  0.6 0.0 copy-start
  0.7 0.0 copy-start.4
  0.7 1.5 %fusion.5 = f32[256,256]{1,0:T(8,128)S(1)} fusion(f32[256,256]{1,0:T(8,128)} %param.5, f32[256,256]{1,0:T(8,128)} %param.7, s32[256,1024]{1,0:T(8,128)} %param.9), kind=kOutput, calls=%fused_computation.11 | convolution fusion | flops 101122048 | bytes 1048576 | tf_op jit(solution)/shard_map/dot_general | solution.py:43
  2.2 0.0 copy-done.1
  2.2 0.0 copy-done
  2.2 0.0 copy-done.4
  2.2 0.0 copy-start.3
  2.2 0.4 multiply_subtract_fusion.4
  2.7 0.0 copy-start.2
  2.7 3.0 %collective-permute-start = (f32[256,256]{1,0:T(8,128)S(1)}, f32[256,256]{1,0:T(8,128)S(1)}, u32[]{:S(2)}, u32[]{:S(2)}) collective-permute-start(f32[256,256]{1,0:T(8,128)S(1)} %get-tuple-element.21), channel_id=1, source_target_pairs={{0,4},{1,5},{2,6},{3,7},{4,8},{5,9},{6,10},{7,11},{8,12},{9,13},{1... | collective-permute-start | bytes 786440 | tf_op jit(solution)/shard_map/ppermute | solution.py:23
  5.7 0.0 copy-done.3
  5.7 0.3 multiply_subtract_fusion.3
  6.0 3.5 %collective-permute-start.3 = (f32[256,256]{1,0:T(8,128)S(1)}, f32[256,256]{1,0:T(8,128)S(1)}, u32[]{:S(2)}, u32[]{:S(2)}) collective-permute-start(f32[256,256]{1,0:T(8,128)S(1)} %get-tuple-element.20), channel_id=1, source_target_pairs={{0,8},{1,9},{2,10},{3,11},{8,16},{9,17},{10,18},{11,19},{16,24},{1... | collective-permute-start | bytes 786440 | tf_op jit(solution)/shard_map/ppermute | solution.py:23
  9.5 1.6 %collective-permute-start.2 = (f32[256,256]{1,0:T(8,128)S(1)}, f32[256,256]{1,0:T(8,128)S(1)}, u32[]{:S(2)}, u32[]{:S(2)}) collective-permute-start(f32[256,256]{1,0:T(8,128)S(1)} %broadcast_select_fusion.1), channel_id=1, source_target_pairs={{0,8},{1,9},{2,10},{3,11},{4,12},{5,13},{6,14},{7,15},{8,16},{9,17... | collective-permute-start | bytes 786440 | tf_op jit(solution)/shard_map/ppermute | solution.py:23
  11.2 0.0 copy-done.2
  11.2 0.1 fusion.6
  11.2 4.6 %collective-permute-done.items_ref = f32[256,256]{1,0:T(8,128)S(1)} collective-permute-done((f32[256,256]{1,0:T(8,128)S(1)}, f32[256,256]{1,0:T(8,128)S(1)}, u32[]{:S(2)}, u32[]{:S(2)}) %collective-permute-start) | collective-permute-done | bytes 262176 | tf_op jit(solution)/shard_map/ppermute | solution.py:23
  15.8 0.7 %visit.2 = (f32[256,256]{1,0:T(8,128)S(1)}, f32[256,256]{1,0:T(8,128)S(1)}) custom-call(f32[256,256]{1,0:T(8,128)S(1)} %get-tuple-element.22.users_ref, f32[256,256]{1,0:T(8,128)S(1)} %collective-permute-done.items_ref, s32[256,256]{1,0:T(8,128)S(1)} %get-tuple-element.43.tile_ref), custom_call_target="tpu_custom_call" | custom-call | flops 201326592 | bytes 1310720 | tf_op jit(solution)/shard_map/visit/pallas_call | solution.py:117
  16.6 0.1 collective-permute-start.4
  16.6 3.4 %collective-permute-start.1 = (f32[256,256]{1,0:T(8,128)S(1)}, f32[256,256]{1,0:T(8,128)S(1)}, u32[]{:S(2)}, u32[]{:S(2)}) collective-permute-start(f32[256,256]{1,0:T(8,128)S(1)} %collective-permute-done.items_ref), channel_id=1, source_target_pairs={{0,4},{1,5},{2,6},{3,7},{8,12},{9,13},{10,14},{11,15},{16,20},{17,... | collective-permute-start | bytes 786440 | tf_op jit(solution)/shard_map/ppermute | solution.py:23
  20.0 0.3 multiply_subtract_fusion.2
  20.3 2.8 %collective-permute-done.2.ahead_ref = f32[256,256]{1,0:T(8,128)S(1)} collective-permute-done((f32[256,256]{1,0:T(8,128)S(1)}, f32[256,256]{1,0:T(8,128)S(1)}, u32[]{:S(2)}, u32[]{:S(2)}) %collective-permute-start.2) | collective-permute-done | bytes 262176 | tf_op jit(solution)/shard_map/ppermute | solution.py:23
  23.1 0.0 collective-permute-done.3.late_ref
  23.1 3.6 %collective-permute-done.1.passed_ref = f32[256,256]{1,0:T(8,128)S(1)} collective-permute-done((f32[256,256]{1,0:T(8,128)S(1)}, f32[256,256]{1,0:T(8,128)S(1)}, u32[]{:S(2)}, u32[]{:S(2)}) %collective-permute-start.1) | collective-permute-done | bytes 262176 | tf_op jit(solution)/shard_map/ppermute | solution.py:23
  26.7 0.0 collective-permute-done.4.old_grad_ref
  26.7 0.8 %local.1 = (f32[256,256]{1,0:T(8,128)S(1)}, f32[256,256]{1,0:T(8,128)S(1)}, f32[256,256]{1,0:T(8,128)S(1)}, f32[256,256]{1,0:T(8,128)S(1)}) custom-call(s32[1]{0:T(128)} %bitcast.by_visit_ref, f32[256,256]{1,0:T(8,128)S(1)} %collective-permute-done.1.passed_ref, f32[256,256]{1,0:T(8,128)S(1)} %collective-permute-done.2.ahead_ref, ...), custom_call_target="tpu_custom_call" | custom-call | flops 201326592 | bytes 1310720 | tf_op jit(solution)/shard_map/local/pallas_call | solution.py:117
  27.5 2.5 %collective-permute-start.5 = (f32[256,256]{1,0:T(8,128)S(1)}, f32[256,256]{1,0:T(8,128)S(1)}, u32[]{:S(2)}, u32[]{:S(2)}) collective-permute-start(f32[256,256]{1,0:T(8,128)S(1)} %get-tuple-element.32), channel_id=1, source_target_pairs={{0,4},{1,5},{2,6},{3,7},{4,8},{5,9},{6,10},{7,11},{8,12},{9,13},{1... | collective-permute-start | bytes 786440 | tf_op jit(solution)/shard_map/ppermute | solution.py:23
  30.1 0.3 multiply_subtract_fusion.1
  30.4 1.9 %collective-permute-start.8 = (f32[256,256]{1,0:T(8,128)S(1)}, f32[256,256]{1,0:T(8,128)S(1)}, u32[]{:S(2)}, u32[]{:S(2)}) collective-permute-start(f32[256,256]{1,0:T(8,128)S(1)} %get-tuple-element.31), channel_id=1, source_target_pairs={{0,9},{1,10},{2,11},{3,8},{4,13},{6,15},{8,17},{9,18},{10,19},{11,... | collective-permute-start | bytes 786440 | tf_op jit(solution)/shard_map/ppermute | solution.py:23
  32.4 2.0 %collective-permute-start.7 = (f32[256,256]{1,0:T(8,128)S(1)}, f32[256,256]{1,0:T(8,128)S(1)}, u32[]{:S(2)}, u32[]{:S(2)}) collective-permute-start(f32[256,256]{1,0:T(8,128)S(1)} %broadcast_select_fusion), channel_id=1, source_target_pairs={{0,9},{1,10},{2,11},{3,8},{4,13},{5,14},{6,15},{7,12},{8,17},{9,18... | collective-permute-start | bytes 786440 | tf_op jit(solution)/shard_map/ppermute | solution.py:23
  34.3 2.3 %collective-permute-done.5.items_ref = f32[256,256]{1,0:T(8,128)S(1)} collective-permute-done((f32[256,256]{1,0:T(8,128)S(1)}, f32[256,256]{1,0:T(8,128)S(1)}, u32[]{:S(2)}, u32[]{:S(2)}) %collective-permute-start.5) | collective-permute-done | bytes 262176 | tf_op jit(solution)/shard_map/ppermute | solution.py:23
  36.6 0.7 %visit.3 = (f32[256,256]{1,0:T(8,128)S(1)}, f32[256,256]{1,0:T(8,128)S(1)}) custom-call(f32[256,256]{1,0:T(8,128)S(1)} %get-tuple-element.29.users_ref, f32[256,256]{1,0:T(8,128)S(1)} %collective-permute-done.5.items_ref, s32[256,256]{1,0:T(8,128)S(1)} %get-tuple-element.42.tile_ref), custom_call_target="tpu_custom_call" | custom-call | flops 201326592 | bytes 1310720 | tf_op jit(solution)/shard_map/visit/pallas_call | solution.py:117
  37.4 0.1 collective-permute-start.9
  37.5 4.2 %collective-permute-start.6 = (f32[256,256]{1,0:T(8,128)S(1)}, f32[256,256]{1,0:T(8,128)S(1)}, u32[]{:S(2)}, u32[]{:S(2)}) collective-permute-start(f32[256,256]{1,0:T(8,128)S(1)} %collective-permute-done.5.items_ref), channel_id=1, source_target_pairs={{0,5},{2,7},{9,14},{11,12},{17,22},{19,20},{25,30},{27,28}} | collective-permute-start | bytes 786440 | tf_op jit(solution)/shard_map/ppermute | solution.py:23
  41.7 1.1 %multiply_subtract_fusion = (f32[256,256]{1,0:T(8,128)}, f32[256,256]{1,0:T(8,128)}) fusion(f32[256,256]{1,0:T(8,128)S(1)} %get-tuple-element.29.users_ref, f32[256,256]{1,0:T(8,128)S(1)} %get-tuple-element.39, f32[256,256]{1,0:T(8,128)S(1)} %get-tuple-element.48, f32[256,256]{1,0:T(8,128)S(1)} %get-tuple-element.30, ...), kind=kOutput, calls=%fused_computation.12 | convolution fusion | flops 101318656 | bytes 1835008 | tf_op jit(solution)/shard_map/dot_general | solution.py:129
  42.8 4.9 %collective-permute-done.7.ahead_ref = f32[256,256]{1,0:T(8,128)S(1)} collective-permute-done((f32[256,256]{1,0:T(8,128)S(1)}, f32[256,256]{1,0:T(8,128)S(1)}, u32[]{:S(2)}, u32[]{:S(2)}) %collective-permute-start.7) | collective-permute-done | bytes 262176 | tf_op jit(solution)/shard_map/ppermute | solution.py:23
  47.7 0.0 collective-permute-done.8.late_ref
  47.7 3.7 %collective-permute-done.9.grad_ref = f32[256,256]{1,0:T(8,128)S(1)} collective-permute-done((f32[256,256]{1,0:T(8,128)S(1)}, f32[256,256]{1,0:T(8,128)S(1)}, u32[]{:S(2)}, u32[]{:S(2)}) %collective-permute-start.9) | collective-permute-done | bytes 262176 | tf_op jit(solution)/shard_map/ppermute | solution.py:23
  51.4 0.0 collective-permute-done.6.passed_ref
  51.4 0.9 %last_update.1 = (f32[256,256]{1,0:T(8,128)}, f32[256,256]{1,0:T(8,128)}) custom-call(s32[1]{0:T(128)} %bitcast.1.by_visit_ref, f32[256,256]{1,0:T(8,128)S(1)} %collective-permute-done.6.passed_ref, f32[256,256]{1,0:T(8,128)S(1)} %collective-permute-done.7.ahead_ref, f32[256,256]{1,0:T(8,128)S(1)} %collective-permute-done.8.late_ref, ...), custom_call_target="tpu_custom_call" | custom-call | flops 524288 | bytes 1572864 | tf_op jit(solution)/shard_map/last_update/pallas_call | solution.py:101
  (2 shorter events, 0.1 us)
Async XLA Ops:
  0.6 1.6 %copy-start.1 = (f32[256,256]{1,0:T(8,128)S(1)}, f32[256,256]{1,0:T(8,128)}, u32[]{:S(2)}) copy-start(f32[256,256]{1,0:T(8,128)} %param.7) | copy-start | bytes 786436
  0.6 1.6 %copy-start = (f32[256,256]{1,0:T(8,128)S(1)}, f32[256,256]{1,0:T(8,128)}, u32[]{:S(2)}) copy-start(f32[256,256]{1,0:T(8,128)} %param.5) | copy-start | bytes 786436
  0.7 1.6 %copy-start.4 = (f32[256,256]{1,0:T(8,128)S(1)}, f32[256,256]{1,0:T(8,128)}, u32[]{:S(2)}) copy-start(f32[256,256]{1,0:T(8,128)} %param.8) | copy-start | bytes 786436
  2.2 3.4 %copy-start.3 = (f32[256,256]{1,0:T(8,128)S(1)}, f32[256,256]{1,0:T(8,128)}, u32[]{:S(2)}) copy-start(f32[256,256]{1,0:T(8,128)} %param.6) | copy-start | bytes 786436
  2.7 8.5 %copy-start.2 = (s32[256,1024]{1,0:T(8,128)S(1)}, s32[256,1024]{1,0:T(8,128)}, u32[]{:S(2)}) copy-start(s32[256,1024]{1,0:T(8,128)} %param.9) | copy-start | bytes 3145732
  2.7 13.2 %collective-permute-start = (f32[256,256]{1,0:T(8,128)S(1)}, f32[256,256]{1,0:T(8,128)S(1)}, u32[]{:S(2)}, u32[]{:S(2)}) collective-permute-start(f32[256,256]{1,0:T(8,128)S(1)} %get-tuple-element.21), channel_id=1, source_target_pairs={{0,4},{1,5},{2,6},{3,7},{4,8},{5,9},{6,10},{7,11},{8,12},{9,13},{1... | collective-permute-start | bytes 786440 | tf_op jit(solution)/shard_map/ppermute | solution.py:23
  6.0 17.1 %collective-permute-start.3 = (f32[256,256]{1,0:T(8,128)S(1)}, f32[256,256]{1,0:T(8,128)S(1)}, u32[]{:S(2)}, u32[]{:S(2)}) collective-permute-start(f32[256,256]{1,0:T(8,128)S(1)} %get-tuple-element.20), channel_id=1, source_target_pairs={{0,8},{1,9},{2,10},{3,11},{8,16},{9,17},{10,18},{11,19},{16,24},{1... | collective-permute-start | bytes 786440 | tf_op jit(solution)/shard_map/ppermute | solution.py:23
  9.5 13.6 %collective-permute-start.2 = (f32[256,256]{1,0:T(8,128)S(1)}, f32[256,256]{1,0:T(8,128)S(1)}, u32[]{:S(2)}, u32[]{:S(2)}) collective-permute-start(f32[256,256]{1,0:T(8,128)S(1)} %broadcast_select_fusion.1), channel_id=1, source_target_pairs={{0,8},{1,9},{2,10},{3,11},{4,12},{5,13},{6,14},{7,15},{8,16},{9,17... | collective-permute-start | bytes 786440 | tf_op jit(solution)/shard_map/ppermute | solution.py:23
  16.6 10.1 %collective-permute-start.4 = (f32[256,256]{1,0:T(8,128)S(1)}, f32[256,256]{1,0:T(8,128)S(1)}, u32[]{:S(2)}, u32[]{:S(2)}) collective-permute-start(f32[256,256]{1,0:T(8,128)S(1)} %get-tuple-element.23), channel_id=1, source_target_pairs={{0,4},{1,5},{2,6},{3,7},{4,8},{5,9},{6,10},{7,11},{8,12},{9,13},{1... | collective-permute-start | bytes 786440 | tf_op jit(solution)/shard_map/ppermute | solution.py:23
  16.6 10.1 %collective-permute-start.1 = (f32[256,256]{1,0:T(8,128)S(1)}, f32[256,256]{1,0:T(8,128)S(1)}, u32[]{:S(2)}, u32[]{:S(2)}) collective-permute-start(f32[256,256]{1,0:T(8,128)S(1)} %collective-permute-done.items_ref), channel_id=1, source_target_pairs={{0,4},{1,5},{2,6},{3,7},{8,12},{9,13},{10,14},{11,15},{16,20},{17,... | collective-permute-start | bytes 786440 | tf_op jit(solution)/shard_map/ppermute | solution.py:23
  27.5 9.1 %collective-permute-start.5 = (f32[256,256]{1,0:T(8,128)S(1)}, f32[256,256]{1,0:T(8,128)S(1)}, u32[]{:S(2)}, u32[]{:S(2)}) collective-permute-start(f32[256,256]{1,0:T(8,128)S(1)} %get-tuple-element.32), channel_id=1, source_target_pairs={{0,4},{1,5},{2,6},{3,7},{4,8},{5,9},{6,10},{7,11},{8,12},{9,13},{1... | collective-permute-start | bytes 786440 | tf_op jit(solution)/shard_map/ppermute | solution.py:23
  30.4 17.3 %collective-permute-start.8 = (f32[256,256]{1,0:T(8,128)S(1)}, f32[256,256]{1,0:T(8,128)S(1)}, u32[]{:S(2)}, u32[]{:S(2)}) collective-permute-start(f32[256,256]{1,0:T(8,128)S(1)} %get-tuple-element.31), channel_id=1, source_target_pairs={{0,9},{1,10},{2,11},{3,8},{4,13},{6,15},{8,17},{9,18},{10,19},{11,... | collective-permute-start | bytes 786440 | tf_op jit(solution)/shard_map/ppermute | solution.py:23
  32.4 15.4 %collective-permute-start.7 = (f32[256,256]{1,0:T(8,128)S(1)}, f32[256,256]{1,0:T(8,128)S(1)}, u32[]{:S(2)}, u32[]{:S(2)}) collective-permute-start(f32[256,256]{1,0:T(8,128)S(1)} %broadcast_select_fusion), channel_id=1, source_target_pairs={{0,9},{1,10},{2,11},{3,8},{4,13},{5,14},{6,15},{7,12},{8,17},{9,18... | collective-permute-start | bytes 786440 | tf_op jit(solution)/shard_map/ppermute | solution.py:23
  37.4 14.0 %collective-permute-start.9 = (f32[256,256]{1,0:T(8,128)S(1)}, f32[256,256]{1,0:T(8,128)S(1)}, u32[]{:S(2)}, u32[]{:S(2)}) collective-permute-start(f32[256,256]{1,0:T(8,128)S(1)} %get-tuple-element.33), channel_id=1, source_target_pairs={{0,5},{1,6},{2,7},{3,4},{4,9},{5,10},{6,11},{7,8},{8,13},{9,14},{1... | collective-permute-start | bytes 786440 | tf_op jit(solution)/shard_map/ppermute | solution.py:23
  37.5 14.0 %collective-permute-start.6 = (f32[256,256]{1,0:T(8,128)S(1)}, f32[256,256]{1,0:T(8,128)S(1)}, u32[]{:S(2)}, u32[]{:S(2)}) collective-permute-start(f32[256,256]{1,0:T(8,128)S(1)} %collective-permute-done.5.items_ref), channel_id=1, source_target_pairs={{0,5},{2,7},{9,14},{11,12},{17,22},{19,20},{25,30},{27,28}} | collective-permute-start | bytes 786440 | tf_op jit(solution)/shard_map/ppermute | solution.py:23
